TPU v7x, 32 devices: a whole 2x2x4 slice. The times are simulated.
32 devices in a mesh: grp: 2 (over y), seq: 4 (over z), blk: 4 (over x, core).
Axes of the slice: x: 2, y: 2, z: 4, core: 2. Of those that a mesh axis runs over, the one named last changes fastest.
Arguments:
- queries: bfloat16 [2048, 64, 128], P(('grp', 'seq', 'blk')), parts along dimension 0, may hold values from -6 to 6
- keys: bfloat16 [2048, 8, 128], P(('grp', 'seq', 'blk')), parts along dimension 0, may hold values from -6 to 6
- values: bfloat16 [2048, 8, 128], P(('grp', 'seq', 'blk')), parts along dimension 0, may hold values from -6 to 6
- vert_blocks: int32 [64, 16], replicated, may hold values from 0 to 15, as said below
- vert_count: int32 [64], replicated, may hold values from 1 to 16, as said below
- slash_offsets: int32 [64, 14], replicated, may hold values from 0 to 15, as said below
- slash_count: int32 [64], replicated, may hold values from 1 to 14, as said below
Outputs:
- attended: bfloat16 [2048, 64, 128], P(('grp', 'seq', 'blk')), parts along dimension 0
There are 2 independent parts, one for each index of `grp`. A program takes and returns all parts, laid end to end along the dimension named above; an argument that names none is the same for every part. Nothing has to cross between parts.
Inputs may be any that keep to these rules, and one draw needn't show every extreme that they name: `vert_blocks`: the 16 entries of each head's row are distinct. `vert_count`: some head uses all 16 entries. `slash_offsets`: the 14 entries of each head's row are distinct, and the first is 0. `slash_count`: some head uses all 14 entries.
All inputs are finite; a program needn't handle non-finite values.
Results may differ from a plain program's by a relative error of at most 0.0047.
Values may be sent and summed in bfloat16 or wider, within the bound.
No kernel may reach another device: no remote copies, remote signals or barrier semaphores. Data moves between devices by JAX's collectives and lax.ppermute only.
A program may use at most 64 MiB of HBM per device.

v0:
```python
import math

import jax
import jax.numpy as jnp
from jax import lax
from jax.sharding import PartitionSpec as P

BLOCK = 64


def slash_plan(query_index, vertical, vert_live, slash, slash_live):
    slash_index = query_index[:, None] - slash[None, :]
    duplicate = jnp.any(
        (slash_index[:, :, None] == vertical[None, None, :]) & vert_live[None, None, :], axis=2
    )
    usable = slash_live[None, :] & (slash_index >= 0) & jnp.logical_not(duplicate)
    return (slash_index, usable)


def sparse_block(
    query_tiles,
    query_index,
    vert_keys,
    vert_values,
    vertical,
    vert_live,
    slash_keys,
    slash_values,
    slash_index,
    slash_live,
):
    tile_count, block_len, head_width = query_tiles.shape
    lane_pos = jnp.arange(block_len, dtype=jnp.int32)
    query_pos = query_index[:, None] * block_len + lane_pos[None, :]
    vert_pos = vertical[:, None] * block_len + lane_pos[None, :]
    slash_pos = slash_index[:, :, None] * block_len + lane_pos[None, None, :]
    score_scale = 1.0 / math.sqrt(head_width)
    vert_scores = (
        jnp.einsum("gid,vjd->givj", query_tiles, vert_keys, preferred_element_type=jnp.float32)
        * score_scale
    )
    slash_scores = (
        jnp.einsum("gid,gsjd->gisj", query_tiles, slash_keys, preferred_element_type=jnp.float32)
        * score_scale
    )
    vert_mask = vert_live[None, None, :, None] & (
        vert_pos[None, None, :, :] <= query_pos[:, :, None, None]
    )
    slash_mask = slash_live[:, None, :, None] & (
        slash_pos[:, None, :, :] <= query_pos[:, :, None, None]
    )
    scores = jnp.concatenate(
        [
            jnp.where(vert_mask, vert_scores, -jnp.inf).reshape(tile_count, block_len, -1),
            jnp.where(slash_mask, slash_scores, -jnp.inf).reshape(tile_count, block_len, -1),
        ],
        axis=2,
    )
    row_max = jnp.max(scores, axis=2, keepdims=True)
    raised = jnp.exp(scores - row_max)
    weights = (raised / jnp.sum(raised, axis=2, keepdims=True)).astype(jnp.bfloat16)
    vert_width = vert_keys.shape[0] * block_len
    result = jnp.einsum(
        "gik,kd->gid",
        weights[:, :, :vert_width],
        vert_values.reshape(vert_width, head_width),
        preferred_element_type=jnp.float32,
    )
    result = result + jnp.einsum(
        "gik,gkd->gid",
        weights[:, :, vert_width:],
        slash_values.reshape(tile_count, -1, head_width),
        preferred_element_type=jnp.float32,
    )
    return result.astype(jnp.bfloat16).reshape(tile_count * block_len, head_width)


def on_device(queries, keys, values, vert_blocks, vert_count, slash_offsets, slash_count):
    owners = lax.axis_size("seq")
    cycle_size = lax.axis_size("blk")
    owner_id = lax.axis_index("seq")
    cycle_id = lax.axis_index("blk")
    shard_rows, head_total, head_width = queries.shape
    kv_total = keys.shape[1]
    group_size = head_total // kv_total
    per_owner = head_total // owners
    kv_owned = max(1, kv_total // owners)
    sharers = max(1, owners // kv_total)
    blocks_per_shard = shard_rows // BLOCK
    query_send = queries.reshape(shard_rows, owners, per_owner, head_width)

    def by_owner(tensor):
        if sharers > 1:
            tensor = jnp.repeat(tensor, sharers, axis=1)
        return tensor.reshape(tensor.shape[0], owners, kv_owned, head_width)

    query_rows, key_part, value_part = (
        lax.all_to_all(query_send, "seq", split_axis=1, concat_axis=0, tiled=True),
        lax.all_to_all(by_owner(keys), "seq", split_axis=1, concat_axis=0, tiled=True),
        lax.all_to_all(by_owner(values), "seq", split_axis=1, concat_axis=0, tiled=True),
    )
    key_rows, value_rows = (
        lax.all_gather(key_part, "blk", axis=0, tiled=True),
        lax.all_gather(value_part, "blk", axis=0, tiled=True),
    )

    def stored(block_id):
        first_row = block_id * BLOCK
        source = first_row // shard_rows
        return (
            source % cycle_size * owners + source // cycle_size
        ) * blocks_per_shard + first_row % shard_rows // BLOCK

    key_heads = jnp.moveaxis(key_rows.reshape(-1, BLOCK, kv_owned, head_width), 2, 0)
    value_heads = jnp.moveaxis(value_rows.reshape(-1, BLOCK, kv_owned, head_width), 2, 0)
    block_total = key_heads.shape[1]
    owned_rows = owners * shard_rows
    group_rows = min(512, owned_rows)
    groups = owned_rows // group_rows
    group_blocks = group_rows // BLOCK
    query_heads = jnp.transpose(query_rows.reshape(owned_rows, per_owner, head_width), (1, 0, 2))

    def attend(step_id):
        slot_id = step_id // groups
        group_id = step_id % groups
        head_id = owner_id * per_owner + slot_id
        kv_local = head_id // group_size - owner_id // sharers * kv_owned
        head_queries = lax.dynamic_index_in_dim(query_heads, slot_id, 0, False)
        query_tiles = lax.dynamic_slice_in_dim(
            head_queries, group_id * group_rows, group_rows, 0
        ).reshape(group_blocks, BLOCK, head_width)
        local_rows = group_id * group_rows + jnp.arange(group_blocks, dtype=jnp.int32) * BLOCK
        query_index = (
            local_rows // shard_rows * cycle_size + cycle_id
        ) * blocks_per_shard + local_rows % shard_rows // BLOCK
        vertical = lax.dynamic_index_in_dim(vert_blocks, head_id, 0, False)
        vert_live = jnp.arange(vertical.shape[0], dtype=jnp.int32) < lax.dynamic_index_in_dim(
            vert_count, head_id, 0, False
        )
        slash = lax.dynamic_index_in_dim(slash_offsets, head_id, 0, False)
        slash_live = jnp.arange(slash.shape[0], dtype=jnp.int32) < lax.dynamic_index_in_dim(
            slash_count, head_id, 0, False
        )
        slash_index, usable = slash_plan(query_index, vertical, vert_live, slash, slash_live)
        clamped = stored(jnp.clip(slash_index, 0, block_total - 1))
        vert_rows = stored(vertical)
        head_keys = lax.dynamic_index_in_dim(key_heads, kv_local, 0, False)
        head_values = lax.dynamic_index_in_dim(value_heads, kv_local, 0, False)
        vert_keys = jnp.take(head_keys, vert_rows, axis=0)
        vert_values = jnp.take(head_values, vert_rows, axis=0)
        slash_keys = jnp.take(head_keys, clamped, axis=0)
        slash_values = jnp.take(head_values, clamped, axis=0)
        return sparse_block(
            query_tiles,
            query_index,
            vert_keys,
            vert_values,
            vertical,
            vert_live,
            slash_keys,
            slash_values,
            slash_index,
            usable,
        )

    attended = lax.map(attend, jnp.arange(per_owner * groups, dtype=jnp.int32))
    attended = attended.reshape(per_owner, owners, shard_rows, head_width)
    returned = lax.all_to_all(attended, "seq", split_axis=1, concat_axis=1, tiled=True)
    return jnp.transpose(returned, (2, 1, 0, 3)).reshape(shard_rows, head_total, head_width)


def solution(mesh):
    return jax.shard_map(
        on_device,
        mesh=mesh,
        in_specs=(
            P(("grp", "seq", "blk"), None, None),
            P(("grp", "seq", "blk"), None, None),
            P(("grp", "seq", "blk"), None, None),
            P(),
            P(),
            P(),
            P(),
        ),
        out_specs=P(("grp", "seq", "blk"), None, None),
        check_vma=False,
    )
```

profile of v0, /device:TPU:1, one launch (start us, length us, event | category | flops | bytes accessed | tf_op | source)
XLA Modules:
  0.0 445.0 jit_solution(8056802432209031698)
XLA Ops:
  1.6 5.4 %all-to-all-start.2 = ((bf16[64,4,2,128]{3,2,0,1:T(2,128)(2,1)}), bf16[64,4,2,128]{3,2,0,1:T(2,128)(2,1)S(1)}, u32[]{:S(2)}, u32[]{:S(2)}) async-start(bf16[64,4,2,128]{3,2,0,1:T(2,128)(2,1)} %copy.90), calls=%async_computation.2 | async-start | bytes 262144 | tf_op jit(solution)/shard_map/all_to_all | solution.py:100
  8.7 3.2 all-to-all-done.2
  11.9 3.4 all-to-all-start.1
  15.3 2.9 copy.83
  20.1 3.5 all-to-all-start
  23.8 10.3 %all_gather.7 = bf16[1024,1,2,128]{3,2,1,0:T(2,128)(2,1)S(1)} all-gather(bf16[256,1,2,128]{3,2,1,0:T(2,128)(2,1)S(1)} %bitcast.122), channel_id=1, replica_groups=mesh['grp'=2,'seq'=4,'blk'=4] {'blk'}, dimensions={0}, use_global_device_ids=true | all-gather | bytes 655360 | tf_op jit(solution)/shard_map/all_gather | solution.py:104
  35.0 7.3 %all_gather.6 = bf16[1024,1,2,128]{3,2,1,0:T(2,128)(2,1)S(1)} all-gather(bf16[256,1,2,128]{3,2,1,0:T(2,128)(2,1)S(1)} %bitcast.123), channel_id=1, replica_groups=mesh['grp'=2,'seq'=4,'blk'=4] {'blk'}, dimensions={0}, use_global_device_ids=true | all-gather | bytes 655360 | tf_op jit(solution)/shard_map/all_gather | solution.py:103
  43.2 5.6 %all-to-all-done = bf16[64,4,16,128]{3,0,2,1:T(8,128)(2,1)S(1)} async-done(((bf16[64,4,16,128]{3,0,2,1:T(8,128)(2,1)}), bf16[64,4,16,128]{3,0,2,1:T(8,128)(2,1)S(1)}, u32[]{:S(2)}, u32[]{:S(2)}) %all-to-all-start) | async-done | bytes 1048608 | tf_op jit(solution)/shard_map/all_to_all | solution.py:98
  50.7 363.8 %while.14 = (s32[]{:T(128)}, bf16[16,256,128]{2,1,0:T(8,128)(2,1)}, s32[16]{0:T(128)S(1)}, s32[]{:T(128)}, s32[64]{0:T(128)S(1)}, /*index=5*/s32[64,16]{1,0:T(8,...) while((s32[]{:T(128)}, bf16[16,256,128]{2,1,0:T(8,128)(2,1)}, ...), condition=%wide.region_5.8_spmd, body=%wide.region_0.7_spmd.sunk | while | flops 258819328 | bytes 23065772 | solution.py:166
  60.2 2.5 fusion.65
  63.4 2.1 fusion.66
  65.5 2.0 copy.113
  67.5 2.2 copy.114
  83.0 2.5 fusion.65
  86.2 2.1 fusion.66
  88.3 2.0 copy.113
  90.3 2.2 copy.114
  105.7 2.5 fusion.65
  108.9 2.1 fusion.66
  111.0 2.0 copy.113
  113.0 2.2 copy.114
  128.4 2.5 fusion.65
  131.6 2.1 fusion.66
  133.7 2.0 copy.113
  135.8 2.2 copy.114
  151.2 2.5 fusion.65
  154.4 2.1 fusion.66
  158.5 2.2 copy.114
  173.9 2.5 fusion.65
  177.1 2.1 fusion.66
  181.2 2.2 copy.114
  196.7 2.5 fusion.65
  199.9 2.1 fusion.66
  201.9 2.0 copy.113
  204.0 2.2 copy.114
  219.4 2.5 fusion.65
  222.6 2.1 fusion.66
  224.7 2.0 copy.113
  226.7 2.2 copy.114
  242.1 2.5 fusion.65
  245.3 2.1 fusion.66
  249.4 2.2 copy.114
  264.9 2.5 fusion.65
  268.1 2.1 fusion.66
  272.2 2.2 copy.114
  287.6 2.5 fusion.65
  290.8 2.1 fusion.66
  294.9 2.2 copy.114
  310.3 2.5 fusion.65
  313.5 2.1 fusion.66
  317.7 2.2 copy.114
  333.1 2.5 fusion.65
  336.3 2.1 fusion.66
  340.4 2.2 copy.114
  355.8 2.5 fusion.65
  359.0 2.1 fusion.66
  363.1 2.2 copy.114
  378.6 2.5 fusion.65
  381.7 2.1 fusion.66
  385.9 2.2 copy.114
  401.3 2.5 fusion.65
  404.5 2.1 fusion.66
  408.6 2.2 copy.114
  416.4 27.3 %all_to_all.56 = bf16[16,4,64,128]{3,0,2,1:T(8,128)(2,1)S(1)} all-to-all(bf16[16,4,64,128]{3,0,2,1:T(8,128)(2,1)S(1)} %bitcast.116), channel_id=1, replica_groups=mesh['grp'=2,'seq'=4,'blk'=4] {'seq'}, dimensions={1} | all-to-all | bytes 2097152 | tf_op jit(solution)/shard_map/all_to_all | solution.py:168
  (559 shorter events, 208.8 us)
Async XLA Ops:
  1.6 10.2 %all-to-all-start.2 = ((bf16[64,4,2,128]{3,2,0,1:T(2,128)(2,1)}), bf16[64,4,2,128]{3,2,0,1:T(2,128)(2,1)S(1)}, u32[]{:S(2)}, u32[]{:S(2)}) async-start(bf16[64,4,2,128]{3,2,0,1:T(2,128)(2,1)} %copy.90), calls=%async_computation.2 | async-start | bytes 262144 | tf_op jit(solution)/shard_map/all_to_all | solution.py:100
  11.9 8.2 %all-to-all-start.1 = ((bf16[64,4,2,128]{3,2,0,1:T(2,128)(2,1)}), bf16[64,4,2,128]{3,2,0,1:T(2,128)(2,1)S(1)}, u32[]{:S(2)}, u32[]{:S(2)}) async-start(bf16[64,4,2,128]{3,2,0,1:T(2,128)(2,1)} %copy.86), calls=%async_computation.1 | async-start | bytes 262144 | tf_op jit(solution)/shard_map/all_to_all | solution.py:99
  15.3 8.3 %copy-start = (s32[64,16]{0,1:T(8,128)S(1)}, s32[64,16]{0,1:T(8,128)}, u32[]{:S(2)}) copy-start(s32[64,16]{0,1:T(8,128)} %param.16) | copy-start | bytes 12292
  15.3 8.4 %copy-start.1 = (s32[64,14]{0,1:T(8,128)S(1)}, s32[64,14]{0,1:T(8,128)}, u32[]{:S(2)}) copy-start(s32[64,14]{0,1:T(8,128)} %param.18) | copy-start | bytes 10756
  20.1 28.7 %all-to-all-start = ((bf16[64,4,16,128]{3,0,2,1:T(8,128)(2,1)}), bf16[64,4,16,128]{3,0,2,1:T(8,128)(2,1)S(1)}, u32[]{:S(2)}, u32[]{:S(2)}) async-start(bf16[64,4,16,128]{3,0,2,1:T(8,128)(2,1)} %bitcast.21), calls=%async_computation | async-start | bytes 2097152 | tf_op jit(solution)/shard_map/all_to_all | solution.py:98
  43.2 7.5 %copy-start.2 = (s32[64]{0:T(128)S(1)}, s32[64]{0:T(128)}, u32[]{:S(2)}) copy-start(s32[64]{0:T(128)} %param.17) | copy-start | bytes 772
  43.2 7.5 %copy-start.3 = (s32[64]{0:T(128)S(1)}, s32[64]{0:T(128)}, u32[]{:S(2)}) copy-start(s32[64]{0:T(128)} %param.19) | copy-start | bytes 772
where the time goes:
time: 450 us; the launch traced here: 445 us
  local copies, waits for them, and re-layouts  198 us (44%)
  matrix products  83.1 us (18%)
  other arithmetic  49.5 us (11%)
  loops' own time  47 us (10%)
  blocking collectives  44.8 us (10%)
  starting transfers between devices  12.3 us (3%)
  waiting for transfers between devices  10.6 us (2%)
    another operation x1, loops' own time, on_device(): attended = lax.map(attend, jnp.arange(per_owner * groups, dtype=jnp.int32))  47 us
    dot_general x16, matrix products, sparse_block(): jnp.einsum('gid,gsjd->gisj', query_tiles, slash_keys, preferred_element_t...  40 us
    reshape x16, local copies, waits for them, and re-layouts, sparse_block(): jnp.where(vert_mask, vert_scores, -jnp.inf)  34.8 us
    dot_general x16, matrix products, sparse_block(): jnp.einsum('gid,vjd->givj', query_tiles, vert_keys, preferred_element_typ...  33.4 us
    reshape x16, local copies, waits for them, and re-layouts, sparse_block(): jnp.where(slash_mask, slash_scores, -jnp.inf)  32.2 us
    all_to_all x1, blocking collectives, on_device(): lax.all_to_all(attended, 'seq', split_axis=1, concat_axis=1, tiled=True)  27.3 us
    squeeze x16, local copies, waits for them, and re-layouts, attend(): head_values = lax.dynamic_index_in_dim(value_heads, kv_local, 0, False)  17.1 us
    dynamic_slice x16, local copies, waits for them, and re-layouts, attend(): head_queries = lax.dynamic_index_in_dim(query_heads, slot_id, 0, False)  13.6 us
  transfers between devices with their start and end apart: 3, of which 3 were waited for; matrix products, arithmetic and copies ran while one was open for 1% of the time, Pallas kernels for 0%

commit v1 on v0

--- a/solution.py
+++ b/solution.py
@@ -1,11 +1,16 @@
+import functools
 import math
 
 import jax
 import jax.numpy as jnp
 from jax import lax
+from jax.experimental import pallas as pl
+from jax.experimental.pallas import tpu as pltpu
 from jax.sharding import PartitionSpec as P
 
 BLOCK = 64
+NEG = -1e30
+GATHER_BYTES = 8 << 20
 
 
 def slash_plan(query_index, vertical, vert_live, slash, slash_live):
@@ -75,7 +80,7 @@
     return result.astype(jnp.bfloat16).reshape(tile_count * block_len, head_width)
 
 
-def on_device(queries, keys, values, vert_blocks, vert_count, slash_offsets, slash_count):
+def by_head_owner(queries, keys, values, vert_blocks, vert_count, slash_offsets, slash_count):
     owners = lax.axis_size("seq")
     cycle_size = lax.axis_size("blk")
     owner_id = lax.axis_index("seq")
@@ -169,6 +174,210 @@
     return jnp.transpose(returned, (2, 1, 0, 3)).reshape(shard_rows, head_total, head_width)
 
 
+def listed(entries, live_count, wanted):
+    row = lax.broadcasted_iota(jnp.int32, entries.shape, 0)
+    hit = (entries == wanted) & (row < live_count)
+    return jnp.sum(jnp.where(hit, 1.0, 0.0), axis=0, keepdims=True)
+
+def block_bias(vert, vcount, slash, scount, query_block, key_blocks):
+    heads = vert.shape[1]
+    rows = []
+    for kb in key_blocks:
+        n = listed(vert, vcount, kb) + listed(slash, scount, query_block - kb)
+        ok = jnp.where((kb >= 0) & (kb <= query_block), 1.0, 0.0)
+        rows.append(n * ok)
+    taken = jnp.concatenate(rows, axis=0)
+    pad = 8 - len(key_blocks)
+    if pad:
+        taken = jnp.concatenate([taken, jnp.zeros((pad, heads), jnp.float32)], axis=0)
+    width = len(key_blocks) * BLOCK
+    spread = (
+        lax.broadcasted_iota(jnp.int32, (8, width), 0)
+        == lax.broadcasted_iota(jnp.int32, (8, width), 1) // BLOCK
+    )
+    count = lax.dot_general(
+        taken, jnp.where(spread, 1.0, 0.0), (((0,), (0,)), ((), ())),
+        preferred_element_type=jnp.float32,
+    )
+    return jnp.where(count > 0.5, 0.0, NEG)
+
+def stage_body(first, last, slots, kv_heads, group, scale, *refs):
+    (ids, vert, vcount, slash, scount, q_own, q_sib), refs = refs[:7], refs[7:]
+    tiles, refs = refs[:slots], refs[slots:]
+    if not first:
+        acc_in, top_in, sum_in = refs[:3]
+        refs = refs[3:]
+    if last:
+        out_own, out_sib, bias_ref = refs
+    else:
+        acc_out, top_out, sum_out, bias_ref = refs
+    core = ids[0]
+    half = kv_heads * group
+    key_blocks = [ids[3 + t] for t in range(slots)]
+    for b in range(2):
+        bias_ref[b] = block_bias(vert[...], vcount[...], slash[...], scount[...], ids[1 + b], key_blocks)
+    lo = pl.multiple_of(core * half, half)
+    width = slots * BLOCK
+    rows = BLOCK * group
+    if first:
+        pos = lax.broadcasted_iota(jnp.int32, (BLOCK, 1, 2 * BLOCK), 0)
+        key = lax.broadcasted_iota(jnp.int32, (BLOCK, 1, 2 * BLOCK), 2)
+    for b in range(2):
+        q_ref, o_ref = (q_own, q_sib)[b], ((out_own, out_sib)[b] if last else None)
+        for pair in range(kv_heads // 2):
+            q16 = q_ref[:, pl.ds(pl.multiple_of(lo + pair * 2 * group, 2 * group), 2 * group), :].astype(jnp.float32)
+            outs = []
+            for one in range(2):
+                g = pair * 2 + one
+                q = q16[:, one * group:(one + 1) * group, :].reshape(rows, 128).astype(jnp.bfloat16)
+                k = jnp.concatenate([t[0, g] for t in tiles], axis=0)
+                v = jnp.concatenate([t[1, g] for t in tiles], axis=0)
+                s = lax.dot_general(q, k, (((1,), (1,)), ((), ())), preferred_element_type=jnp.float32)
+                s = s.reshape(BLOCK, group, width)
+                head = pl.ds(pl.multiple_of(lo + g * group, group), group)
+                s = s + bias_ref[b, head, :][None]
+                if first:
+                    lane_pos = key - b * BLOCK
+                    causal = jnp.where((lane_pos > pos) & (lane_pos < BLOCK), NEG, 0.0)
+                    s = jnp.concatenate([s[:, :, :128] + causal, s[:, :, 128:]], axis=2)
+                s = s.reshape(rows, width)
+                top = jnp.broadcast_to(jnp.max(s, axis=1, keepdims=True), (rows, 128))
+                if not first:
+                    old_top = top_in[b, g]
+                    top = jnp.maximum(top, old_top)
+                    shrink = jnp.exp2((old_top - top) * scale)
+                p = jnp.exp2((s - jnp.concatenate([top] * (width // 128), axis=1)) * scale)
+                total = jnp.broadcast_to(jnp.sum(p, axis=1, keepdims=True), (rows, 128))
+                acc = jnp.dot(p.astype(jnp.bfloat16), v, preferred_element_type=jnp.float32)
+                if not first:
+                    total = total + sum_in[b, g] * shrink
+                    acc = acc + acc_in[b, g] * shrink
+                if last:
+                    outs.append((acc / total).reshape(BLOCK, group, 128))
+                else:
+                    acc_out[b, g] = acc
+                    top_out[b, g] = top
+                    sum_out[b, g] = total
+            if last:
+                o_ref[:, pair * 2 * group:(pair + 1) * 2 * group, :] = jnp.concatenate(outs, axis=1).astype(jnp.bfloat16)
+
+def attend_stage(ids, patterns, q_own, q_sib, tiles, state, last):
+    _, kv_heads, _, width = tiles[0].shape
+    heads = q_own.shape[1]
+    half = heads // 2
+    group = half // kv_heads
+    rows = BLOCK * group
+    first = state is None
+    scale = 1.0 / math.sqrt(width) * math.log2(math.e)
+    vm = pl.BlockSpec(memory_space=pltpu.VMEM)
+    args = [ids, *patterns, q_own, q_sib, *tiles] + ([] if first else list(state))
+    specs = [pl.BlockSpec(memory_space=pltpu.SMEM)] + [vm] * (len(args) - 1)
+    if last:
+        out = [jax.ShapeDtypeStruct((BLOCK, half, width), jnp.bfloat16)] * 2
+    else:
+        out = [jax.ShapeDtypeStruct((2, kv_heads, rows, width), jnp.float32)] * 3
+
+    flops = 4 * 2 * half * BLOCK * BLOCK * len(tiles) * width
+    return pl.pallas_call(
+        functools.partial(stage_body, first, last, len(tiles), kv_heads, group, scale),
+        out_shape=out,
+        in_specs=specs,
+        out_specs=[vm] * len(out),
+        scratch_shapes=[pltpu.VMEM((2, heads, BLOCK * len(tiles)), jnp.float32)],
+        compiler_params=pltpu.CompilerParams(vmem_limit_bytes=32 * 1024 * 1024),
+        cost_estimate=pl.CostEstimate(flops=flops, bytes_accessed=4 << 20, transcendentals=flops // (4 * width)),
+        name="attend",
+    )(*args)
+
+
+def split_body(core_ref, k_ref, v_ref, keep_ref, give_ref, turned):
+    half = k_ref.shape[1] // 2
+    for which, ref in enumerate((k_ref, v_ref)):
+        turned[which] = jnp.swapaxes(ref[...].astype(jnp.float32), 0, 1).astype(jnp.bfloat16)
+    core = core_ref[0]
+    keep_ref[...] = turned[:, pl.ds(core * half, half)]
+    give_ref[...] = turned[:, pl.ds((1 - core) * half, half)]
+
+
+def split_heads(core, keys, values):
+    rows, kv_total, width = keys.shape
+    vm = pl.BlockSpec(memory_space=pltpu.VMEM)
+    half = jax.ShapeDtypeStruct((2, kv_total // 2, rows, width), jnp.bfloat16)
+    return pl.pallas_call(
+        split_body,
+        out_shape=[half, half],
+        in_specs=[pl.BlockSpec(memory_space=pltpu.SMEM), vm, vm],
+        out_specs=[vm, vm],
+        scratch_shapes=[pltpu.VMEM((2, kv_total, rows, width), jnp.bfloat16)],
+        compiler_params=pltpu.CompilerParams(vmem_limit_bytes=8 * 1024 * 1024),
+        cost_estimate=pl.CostEstimate(flops=0, bytes_accessed=512 * 1024, transcendentals=0),
+        name="split",
+    )(core, keys, values)
+
+
+def join_body(core_ref, mine_ref, other_ref, out_ref):
+    half = mine_ref.shape[1]
+    core = core_ref[0]
+    out_ref[:, pl.ds(pl.multiple_of(core * half, half), half), :] = mine_ref[...]
+    out_ref[:, pl.ds(pl.multiple_of((1 - core) * half, half), half), :] = other_ref[...]
+
+
+def join_heads(core, mine, other):
+    rows, half, width = mine.shape
+    vm = pl.BlockSpec(memory_space=pltpu.VMEM)
+    return pl.pallas_call(
+        join_body,
+        out_shape=jax.ShapeDtypeStruct((rows, 2 * half, width), jnp.bfloat16),
+        in_specs=[pl.BlockSpec(memory_space=pltpu.SMEM), vm, vm],
+        out_specs=vm,
+        compiler_params=pltpu.CompilerParams(vmem_limit_bytes=8 * 1024 * 1024),
+        cost_estimate=pl.CostEstimate(flops=0, bytes_accessed=2 << 20, transcendentals=0),
+        name="join",
+    )(core, mine, other)
+
+
+def by_key_block(queries, keys, values, vert_blocks, vert_count, slash_offsets, slash_count):
+    planes = lax.axis_size("seq")
+    plane = lax.axis_index("seq")
+    place = lax.axis_index("blk")
+    core, column = place % 2, place // 2
+    up = [(i, i + 1) for i in range(planes - 1)]
+
+    def climb(tile):
+        return lax.ppermute(tile, "seq", up)
+
+    def across(tile):
+        return lax.ppermute(tile, "blk", [(0, 2), (2, 0), (1, 3), (3, 1)])
+
+    def sibling(tile):
+        return lax.ppermute(tile, "blk", [(0, 1), (1, 0), (2, 3), (3, 2)])
+
+    core_id = core[None]
+    keep, give = split_heads(core_id, keys, values)
+    patterns = (vert_blocks.T, vert_count[None], slash_offsets.T, slash_count[None])
+    mine, theirs = keep, sibling(give)
+    sibling_queries = sibling(queries)
+    state = None
+    slots = jnp.stack([2 * column + core, 2 * column + 1 - core, 2 * (1 - column) + core, 2 * (1 - column) + 1 - core])
+    own_ids = jnp.stack([core, plane * 4 + slots[0], plane * 4 + slots[1]])
+    for stage in range(planes):
+        tiles = [mine, theirs, across(mine), across(theirs)]
+        ids = jnp.concatenate([own_ids, (plane - stage) * 4 + slots])
+        last = stage == planes - 1
+        state = attend_stage(ids, patterns, queries, sibling_queries, tiles, state, last)
+        if not last:
+            mine, theirs = climb(mine), climb(theirs)
+    own_rows, sibling_rows = state
+    return join_heads(core_id, own_rows, sibling(sibling_rows))
+
+
+def on_device(queries, keys, values, vert_blocks, vert_count, slash_offsets, slash_count):
+    gathered = 2 * keys.size * keys.dtype.itemsize * lax.axis_size("seq") * lax.axis_size("blk")
+    fits = gathered <= GATHER_BYTES and keys.shape[0] == BLOCK and lax.axis_size("blk") == 4
+    plan = by_key_block if fits else by_head_owner
+    return plan(queries, keys, values, vert_blocks, vert_count, slash_offsets, slash_count)
+
+
 def solution(mesh):
     return jax.shard_map(
         on_device,

time: 450 us -> 53.7 us (0.12)
  local copies, waits for them, and re-layouts: 198 us -> 5.76 us
  matrix products: 83.1 us -> 0 us
  other arithmetic: 49.5 us -> 0.24 us
  loops' own time: 47 us -> 0 us
  blocking collectives: 44.8 us -> 0 us
  starting transfers between devices: 12.3 us -> 31.2 us
  Pallas kernels: 0 us -> 12 us
  waiting for transfers between devices: 10.6 us -> 3.42 us
    dot_general x64 -> x0, matrix products: 83.1 us -> none  [the longest x16 40 us: sparse_block(): jnp.einsum('gid,gsjd->gisj', query_tiles, slash_keys, preferred_element_t...]
    reshape x36 -> x0, local copies, waits for them, and re-layouts: 72.1 us -> none  [the longest x16 34.8 us: sparse_block(): jnp.where(vert_mask, vert_scores, -jnp.inf)]
    another operation x1 -> x0, loops' own time: 47 us -> none  [on_device(): attended = lax.map(attend, jnp.arange(per_owner * groups, dtype=jnp.int32))]
    dynamic_slice x64 -> x0, local copies, waits for them, and re-layouts: 42.8 us -> none  [the longest x16 13.6 us: attend(): head_queries = lax.dynamic_index_in_dim(query_heads, slot_id, 0, False)]
    gather x64 -> x0, local copies, waits for them, and re-layouts: 42.2 us -> none  [the longest x16 11.6 us: attend(): slash_keys = jnp.take(head_keys, clamped, axis=0)]
    ppermute x0 -> x17, starting transfers between devices: none -> 31.2 us  [the longest x6 19.5 us: climb(): return lax.ppermute(tile, 'seq', up)]
    all_to_all x1 -> x0, blocking collectives: 27.3 us -> none  [on_device(): lax.all_to_all(attended, 'seq', split_axis=1, concat_axis=1, tiled=True)]
    all_gather x2 -> x0, blocking collectives: 17.5 us -> none  [the longest x1 10.3 us: on_device(): lax.all_gather(value_part, 'blk', axis=0, tiled=True)]
  transfers between devices with their start and end apart: 3 -> 17, of which waited for: 3 -> 2; matrix products, arithmetic and copies ran while one was open for 1% -> 0% of each run, Pallas kernels for 0% -> 15%
where the time goes in v1:
time: 53.7 us; the launch traced here: 52.8 us
  starting transfers between devices  31.2 us (58%)
  Pallas kernels  12 us (22%)
  local copies, waits for them, and re-layouts  5.76 us (11%)
  waiting for transfers between devices  3.42 us (6%)
    ppermute x6, starting transfers between devices, climb(): return lax.ppermute(tile, 'seq', up)  19.5 us
    pallas_call x4, Pallas kernels, attend_stage(): pl.pallas_call(functools.partial(stage_body, first, last, len(tiles), kv_...  10.8 us
    ppermute x8, starting transfers between devices, across(): return lax.ppermute(tile, 'blk', [(0, 2), (2, 0), (1, 3), (3, 1)])  6.91 us
    unnamed x24, local copies, waits for them, and re-layouts  5.76 us
    ppermute x3, starting transfers between devices, sibling(): return lax.ppermute(tile, 'blk', [(0, 1), (1, 0), (2, 3), (3, 2)])  4.8 us
    ppermute x6, waiting for transfers between devices, climb(): return lax.ppermute(tile, 'seq', up)  1.86 us
    ppermute x3, waiting for transfers between devices, sibling(): return lax.ppermute(tile, 'blk', [(0, 1), (1, 0), (2, 3), (3, 2)])  1.54 us
  transfers between devices with their start and end apart: 17, of which 2 were waited for; matrix products, arithmetic and copies ran while one was open for 0% of the time, Pallas kernels for 15%

profile of v1, /device:TPU:1, one launch (start us, length us, event | category | flops | bytes accessed | tf_op | source)
XLA Modules:
  0.0 52.8 jit_solution(9643362279405724318)
XLA Ops:
  0.0 0.1 collective-permute-start
  0.1 0.0 copy-start.6
  0.1 0.9 %copy-done.6 = bf16[64,8,128]{2,1,0:T(8,128)(2,1)S(1)} copy-done((bf16[64,8,128]{2,1,0:T(8,128)(2,1)S(1)}, bf16[64,8,128]{2,1,0:T(8,128)(2,1)}, u32[]{:S(2)}) %copy-start.6) | copy-done | bytes 131096
  1.0 0.0 copy-start.7
  1.0 0.9 %copy-done.7 = bf16[64,8,128]{2,1,0:T(8,128)(2,1)S(1)} copy-done((bf16[64,8,128]{2,1,0:T(8,128)(2,1)S(1)}, bf16[64,8,128]{2,1,0:T(8,128)(2,1)}, u32[]{:S(2)}) %copy-start.7) | copy-done | bytes 131096
  1.9 0.1 split.1
  2.0 0.5 collective-permute-start.4
  2.5 4.2 %collective-permute-start.1 = (bf16[2,4,64,128]{3,2,1,0:T(8,128)(2,1)S(1)}, bf16[2,4,64,128]{3,2,1,0:T(8,128)(2,1)S(1)}, u32[]{:S(2)}, u32[]{:S(2)}) collective-permute-start(bf16[2,4,64,128]{3,2,1,0:T(8,128)(2,1)S(1)} %get-tuple-element.18.refs_7_), channel_id=1, source_target_pairs={{0,4},{4,8},{8,12},{1,5},{5,9},{9,13},{2,6},{6,10},{10,14},{3,7},{... | collective-permute-start | bytes 393224 | tf_op jit(solution)/shard_map/ppermute | solution.py:347
  6.8 1.3 %collective-permute-start.14 = (bf16[2,4,64,128]{3,2,1,0:T(8,128)(2,1)S(1)}, bf16[2,4,64,128]{3,2,1,0:T(8,128)(2,1)S(1)}, u32[]{:S(2)}, u32[]{:S(2)}) collective-permute-start(bf16[2,4,64,128]{3,2,1,0:T(8,128)(2,1)S(1)} %get-tuple-element.18.refs_7_), channel_id=1, source_target_pairs={{0,2},{2,0},{1,3},{3,1},{4,6},{6,4},{5,7},{7,5},{8,10},{10,8},{9,1... | collective-permute-start | bytes 393224 | tf_op jit(solution)/shard_map/ppermute | solution.py:350
  8.0 0.0 collective-permute-done.4.refs_8_
  8.0 3.2 %collective-permute-start.5 = (bf16[2,4,64,128]{3,2,1,0:T(8,128)(2,1)S(1)}, bf16[2,4,64,128]{3,2,1,0:T(8,128)(2,1)S(1)}, u32[]{:S(2)}, u32[]{:S(2)}) collective-permute-start(bf16[2,4,64,128]{3,2,1,0:T(8,128)(2,1)S(1)} %collective-permute-done.4.refs_8_), channel_id=1, source_target_pairs={{0,4},{4,8},{8,12},{1,5},{5,9},{9,13},{2,6},{6,10},{10,14},{3,7},{... | collective-permute-start | bytes 393224 | tf_op jit(solution)/shard_map/ppermute | solution.py:347
  11.2 0.0 collective-permute-done.1.refs_7_
  11.3 3.2 %collective-permute-start.2 = (bf16[2,4,64,128]{3,2,1,0:T(8,128)(2,1)S(1)}, bf16[2,4,64,128]{3,2,1,0:T(8,128)(2,1)S(1)}, u32[]{:S(2)}, u32[]{:S(2)}) collective-permute-start(bf16[2,4,64,128]{3,2,1,0:T(8,128)(2,1)S(1)} %collective-permute-done.1.refs_7_), channel_id=1, source_target_pairs={{0,4},{4,8},{8,12},{1,5},{5,9},{9,13},{2,6},{6,10},{10,14},{3,7},{... | collective-permute-start | bytes 393224 | tf_op jit(solution)/shard_map/ppermute | solution.py:347
  14.5 0.1 broadcast_add_fusion
  14.6 0.3 collective-permute-start.15
  14.8 0.0 collective-permute-done.14.refs_9_
  14.8 1.2 %collective-permute-start.12 = (bf16[2,4,64,128]{3,2,1,0:T(8,128)(2,1)S(1)}, bf16[2,4,64,128]{3,2,1,0:T(8,128)(2,1)S(1)}, u32[]{:S(2)}, u32[]{:S(2)}) collective-permute-start(bf16[2,4,64,128]{3,2,1,0:T(8,128)(2,1)S(1)} %collective-permute-done.1.refs_7_), channel_id=1, source_target_pairs={{0,2},{2,0},{1,3},{3,1},{4,6},{6,4},{5,7},{7,5},{8,10},{10,8},{9,1... | collective-permute-start | bytes 393224 | tf_op jit(solution)/shard_map/ppermute | solution.py:350
  16.1 0.0 collective-permute-done.5.refs_8_
  16.1 2.0 %collective-permute-start.6 = (bf16[2,4,64,128]{3,2,1,0:T(8,128)(2,1)S(1)}, bf16[2,4,64,128]{3,2,1,0:T(8,128)(2,1)S(1)}, u32[]{:S(2)}, u32[]{:S(2)}) collective-permute-start(bf16[2,4,64,128]{3,2,1,0:T(8,128)(2,1)S(1)} %collective-permute-done.5.refs_8_), channel_id=1, source_target_pairs={{0,4},{4,8},{8,12},{1,5},{5,9},{9,13},{2,6},{6,10},{10,14},{3,7},{... | collective-permute-start | bytes 393224 | tf_op jit(solution)/shard_map/ppermute | solution.py:347
  18.0 0.0 collective-permute-done.2.refs_7_
  18.0 3.2 %collective-permute-start.3 = (bf16[2,4,64,128]{3,2,1,0:T(8,128)(2,1)S(1)}, bf16[2,4,64,128]{3,2,1,0:T(8,128)(2,1)S(1)}, u32[]{:S(2)}, u32[]{:S(2)}) collective-permute-start(bf16[2,4,64,128]{3,2,1,0:T(8,128)(2,1)S(1)} %collective-permute-done.2.refs_7_), channel_id=1, source_target_pairs={{0,4},{4,8},{8,12},{1,5},{5,9},{9,13},{2,6},{6,10},{10,14},{3,7},{... | collective-permute-start | bytes 393224 | tf_op jit(solution)/shard_map/ppermute | solution.py:347
  21.3 0.1 pad_add_fusion.5
  21.3 0.0 collective-permute-done.15.refs_10_
  21.3 1.2 %collective-permute-start.13 = (bf16[2,4,64,128]{3,2,1,0:T(8,128)(2,1)S(1)}, bf16[2,4,64,128]{3,2,1,0:T(8,128)(2,1)S(1)}, u32[]{:S(2)}, u32[]{:S(2)}) collective-permute-start(bf16[2,4,64,128]{3,2,1,0:T(8,128)(2,1)S(1)} %collective-permute-done.5.refs_8_), channel_id=1, source_target_pairs={{0,2},{2,0},{1,3},{3,1},{4,6},{6,4},{5,7},{7,5},{8,10},{10,8},{9,1... | collective-permute-start | bytes 393224 | tf_op jit(solution)/shard_map/ppermute | solution.py:350
  22.6 0.0 collective-permute-done.12.refs_9_
  22.6 0.3 collective-permute-start.10
  22.8 0.0 collective-permute-done.6.refs_8_
  22.8 1.2 %collective-permute-start.11 = (bf16[2,4,64,128]{3,2,1,0:T(8,128)(2,1)S(1)}, bf16[2,4,64,128]{3,2,1,0:T(8,128)(2,1)S(1)}, u32[]{:S(2)}, u32[]{:S(2)}) collective-permute-start(bf16[2,4,64,128]{3,2,1,0:T(8,128)(2,1)S(1)} %collective-permute-done.6.refs_8_), channel_id=1, source_target_pairs={{0,2},{2,0},{1,3},{3,1},{4,6},{6,4},{5,7},{7,5},{8,10},{10,8},{9,1... | collective-permute-start | bytes 393224 | tf_op jit(solution)/shard_map/ppermute | solution.py:350
  24.0 0.0 collective-permute-done.3.refs_7_
  24.0 3.7 %collective-permute-start.7 = (bf16[2,4,64,128]{3,2,1,0:T(8,128)(2,1)S(1)}, bf16[2,4,64,128]{3,2,1,0:T(8,128)(2,1)S(1)}, u32[]{:S(2)}, u32[]{:S(2)}) collective-permute-start(bf16[2,4,64,128]{3,2,1,0:T(8,128)(2,1)S(1)} %collective-permute-done.6.refs_8_), channel_id=1, source_target_pairs={{0,4},{4,8},{8,12},{1,5},{5,9},{9,13},{2,6},{6,10},{10,14},{3,7},{... | collective-permute-start | bytes 393224 | tf_op jit(solution)/shard_map/ppermute | solution.py:347
  27.8 0.1 pad_add_fusion.4
  27.8 1.8 %collective-permute-done.7.refs_8_ = bf16[2,4,64,128]{3,2,1,0:T(8,128)(2,1)S(1)} collective-permute-done((bf16[2,4,64,128]{3,2,1,0:T(8,128)(2,1)S(1)}, bf16[2,4,64,128]{3,2,1,0:T(8,128)(2,1)S(1)}, u32[]{:S(2)}, u32[]{:S(2)}) %collective-permute-start.7) | collective-permute-done | bytes 131104 | tf_op jit(solution)/shard_map/ppermute | solution.py:347
  29.7 1.2 %collective-permute-start.8 = (bf16[2,4,64,128]{3,2,1,0:T(8,128)(2,1)S(1)}, bf16[2,4,64,128]{3,2,1,0:T(8,128)(2,1)S(1)}, u32[]{:S(2)}, u32[]{:S(2)}) collective-permute-start(bf16[2,4,64,128]{3,2,1,0:T(8,128)(2,1)S(1)} %collective-permute-done.3.refs_7_), channel_id=1, source_target_pairs={{0,2},{2,0},{1,3},{3,1},{4,6},{6,4},{5,7},{7,5},{8,10},{10,8},{9,1... | collective-permute-start | bytes 393224 | tf_op jit(solution)/shard_map/ppermute | solution.py:350
  30.9 0.0 collective-permute-done.refs_6_
  30.9 0.3 collective-permute-start.9
  31.1 0.0 copy-start
  31.1 1.2 %copy-done = bf16[64,64,128]{2,1,0:T(8,128)(2,1)S(1)} copy-done((bf16[64,64,128]{2,1,0:T(8,128)(2,1)S(1)}, bf16[64,64,128]{2,1,0:T(8,128)(2,1)}, u32[]{:S(2)}) %copy-start) | copy-done | bytes 1048600
  32.4 0.0 copy-start.2
  32.4 0.7 %copy-done.2 = s32[64,16]{0,1:T(8,128)S(1)} copy-done((s32[64,16]{0,1:T(8,128)S(1)}, s32[64,16]{0,1:T(8,128)}, u32[]{:S(2)}) %copy-start.2) | copy-done | bytes 4120
  33.1 0.0 copy-start.4
  33.1 0.7 %copy-done.4 = s32[64,14]{0,1:T(8,128)S(1)} copy-done((s32[64,14]{0,1:T(8,128)S(1)}, s32[64,14]{0,1:T(8,128)}, u32[]{:S(2)}) %copy-start.4) | copy-done | bytes 3608
  33.8 0.7 %copy-done.8 = s32[64]{0:T(128)S(1)} copy-done((s32[64]{0:T(128)S(1)}, s32[64]{0:T(128)}, u32[]{:S(2)}) %copy-start.8) | copy-done | bytes 280
  34.4 0.7 %copy-done.10 = s32[64]{0:T(128)S(1)} copy-done((s32[64]{0:T(128)S(1)}, s32[64]{0:T(128)}, u32[]{:S(2)}) %copy-start.10) | copy-done | bytes 280
  35.1 2.2 %attend.4 = (f32[2,4,512,128]{3,2,1,0:T(8,128)S(1)}, f32[2,4,512,128]{3,2,1,0:T(8,128)S(1)}, f32[2,4,512,128]{3,2,1,0:T(8,128)S(1)}) custom-call(s32[7]{0:T(128)S(1)} %get-tuple-element.31.refs_0_, s32[16,64]{1,0:T(8,128)S(1)} %bitcast.11, s32[1,64]{1,0:T(1,128)S(1)} %bitcast.19, s32[14,64]{1,0:T(8,128)S(1)} %bitcast.15, s32[1,64]{1,0:T(1,128)S(1)} %bitcast.23, ...), custom_call_target="tpu_custom_call" | custom-call | flops 536870912 | bytes 4194304 | tf_op jit(solution)/shard_map/attend/pallas_call | solution.py:281
  37.3 0.0 collective-permute-done.13.refs_10_
  37.3 0.0 copy-done.1
  37.3 0.0 copy-start.3
  37.3 0.0 copy-start.5
  37.3 0.0 copy-start.9
  37.3 0.0 copy-start.11
  37.3 2.8 %attend.5 = (f32[2,4,512,128]{3,2,1,0:T(8,128)S(1)}, f32[2,4,512,128]{3,2,1,0:T(8,128)S(1)}, f32[2,4,512,128]{3,2,1,0:T(8,128)S(1)}) custom-call(s32[7]{0:T(128)S(1)} %get-tuple-element.35.refs_0_, s32[16,64]{1,0:T(8,128)S(1)} %bitcast.12, s32[1,64]{1,0:T(1,128)S(1)} %bitcast.20, s32[14,64]{1,0:T(8,128)S(1)} %bitcast.16, s32[1,64]{1,0:T(1,128)S(1)} %bitcast.24, ...), custom_call_target="tpu_custom_call" | custom-call | flops 536870912 | bytes 4194304 | tf_op jit(solution)/shard_map/attend/pallas_call | solution.py:281
  40.2 0.0 collective-permute-done.10.refs_9_
  40.2 0.0 collective-permute-done.11.refs_10_
  40.2 0.0 copy-done.3
  40.2 0.0 copy-done.5
  40.2 0.0 copy-done.9
  40.2 0.0 copy-done.11
  40.2 2.8 %attend.6 = (f32[2,4,512,128]{3,2,1,0:T(8,128)S(1)}, f32[2,4,512,128]{3,2,1,0:T(8,128)S(1)}, f32[2,4,512,128]{3,2,1,0:T(8,128)S(1)}) custom-call(s32[7]{0:T(128)S(1)} %get-tuple-element.36.refs_0_, s32[16,64]{1,0:T(8,128)S(1)} %bitcast.13, s32[1,64]{1,0:T(1,128)S(1)} %bitcast.21, s32[14,64]{1,0:T(8,128)S(1)} %bitcast.17, s32[1,64]{1,0:T(1,128)S(1)} %bitcast.25, ...), custom_call_target="tpu_custom_call" | custom-call | flops 536870912 | bytes 4194304 | tf_op jit(solution)/shard_map/attend/pallas_call | solution.py:281
  43.0 0.0 collective-permute-done.8.refs_9_
  43.0 0.0 collective-permute-done.9.refs_10_
  43.0 3.0 %attend.7 = (bf16[64,32,128]{2,1,0:T(8,128)(2,1)S(1)}, bf16[64,32,128]{2,1,0:T(8,128)(2,1)S(1)}) custom-call(s32[7]{0:T(128)S(1)} %get-tuple-element.37.refs_0_, s32[16,64]{1,0:T(8,128)S(1)} %bitcast.14, s32[1,64]{1,0:T(1,128)S(1)} %bitcast.22, s32[14,64]{1,0:T(8,128)S(1)} %bitcast.18, s32[1,64]{1,0:T(1,128)S(1)} %bitcast.26, ...), custom_call_target="tpu_custom_call" | custom-call | flops 536870912 | bytes 4194304 | tf_op jit(solution)/shard_map/attend/pallas_call | solution.py:281
  46.0 4.2 %collective-permute-start.16 = (bf16[64,32,128]{2,1,0:T(8,128)(2,1)S(1)}, bf16[64,32,128]{2,1,0:T(8,128)(2,1)S(1)}, u32[]{:S(2)}, u32[]{:S(2)}) collective-permute-start(bf16[64,32,128]{2,1,0:T(8,128)(2,1)S(1)} %get-tuple-element.30), channel_id=1, source_target_pairs={{0,1},{1,0},{2,3},{3,2},{4,5},{5,4},{6,7},{7,6},{8,9},{9,8},{10,11... | collective-permute-start | bytes 1572872 | tf_op jit(solution)/shard_map/ppermute | solution.py:353
  50.2 1.5 %collective-permute-done.16.other_ref = bf16[64,32,128]{2,1,0:T(8,128)(2,1)S(1)} collective-permute-done((bf16[64,32,128]{2,1,0:T(8,128)(2,1)S(1)}, bf16[64,32,128]{2,1,0:T(8,128)(2,1)S(1)}, u32[]{:S(2)}, u32[]{:S(2)}) %collective-permute-start.16) | collective-permute-done | bytes 524320 | tf_op jit(solution)/shard_map/ppermute | solution.py:353
  51.8 1.1 %join.1 = bf16[64,64,128]{2,1,0:T(8,128)(2,1)} custom-call(s32[1]{0:T(128)} %bitcast.core_ref, bf16[64,32,128]{2,1,0:T(8,128)(2,1)S(1)} %get-tuple-element.29.mine_ref, bf16[64,32,128]{2,1,0:T(8,128)(2,1)S(1)} %collective-permute-done.16.other_ref), custom_call_target="tpu_custom_call" | custom-call | bytes 2097152 | tf_op jit(solution)/shard_map/join/pallas_call | solution.py:328
  (4 shorter events, 0.0 us)
Async XLA Ops:
  0.0 30.9 %collective-permute-start = (bf16[64,64,128]{2,1,0:T(8,128)(2,1)}, bf16[64,64,128]{2,1,0:T(8,128)(2,1)S(1)}, u32[]{:S(2)}, u32[]{:S(2)}) collective-permute-start(bf16[64,64,128]{2,1,0:T(8,128)(2,1)} %refs_5_.7), channel_id=1, source_target_pairs={{0,1},{1,0},{2,3},{3,2},{4,5},{5,4},{6,7},{7,6},{8,9},{9,8},{10,11... | collective-permute-start | bytes 3145736 | tf_op jit(solution)/shard_map/ppermute | solution.py:353
  0.1 0.9 %copy-start.6 = (bf16[64,8,128]{2,1,0:T(8,128)(2,1)S(1)}, bf16[64,8,128]{2,1,0:T(8,128)(2,1)}, u32[]{:S(2)}) copy-start(bf16[64,8,128]{2,1,0:T(8,128)(2,1)} %k_ref.1) | copy-start | bytes 393220
  1.0 0.9 %copy-start.7 = (bf16[64,8,128]{2,1,0:T(8,128)(2,1)S(1)}, bf16[64,8,128]{2,1,0:T(8,128)(2,1)}, u32[]{:S(2)}) copy-start(bf16[64,8,128]{2,1,0:T(8,128)(2,1)} %v_ref.1) | copy-start | bytes 393220
  2.0 6.0 %collective-permute-start.4 = (bf16[2,4,64,128]{3,2,1,0:T(8,128)(2,1)S(1)}, bf16[2,4,64,128]{3,2,1,0:T(8,128)(2,1)S(1)}, u32[]{:S(2)}, u32[]{:S(2)}) collective-permute-start(bf16[2,4,64,128]{3,2,1,0:T(8,128)(2,1)S(1)} %get-tuple-element.19), channel_id=1, source_target_pairs={{0,1},{1,0},{2,3},{3,2},{4,5},{5,4},{6,7},{7,6},{8,9},{9,8},{10,11... | collective-permute-start | bytes 393224 | tf_op jit(solution)/shard_map/ppermute | solution.py:353
  2.5 8.7 %collective-permute-start.1 = (bf16[2,4,64,128]{3,2,1,0:T(8,128)(2,1)S(1)}, bf16[2,4,64,128]{3,2,1,0:T(8,128)(2,1)S(1)}, u32[]{:S(2)}, u32[]{:S(2)}) collective-permute-start(bf16[2,4,64,128]{3,2,1,0:T(8,128)(2,1)S(1)} %get-tuple-element.18.refs_7_), channel_id=1, source_target_pairs={{0,4},{4,8},{8,12},{1,5},{5,9},{9,13},{2,6},{6,10},{10,14},{3,7},{... | collective-permute-start | bytes 393224 | tf_op jit(solution)/shard_map/ppermute | solution.py:347
  6.8 8.1 %collective-permute-start.14 = (bf16[2,4,64,128]{3,2,1,0:T(8,128)(2,1)S(1)}, bf16[2,4,64,128]{3,2,1,0:T(8,128)(2,1)S(1)}, u32[]{:S(2)}, u32[]{:S(2)}) collective-permute-start(bf16[2,4,64,128]{3,2,1,0:T(8,128)(2,1)S(1)} %get-tuple-element.18.refs_7_), channel_id=1, source_target_pairs={{0,2},{2,0},{1,3},{3,1},{4,6},{6,4},{5,7},{7,5},{8,10},{10,8},{9,1... | collective-permute-start | bytes 393224 | tf_op jit(solution)/shard_map/ppermute | solution.py:350
  8.0 8.0 %collective-permute-start.5 = (bf16[2,4,64,128]{3,2,1,0:T(8,128)(2,1)S(1)}, bf16[2,4,64,128]{3,2,1,0:T(8,128)(2,1)S(1)}, u32[]{:S(2)}, u32[]{:S(2)}) collective-permute-start(bf16[2,4,64,128]{3,2,1,0:T(8,128)(2,1)S(1)} %collective-permute-done.4.refs_8_), channel_id=1, source_target_pairs={{0,4},{4,8},{8,12},{1,5},{5,9},{9,13},{2,6},{6,10},{10,14},{3,7},{... | collective-permute-start | bytes 393224 | tf_op jit(solution)/shard_map/ppermute | solution.py:347
  11.3 6.8 %collective-permute-start.2 = (bf16[2,4,64,128]{3,2,1,0:T(8,128)(2,1)S(1)}, bf16[2,4,64,128]{3,2,1,0:T(8,128)(2,1)S(1)}, u32[]{:S(2)}, u32[]{:S(2)}) collective-permute-start(bf16[2,4,64,128]{3,2,1,0:T(8,128)(2,1)S(1)} %collective-permute-done.1.refs_7_), channel_id=1, source_target_pairs={{0,4},{4,8},{8,12},{1,5},{5,9},{9,13},{2,6},{6,10},{10,14},{3,7},{... | collective-permute-start | bytes 393224 | tf_op jit(solution)/shard_map/ppermute | solution.py:347
  14.6 6.8 %collective-permute-start.15 = (bf16[2,4,64,128]{3,2,1,0:T(8,128)(2,1)S(1)}, bf16[2,4,64,128]{3,2,1,0:T(8,128)(2,1)S(1)}, u32[]{:S(2)}, u32[]{:S(2)}) collective-permute-start(bf16[2,4,64,128]{3,2,1,0:T(8,128)(2,1)S(1)} %collective-permute-done.4.refs_8_), channel_id=1, source_target_pairs={{0,2},{2,0},{1,3},{3,1},{4,6},{6,4},{5,7},{7,5},{8,10},{10,8},{9,1... | collective-permute-start | bytes 393224 | tf_op jit(solution)/shard_map/ppermute | solution.py:350
  14.8 7.7 %collective-permute-start.12 = (bf16[2,4,64,128]{3,2,1,0:T(8,128)(2,1)S(1)}, bf16[2,4,64,128]{3,2,1,0:T(8,128)(2,1)S(1)}, u32[]{:S(2)}, u32[]{:S(2)}) collective-permute-start(bf16[2,4,64,128]{3,2,1,0:T(8,128)(2,1)S(1)} %collective-permute-done.1.refs_7_), channel_id=1, source_target_pairs={{0,2},{2,0},{1,3},{3,1},{4,6},{6,4},{5,7},{7,5},{8,10},{10,8},{9,1... | collective-permute-start | bytes 393224 | tf_op jit(solution)/shard_map/ppermute | solution.py:350
  16.1 6.8 %collective-permute-start.6 = (bf16[2,4,64,128]{3,2,1,0:T(8,128)(2,1)S(1)}, bf16[2,4,64,128]{3,2,1,0:T(8,128)(2,1)S(1)}, u32[]{:S(2)}, u32[]{:S(2)}) collective-permute-start(bf16[2,4,64,128]{3,2,1,0:T(8,128)(2,1)S(1)} %collective-permute-done.5.refs_8_), channel_id=1, source_target_pairs={{0,4},{4,8},{8,12},{1,5},{5,9},{9,13},{2,6},{6,10},{10,14},{3,7},{... | collective-permute-start | bytes 393224 | tf_op jit(solution)/shard_map/ppermute | solution.py:347
  18.0 6.0 %collective-permute-start.3 = (bf16[2,4,64,128]{3,2,1,0:T(8,128)(2,1)S(1)}, bf16[2,4,64,128]{3,2,1,0:T(8,128)(2,1)S(1)}, u32[]{:S(2)}, u32[]{:S(2)}) collective-permute-start(bf16[2,4,64,128]{3,2,1,0:T(8,128)(2,1)S(1)} %collective-permute-done.2.refs_7_), channel_id=1, source_target_pairs={{0,4},{4,8},{8,12},{1,5},{5,9},{9,13},{2,6},{6,10},{10,14},{3,7},{... | collective-permute-start | bytes 393224 | tf_op jit(solution)/shard_map/ppermute | solution.py:347
  21.3 15.9 %collective-permute-start.13 = (bf16[2,4,64,128]{3,2,1,0:T(8,128)(2,1)S(1)}, bf16[2,4,64,128]{3,2,1,0:T(8,128)(2,1)S(1)}, u32[]{:S(2)}, u32[]{:S(2)}) collective-permute-start(bf16[2,4,64,128]{3,2,1,0:T(8,128)(2,1)S(1)} %collective-permute-done.5.refs_8_), channel_id=1, source_target_pairs={{0,2},{2,0},{1,3},{3,1},{4,6},{6,4},{5,7},{7,5},{8,10},{10,8},{9,1... | collective-permute-start | bytes 393224 | tf_op jit(solution)/shard_map/ppermute | solution.py:350
  22.6 17.6 %collective-permute-start.10 = (bf16[2,4,64,128]{3,2,1,0:T(8,128)(2,1)S(1)}, bf16[2,4,64,128]{3,2,1,0:T(8,128)(2,1)S(1)}, u32[]{:S(2)}, u32[]{:S(2)}) collective-permute-start(bf16[2,4,64,128]{3,2,1,0:T(8,128)(2,1)S(1)} %collective-permute-done.2.refs_7_), channel_id=1, source_target_pairs={{0,2},{2,0},{1,3},{3,1},{4,6},{6,4},{5,7},{7,5},{8,10},{10,8},{9,1... | collective-permute-start | bytes 393224 | tf_op jit(solution)/shard_map/ppermute | solution.py:350
  22.8 17.3 %collective-permute-start.11 = (bf16[2,4,64,128]{3,2,1,0:T(8,128)(2,1)S(1)}, bf16[2,4,64,128]{3,2,1,0:T(8,128)(2,1)S(1)}, u32[]{:S(2)}, u32[]{:S(2)}) collective-permute-start(bf16[2,4,64,128]{3,2,1,0:T(8,128)(2,1)S(1)} %collective-permute-done.6.refs_8_), channel_id=1, source_target_pairs={{0,2},{2,0},{1,3},{3,1},{4,6},{6,4},{5,7},{7,5},{8,10},{10,8},{9,1... | collective-permute-start | bytes 393224 | tf_op jit(solution)/shard_map/ppermute | solution.py:350
  24.0 5.6 %collective-permute-start.7 = (bf16[2,4,64,128]{3,2,1,0:T(8,128)(2,1)S(1)}, bf16[2,4,64,128]{3,2,1,0:T(8,128)(2,1)S(1)}, u32[]{:S(2)}, u32[]{:S(2)}) collective-permute-start(bf16[2,4,64,128]{3,2,1,0:T(8,128)(2,1)S(1)} %collective-permute-done.6.refs_8_), channel_id=1, source_target_pairs={{0,4},{4,8},{8,12},{1,5},{5,9},{9,13},{2,6},{6,10},{10,14},{3,7},{... | collective-permute-start | bytes 393224 | tf_op jit(solution)/shard_map/ppermute | solution.py:347
  29.7 13.3 %collective-permute-start.8 = (bf16[2,4,64,128]{3,2,1,0:T(8,128)(2,1)S(1)}, bf16[2,4,64,128]{3,2,1,0:T(8,128)(2,1)S(1)}, u32[]{:S(2)}, u32[]{:S(2)}) collective-permute-start(bf16[2,4,64,128]{3,2,1,0:T(8,128)(2,1)S(1)} %collective-permute-done.3.refs_7_), channel_id=1, source_target_pairs={{0,2},{2,0},{1,3},{3,1},{4,6},{6,4},{5,7},{7,5},{8,10},{10,8},{9,1... | collective-permute-start | bytes 393224 | tf_op jit(solution)/shard_map/ppermute | solution.py:350
  30.9 12.1 %collective-permute-start.9 = (bf16[2,4,64,128]{3,2,1,0:T(8,128)(2,1)S(1)}, bf16[2,4,64,128]{3,2,1,0:T(8,128)(2,1)S(1)}, u32[]{:S(2)}, u32[]{:S(2)}) collective-permute-start(bf16[2,4,64,128]{3,2,1,0:T(8,128)(2,1)S(1)} %collective-permute-done.7.refs_8_), channel_id=1, source_target_pairs={{0,2},{2,0},{1,3},{3,1},{4,6},{6,4},{5,7},{7,5},{8,10},{10,8},{9,1... | collective-permute-start | bytes 393224 | tf_op jit(solution)/shard_map/ppermute | solution.py:350
  31.1 1.2 %copy-start = (bf16[64,64,128]{2,1,0:T(8,128)(2,1)S(1)}, bf16[64,64,128]{2,1,0:T(8,128)(2,1)}, u32[]{:S(2)}) copy-start(bf16[64,64,128]{2,1,0:T(8,128)(2,1)} %refs_5_.7) | copy-start | bytes 3145732
  32.4 0.7 %copy-start.2 = (s32[64,16]{0,1:T(8,128)S(1)}, s32[64,16]{0,1:T(8,128)}, u32[]{:S(2)}) copy-start(s32[64,16]{0,1:T(8,128)} %param.10) | copy-start | bytes 12292
  33.1 0.7 %copy-start.4 = (s32[64,14]{0,1:T(8,128)S(1)}, s32[64,14]{0,1:T(8,128)}, u32[]{:S(2)}) copy-start(s32[64,14]{0,1:T(8,128)} %param.12) | copy-start | bytes 10756
  33.8 0.7 %copy-start.8 = (s32[64]{0:T(128)S(1)}, s32[64]{0:T(128)}, u32[]{:S(2)}) copy-start(s32[64]{0:T(128)} %param.11) | copy-start | bytes 772
  34.4 0.7 %copy-start.10 = (s32[64]{0:T(128)S(1)}, s32[64]{0:T(128)}, u32[]{:S(2)}) copy-start(s32[64]{0:T(128)} %param.13) | copy-start | bytes 772
  35.1 2.2 %copy-start.1 = (bf16[64,64,128]{2,1,0:T(8,128)(2,1)S(1)}, bf16[64,64,128]{2,1,0:T(8,128)(2,1)}, u32[]{:S(2)}) copy-start(bf16[64,64,128]{2,1,0:T(8,128)(2,1)} %refs_5_.7) | copy-start | bytes 3145732
  37.3 2.9 %copy-start.3 = (s32[64,16]{0,1:T(8,128)S(1)}, s32[64,16]{0,1:T(8,128)}, u32[]{:S(2)}) copy-start(s32[64,16]{0,1:T(8,128)} %param.10) | copy-start | bytes 12292
  37.3 2.9 %copy-start.5 = (s32[64,14]{0,1:T(8,128)S(1)}, s32[64,14]{0,1:T(8,128)}, u32[]{:S(2)}) copy-start(s32[64,14]{0,1:T(8,128)} %param.12) | copy-start | bytes 10756
  37.3 2.9 %copy-start.9 = (s32[64]{0:T(128)S(1)}, s32[64]{0:T(128)}, u32[]{:S(2)}) copy-start(s32[64]{0:T(128)} %param.11) | copy-start | bytes 772
  37.3 2.9 %copy-start.11 = (s32[64]{0:T(128)S(1)}, s32[64]{0:T(128)}, u32[]{:S(2)}) copy-start(s32[64]{0:T(128)} %param.13) | copy-start | bytes 772
  46.0 5.8 %collective-permute-start.16 = (bf16[64,32,128]{2,1,0:T(8,128)(2,1)S(1)}, bf16[64,32,128]{2,1,0:T(8,128)(2,1)S(1)}, u32[]{:S(2)}, u32[]{:S(2)}) collective-permute-start(bf16[64,32,128]{2,1,0:T(8,128)(2,1)S(1)} %get-tuple-element.30), channel_id=1, source_target_pairs={{0,1},{1,0},{2,3},{3,2},{4,5},{5,4},{6,7},{7,6},{8,9},{9,8},{10,11... | collective-permute-start | bytes 1572872 | tf_op jit(solution)/shard_map/ppermute | solution.py:353

commit v2 on v0

--- a/solution.py
+++ b/solution.py
@@ -1,11 +1,16 @@
+import functools
 import math
 
 import jax
 import jax.numpy as jnp
 from jax import lax
+from jax.experimental import pallas as pl
+from jax.experimental.pallas import tpu as pltpu
 from jax.sharding import PartitionSpec as P
 
 BLOCK = 64
+NEG = -1e30
+GATHER_BYTES = 8 << 20
 
 
 def slash_plan(query_index, vertical, vert_live, slash, slash_live):
@@ -75,7 +80,7 @@
     return result.astype(jnp.bfloat16).reshape(tile_count * block_len, head_width)
 
 
-def on_device(queries, keys, values, vert_blocks, vert_count, slash_offsets, slash_count):
+def by_head_owner(queries, keys, values, vert_blocks, vert_count, slash_offsets, slash_count):
     owners = lax.axis_size("seq")
     cycle_size = lax.axis_size("blk")
     owner_id = lax.axis_index("seq")
@@ -169,6 +174,288 @@
     return jnp.transpose(returned, (2, 1, 0, 3)).reshape(shard_rows, head_total, head_width)
 
 
+def listed(entries, live_count, wanted):
+    row = lax.broadcasted_iota(jnp.int32, entries.shape, 0)
+    hit = (entries == wanted) & (row < live_count)
+    return jnp.sum(jnp.where(hit, 1.0, 0.0), axis=0, keepdims=True)
+
+def pattern_body(stages, vert_rows, slash_rows, ids, lists, out_ref, taken_ref):
+    vert, vcount = lists[:vert_rows], lists[vert_rows:vert_rows + 1]
+    slash, scount = lists[vert_rows + 1:vert_rows + 1 + slash_rows], lists[vert_rows + 1 + slash_rows:]
+    half = out_ref.shape[2]
+    slots = out_ref.shape[3] // BLOCK
+    lo = pl.multiple_of(ids[0] * half, half)
+    spread = (
+        lax.broadcasted_iota(jnp.int32, (8, slots * BLOCK), 0)
+        == lax.broadcasted_iota(jnp.int32, (8, slots * BLOCK), 1) // BLOCK
+    )
+    spread = jnp.where(spread, 1.0, 0.0)
+    pad = jnp.zeros((8 - slots, lists.shape[1]), jnp.float32)
+    for stage in range(stages):
+        for b in range(2):
+            rows = []
+            for slot in range(slots):
+                key_block, query_block = ids[3 + stage * slots + slot], ids[1 + b]
+                n = listed(vert, vcount, key_block) + listed(slash, scount, query_block - key_block)
+                rows.append(n * jnp.where((key_block >= 0) & (key_block <= query_block), 1.0, 0.0))
+            taken = lax.dot_general(
+                jnp.concatenate(rows + [pad], axis=0),
+                spread,
+                (((0,), (0,)), ((), ())),
+                preferred_element_type=jnp.float32,
+            )
+            taken_ref[...] = jnp.where(taken > 0.5, 0.0, NEG)
+            out_ref[stage, b] = taken_ref[pl.ds(lo, half), :]
+
+
+def pattern_bias(ids, stages, slots, vert_rows, slash_rows, lists):
+    heads = lists.shape[1]
+    vm = pl.BlockSpec(memory_space=pltpu.VMEM)
+    return pl.pallas_call(
+        functools.partial(pattern_body, stages, vert_rows, slash_rows),
+        out_shape=jax.ShapeDtypeStruct((stages, 2, heads // 2, slots * BLOCK), jnp.float32),
+        in_specs=[pl.BlockSpec(memory_space=pltpu.SMEM), vm],
+        out_specs=vm,
+        scratch_shapes=[pltpu.VMEM((heads, slots * BLOCK), jnp.float32)],
+        compiler_params=pltpu.CompilerParams(vmem_limit_bytes=8 * 1024 * 1024),
+        cost_estimate=pl.CostEstimate(flops=1000, bytes_accessed=1000, transcendentals=0),
+        name="pattern",
+    )(ids, lists)
+
+
+def stage_body(stage, rows_of, slots, group, scale, *refs):
+    last = rows_of is not None
+    (bias, q_own, q_sib), refs = refs[:3], refs[3:]
+    tiles, refs = refs[:slots], refs[slots:]
+    first = stage == 0
+    if not first:
+        acc_in, top_in, sum_in = refs[:3]
+        refs = refs[3:]
+    if last:
+        core, out, *refs = refs
+        done_ref, *sems = refs if rows_of == "own" else (out,)
+    else:
+        acc_out, top_out, sum_out = refs
+    kv_heads, rows, head_width = q_own.shape
+    width = slots * BLOCK
+    if first:
+        pos = lax.broadcasted_iota(jnp.int32, (BLOCK, 1, 2 * BLOCK), 0)
+        key = lax.broadcasted_iota(jnp.int32, (BLOCK, 1, 2 * BLOCK), 2)
+    for b in {None: (0, 1), "own": (0,), "sibling": (1,)}[rows_of]:
+        q_ref = (q_own, q_sib)[b]
+        outs = []
+        for g in range(kv_heads):
+            k = jnp.concatenate([t[0, g] for t in tiles], axis=0)
+            v = jnp.concatenate([t[1, g] for t in tiles], axis=0)
+            s = lax.dot_general(q_ref[g], k, (((1,), (1,)), ((), ())), preferred_element_type=jnp.float32)
+            s = s.reshape(BLOCK, group, width) + bias[stage, b, g * group:(g + 1) * group, :][None]
+            if first:
+                offset = key - b * BLOCK
+                causal = jnp.where((offset > pos) & (offset < BLOCK), NEG, 0.0)
+                s = jnp.concatenate([s[:, :, :2 * BLOCK] + causal, s[:, :, 2 * BLOCK:]], axis=2)
+            s = s.reshape(rows, width)
+            top = jnp.broadcast_to(jnp.max(s, axis=1, keepdims=True), (rows, head_width))
+            if not first:
+                old_top = top_in[b, g]
+                top = jnp.maximum(top, old_top)
+                shrink = jnp.exp2((old_top - top) * scale)
+            p = jnp.exp2((s - jnp.concatenate([top] * (width // head_width), axis=1)) * scale)
+            total = jnp.broadcast_to(jnp.sum(p, axis=1, keepdims=True), (rows, head_width))
+            acc = jnp.dot(p.astype(jnp.bfloat16), v, preferred_element_type=jnp.float32)
+            if not first:
+                total = total + sum_in[b, g] * shrink
+                acc = acc + acc_in[b, g] * shrink
+            if not last:
+                acc_out[b, g] = acc
+                top_out[b, g] = top
+                sum_out[b, g] = total
+                continue
+            outs.append((acc / total).reshape(BLOCK, group, head_width))
+            if g % 2:
+                pair = jnp.concatenate(outs, axis=1).astype(jnp.bfloat16)
+                done_ref[:, (g - 1) * group:(g + 1) * group, :] = pair
+                outs = []
+    if last and rows_of == "own":
+        half = kv_heads * group
+        place = pl.ds(pl.multiple_of(core[0] * half, half), half)
+        send = pltpu.make_async_copy(done_ref, out.at[:, place, :], sems[0])
+        send.start()
+        send.wait()
+
+
+def attend_stage(stage, bias, q_own, q_sib, tiles, state, rows_of=None, core=None):
+    kv_heads, rows, head_width = q_own.shape
+    group = rows // BLOCK
+    scale = 1.0 / math.sqrt(head_width) * math.log2(math.e)
+    vm = pl.BlockSpec(memory_space=pltpu.VMEM)
+    args = [bias, q_own, q_sib, *tiles, *state]
+    specs, scratch = [vm] * len(args), []
+    half = (BLOCK, kv_heads * group, head_width)
+    if rows_of is None:
+        out = [jax.ShapeDtypeStruct((2, kv_heads, rows, head_width), jnp.float32)] * 3
+        out_specs = [vm] * 3
+    else:
+        args, specs = args + [core], specs + [pl.BlockSpec(memory_space=pltpu.SMEM)]
+        out, out_specs = jax.ShapeDtypeStruct(half, jnp.bfloat16), vm
+        if rows_of == "own":
+            out = jax.ShapeDtypeStruct((BLOCK, 2 * half[1], head_width), jnp.bfloat16)
+            out_specs = pl.BlockSpec(memory_space=pl.ANY)
+            scratch = [pltpu.VMEM(half, jnp.bfloat16), pltpu.SemaphoreType.DMA]
+    return pl.pallas_call(
+        functools.partial(stage_body, stage, rows_of, len(tiles), group, scale),
+        out_shape=out,
+        in_specs=specs,
+        out_specs=out_specs,
+        scratch_shapes=scratch,
+        compiler_params=pltpu.CompilerParams(vmem_limit_bytes=16 * 1024 * 1024),
+        cost_estimate=pl.CostEstimate(flops=1000, bytes_accessed=1000, transcendentals=0),
+        name="attend",
+    )(*args)
+
+
+def turn_body(core_ref, q_own, q_sib, own_ref, sib_ref):
+    kv_half, rows, width = own_ref.shape
+    group = rows // BLOCK
+    for q_ref, out in ((q_own, own_ref), (q_sib, sib_ref)):
+        for pair in range(kv_half // 2):
+            lo = pl.multiple_of((core_ref[0] * kv_half + pair * 2) * group, 2 * group)
+            both = q_ref[:, pl.ds(lo, 2 * group), :].astype(jnp.float32)
+            for one in range(2):
+                mine = both[:, one * group:(one + 1) * group, :].reshape(rows, width)
+                out[pair * 2 + one] = mine.astype(jnp.bfloat16)
+
+
+def turn_queries(core, own, sib, kv_total):
+    positions, heads, width = own.shape
+    vm = pl.BlockSpec(memory_space=pltpu.VMEM)
+    half = jax.ShapeDtypeStruct((kv_total // 2, positions * heads // kv_total, width), jnp.bfloat16)
+    return pl.pallas_call(
+        turn_body,
+        out_shape=[half, half],
+        in_specs=[pl.BlockSpec(memory_space=pltpu.SMEM), vm, vm],
+        out_specs=[vm, vm],
+        compiler_params=pltpu.CompilerParams(vmem_limit_bytes=8 * 1024 * 1024),
+        cost_estimate=pl.CostEstimate(flops=1000, bytes_accessed=1000, transcendentals=0),
+        name="turn",
+    )(core, own, sib)
+
+
+def split_body(core_ref, k_hbm, v_hbm, keep_ref, give_ref, raw, turned, sems):
+    half = turned.shape[1] // 2
+    fetches = [pltpu.make_async_copy(hbm, raw.at[n], sems.at[n]) for n, hbm in enumerate((k_hbm, v_hbm))]
+    for fetch in fetches:
+        fetch.start()
+    core = core_ref[0]
+    for n, fetch in enumerate(fetches):
+        fetch.wait()
+        turned[n] = jnp.swapaxes(raw[n].astype(jnp.float32), 0, 1).astype(jnp.bfloat16)
+    keep_ref[...] = turned[:, pl.ds(core * half, half)]
+    give_ref[...] = turned[:, pl.ds((1 - core) * half, half)]
+
+
+def split_heads(core, keys, values):
+    rows, kv_total, width = keys.shape
+    vm, hbm = pl.BlockSpec(memory_space=pltpu.VMEM), pl.BlockSpec(memory_space=pltpu.HBM)
+    half = jax.ShapeDtypeStruct((2, kv_total // 2, rows, width), jnp.bfloat16)
+    return pl.pallas_call(
+        split_body,
+        out_shape=[half, half],
+        in_specs=[pl.BlockSpec(memory_space=pltpu.SMEM), hbm, hbm],
+        out_specs=[vm, vm],
+        scratch_shapes=[
+            pltpu.VMEM((2, rows, kv_total, width), jnp.bfloat16),
+            pltpu.VMEM((2, kv_total, rows, width), jnp.bfloat16),
+            pltpu.SemaphoreType.DMA((2,)),
+        ],
+        compiler_params=pltpu.CompilerParams(vmem_limit_bytes=60 * 1024 * 1024),
+        cost_estimate=pl.CostEstimate(flops=1000, bytes_accessed=1000, transcendentals=0),
+        name="split",
+    )(core, keys, values)
+
+
+def join_body(core_ref, other_ref, begun_ref, out_ref, sem):
+    half = other_ref.shape[1]
+    place = pl.ds(pl.multiple_of((1 - core_ref[0]) * half, half), half)
+    send = pltpu.make_async_copy(other_ref, out_ref.at[:, place, :], sem)
+    send.start()
+    send.wait()
+
+
+def join_heads(core, other, begun):
+    somewhere = pl.BlockSpec(memory_space=pl.ANY)
+    return pl.pallas_call(
+        join_body,
+        out_shape=jax.ShapeDtypeStruct(begun.shape, begun.dtype),
+        in_specs=[pl.BlockSpec(memory_space=pltpu.SMEM), pl.BlockSpec(memory_space=pltpu.VMEM), somewhere],
+        out_specs=somewhere,
+        scratch_shapes=[pltpu.SemaphoreType.DMA],
+        input_output_aliases={2: 0},
+        compiler_params=pltpu.CompilerParams(vmem_limit_bytes=8 * 1024 * 1024),
+        cost_estimate=pl.CostEstimate(flops=1000, bytes_accessed=1000, transcendentals=0),
+        name="join",
+    )(core, other, begun)
+
+
+def by_key_block(queries, keys, values, vert_blocks, vert_count, slash_offsets, slash_count):
+    planes = lax.axis_size("seq")
+    plane = lax.axis_index("seq")
+    place = lax.axis_index("blk")
+    core, column = place % 2, place // 2
+
+    def trade(tile, step):
+        return lax.ppermute(tile, "seq", [(i, i ^ step) for i in range(planes)])
+
+    def across(tile):
+        return lax.ppermute(tile, "blk", [(0, 2), (2, 0), (1, 3), (3, 1)])
+
+    def sibling(tile):
+        return lax.ppermute(tile, "blk", [(0, 1), (1, 0), (2, 3), (3, 2)])
+
+    core_id = core[None]
+    sibling_queries = sibling(queries)
+    keep, give = split_heads(core_id, keys, values)
+    slots = jnp.stack([2 * column + core, 2 * column + 1 - core, 2 * (1 - column) + core, 2 * (1 - column) + 1 - core])
+    ids = jnp.concatenate(
+        [jnp.stack([core, plane * 4 + slots[0], plane * 4 + slots[1]])]
+        + [(plane ^ step) * 4 + slots for step in (0, 1, 3, 2)]
+    )
+    a, b = keep, sibling(give)
+    far_a, x_a, near_a = trade(a, 3), across(a), trade(a, 1)
+    b, queries_b = lax.optimization_barrier((b, sibling_queries))
+    far_b = trade(b, 3)
+    q_keep, q_sib = turn_queries(core_id, queries, queries_b, 2 * give.shape[1])
+    lists = jnp.concatenate([vert_blocks.T, vert_count[None], slash_offsets.T, slash_count[None]])
+    bias = pattern_bias(ids, planes, 4, vert_blocks.shape[1], slash_offsets.shape[1], lists)
+    x_b = across(b)
+    late_b, near_a, bias, q_keep, q_sib = lax.optimization_barrier((b, near_a, bias, q_keep, q_sib))
+    near_b = trade(late_b, 1)
+    x_near_a = across(near_a)
+    far_a, q_sib, bias, x_b = lax.optimization_barrier((far_a, q_sib, bias, x_b))
+    last_a = trade(far_a, 1)
+    x_far_a = across(far_a)
+    x_near_b = across(near_b)
+    state = attend_stage(0, bias, q_keep, q_sib, [a, b, x_a, x_b], ())
+    far_b, state = lax.optimization_barrier((far_b, state))
+    last_b = trade(far_b, 1)
+    x_far_b = across(far_b)
+    state = attend_stage(1, bias, q_keep, q_sib, [near_a, near_b, x_near_a, x_near_b], state)
+    go_b, state = lax.optimization_barrier((last_b, state))
+    x_last_a, x_last_b = trade(x_far_a, 1), across(go_b)
+    state = attend_stage(2, bias, q_keep, q_sib, [far_a, far_b, x_far_a, x_far_b], state)
+    tiles = [last_a, last_b, x_last_a, x_last_b]
+    sibling_rows = attend_stage(3, bias, q_keep, q_sib, tiles, state, "sibling", core_id)
+    state, sibling_rows = lax.optimization_barrier((state, sibling_rows))
+    own_rows = attend_stage(3, bias, q_keep, q_sib, tiles, state, "own", core_id)
+    return join_heads(core_id, sibling(sibling_rows), own_rows)
+
+
+def on_device(queries, keys, values, vert_blocks, vert_count, slash_offsets, slash_count):
+    gathered = 2 * keys.size * keys.dtype.itemsize * lax.axis_size("seq") * lax.axis_size("blk")
+    fits = gathered <= GATHER_BYTES and keys.shape[0] == BLOCK and lax.axis_size("blk") == 4
+    plan = by_key_block if fits else by_head_owner
+    return plan(queries, keys, values, vert_blocks, vert_count, slash_offsets, slash_count)
+
+
 def solution(mesh):
     return jax.shard_map(
         on_device,

time: 450 us -> 38.8 us (0.09); the launches traced: 445 us -> 38.5 us
  local copies, waits for them, and re-layouts: 198 us -> 1.3 us
  matrix products: 83.1 us -> 0 us
  other arithmetic: 49.5 us -> 0.85 us
  loops' own time: 47 us -> 0 us
  blocking collectives: 44.8 us -> 0 us
  Pallas kernels: 0 us -> 11.9 us
  starting transfers between devices: 12.3 us -> 18.9 us
  waiting for transfers between devices: 10.6 us -> 5.52 us
    dot_general x64 -> x0, matrix products: 83.1 us -> none  [the longest x16 40 us: sparse_block(): jnp.einsum('gid,gsjd->gisj', query_tiles, slash_keys, preferred_element_t...]
    reshape x36 -> x0, local copies, waits for them, and re-layouts: 72.1 us -> none  [the longest x16 34.8 us: sparse_block(): jnp.where(vert_mask, vert_scores, -jnp.inf)]
    another operation x1 -> x0, loops' own time: 47 us -> none  [on_device(): attended = lax.map(attend, jnp.arange(per_owner * groups, dtype=jnp.int32))]
    dynamic_slice x64 -> x0, local copies, waits for them, and re-layouts: 42.8 us -> none  [the longest x16 13.6 us: attend(): head_queries = lax.dynamic_index_in_dim(query_heads, slot_id, 0, False)]
    gather x64 -> x0, local copies, waits for them, and re-layouts: 42.2 us -> none  [the longest x16 11.6 us: attend(): slash_keys = jnp.take(head_keys, clamped, axis=0)]
    all_to_all x1 -> x0, blocking collectives: 27.3 us -> none  [on_device(): lax.all_to_all(attended, 'seq', split_axis=1, concat_axis=1, tiled=True)]
    ppermute x0 -> x17, starting transfers between devices: none -> 18.9 us  [the longest x7 7.86 us: trade(): return lax.ppermute(tile, 'seq', [(i, i ^ step) for i in range(planes)])]
    all_gather x2 -> x0, blocking collectives: 17.5 us -> none  [the longest x1 10.3 us: on_device(): lax.all_gather(value_part, 'blk', axis=0, tiled=True)]
  transfers between devices with their start and end apart: 3 -> 17, of which waited for: 3 -> 6; matrix products, arithmetic and copies ran while one was open for 1% -> 2% of each run, Pallas kernels for 0% -> 26%
where the time goes in v2:
time: 38.8 us; the launch traced here: 38.5 us
  starting transfers between devices  18.9 us (49%)
  Pallas kernels  11.9 us (31%)
  waiting for transfers between devices  5.52 us (14%)
  local copies, waits for them, and re-layouts  1.3 us (3%)
  other arithmetic  0.85 us (2%)
    pallas_call x5, Pallas kernels, attend_stage(): pl.pallas_call(functools.partial(stage_body, stage, rows_of, len(tiles),...  8.26 us
    ppermute x7, starting transfers between devices, trade(): return lax.ppermute(tile, 'seq', [(i, i ^ step) for i in range(planes)])  7.86 us
    ppermute x7, starting transfers between devices, across(): return lax.ppermute(tile, 'blk', [(0, 2), (2, 0), (1, 3), (3, 1)])  6.72 us
    ppermute x3, starting transfers between devices, sibling(): return lax.ppermute(tile, 'blk', [(0, 1), (1, 0), (2, 3), (3, 2)])  4.29 us
    ppermute x7, waiting for transfers between devices, across(): return lax.ppermute(tile, 'blk', [(0, 2), (2, 0), (1, 3), (3, 1)])  4.17 us
    pallas_call x1, Pallas kernels, split_heads(): pl.pallas_call(split_body, out_shape=[half, half], in_specs=[pl.BlockSpec...  1.74 us
    ppermute x7, waiting for transfers between devices, trade(): return lax.ppermute(tile, 'seq', [(i, i ^ step) for i in range(planes)])  1.34 us
    unnamed x4, local copies, waits for them, and re-layouts  1.23 us
  transfers between devices with their start and end apart: 17, of which 6 were waited for; matrix products, arithmetic and copies ran while one was open for 2% of the time, Pallas kernels for 26%

profile of v2, /device:TPU:1, one launch (start us, length us, event | category | flops | bytes accessed | tf_op | source)
XLA Modules:
  0.0 38.5 jit_solution(5692764630096682931)
XLA Ops:
  0.0 0.1 collective-permute-start.2
  0.1 1.7 %split.1 = (bf16[2,4,64,128]{3,2,1,0:T(8,128)(2,1)}, bf16[2,4,64,128]{3,2,1,0:T(8,128)(2,1)}) custom-call(s32[1]{0:T(128)} %bitcast.core_ref.refs_10_, bf16[64,8,128]{2,1,0:T(8,128)(2,1)} %k_hbm.1, bf16[64,8,128]{2,1,0:T(8,128)(2,1)} %v_hbm.1), custom_call_target="tpu_custom_call" | custom-call | flops 1000 | bytes 1000 | tf_op jit(solution)/shard_map/split/pallas_call | solution.py:360
  1.8 0.0 copy-start.1
  1.8 0.5 %collective-permute-start.1 = (bf16[2,4,64,128]{3,2,1,0:T(8,128)(2,1)}, bf16[2,4,64,128]{3,2,1,0:T(8,128)(2,1)S(1)}, u32[]{:S(2)}, u32[]{:S(2)}) collective-permute-start(bf16[2,4,64,128]{3,2,1,0:T(8,128)(2,1)} %get-tuple-element.42), channel_id=1, source_target_pairs={{0,1},{1,0},{2,3},{3,2},{4,5},{5,4},{6,7},{7,6},{8,9},{9,8},{10,11... | collective-permute-start | bytes 393224 | tf_op jit(solution)/shard_map/ppermute | solution.py:412
  2.3 2.4 %collective-permute-start.3 = (bf16[2,4,64,128]{3,2,1,0:T(8,128)(2,1)}, bf16[2,4,64,128]{3,2,1,0:T(8,128)(2,1)S(1)}, u32[]{:S(2)}, u32[]{:S(2)}) collective-permute-start(bf16[2,4,64,128]{3,2,1,0:T(8,128)(2,1)} %get-tuple-element.41.refs_3_), channel_id=1, source_target_pairs={{0,4},{4,0},{8,12},{12,8},{1,5},{5,1},{9,13},{13,9},{2,6},{6,2},{1... | collective-permute-start | bytes 393224 | tf_op jit(solution)/shard_map/ppermute | solution.py:406
  4.7 0.1 broadcast_add_fusion
  4.8 0.1 concatenate.6.ids
  4.9 0.8 %pad_add_fusion.lists = s32[32,64]{1,0:T(8,128)S(1)} fusion(s32[1,64]{1,0:T(1,128)} %bitcast.13, s32[14,64]{1,0:T(8,128)} %bitcast.11, s32[1,64]{1,0:T(1,128)} %bitcast.14, s32[16,64]{1,0:T(8,128)} %bitcast.12), kind=kLoop, calls=%fused_computation | loop fusion | flops 6144 | bytes 16384 | tf_op jit(solution)/shard_map/concatenate | solution.py:427
  5.6 2.2 %collective-permute-start = (bf16[2,4,64,128]{3,2,1,0:T(8,128)(2,1)}, bf16[2,4,64,128]{3,2,1,0:T(8,128)(2,1)S(1)}, u32[]{:S(2)}, u32[]{:S(2)}) collective-permute-start(bf16[2,4,64,128]{3,2,1,0:T(8,128)(2,1)} %get-tuple-element.41.refs_3_), channel_id=1, source_target_pairs={{0,12},{4,8},{8,4},{12,0},{1,13},{5,9},{9,5},{13,1},{2,14},{6,10},... | collective-permute-start | bytes 393224 | tf_op jit(solution)/shard_map/ppermute | solution.py:406
  7.9 0.9 %pattern.1.refs_0_ = f32[4,2,32,256]{3,2,1,0:T(8,128)S(1)} custom-call(s32[19]{0:T(128)S(1)} %concatenate.6.ids, s32[32,64]{1,0:T(8,128)S(1)} %pad_add_fusion.lists), custom_call_target="tpu_custom_call" | custom-call | flops 1000 | bytes 1000 | tf_op jit(solution)/shard_map/pattern/pallas_call | solution.py:214
  8.8 0.0 collective-permute-done.1.refs_4_
  8.8 0.0 collective-permute-done.2.q_sib
  8.8 0.0 copy-start
  8.8 1.2 %copy-done = bf16[64,64,128]{2,1,0:T(8,128)(2,1)S(1)} copy-done((bf16[64,64,128]{2,1,0:T(8,128)(2,1)S(1)}, bf16[64,64,128]{2,1,0:T(8,128)(2,1)}, u32[]{:S(2)}) %copy-start) | copy-done | bytes 1048600
  10.0 0.2 turn.1
  10.2 1.3 %collective-permute-start.4 = (bf16[2,4,64,128]{3,2,1,0:T(8,128)(2,1)S(1)}, bf16[2,4,64,128]{3,2,1,0:T(8,128)(2,1)S(1)}, u32[]{:S(2)}, u32[]{:S(2)}) collective-permute-start(bf16[2,4,64,128]{3,2,1,0:T(8,128)(2,1)S(1)} %collective-permute-done.1.refs_4_), channel_id=1, source_target_pairs={{0,2},{2,0},{1,3},{3,1},{4,6},{6,4},{5,7},{7,5},{8,10},{10,8},{9,1... | collective-permute-start | bytes 393224 | tf_op jit(solution)/shard_map/ppermute | solution.py:409
  11.5 0.0 collective-permute-done.3.refs_3_
  11.5 0.4 %collective-permute-start.10 = (bf16[2,4,64,128]{3,2,1,0:T(8,128)(2,1)S(1)}, bf16[2,4,64,128]{3,2,1,0:T(8,128)(2,1)S(1)}, u32[]{:S(2)}, u32[]{:S(2)}) collective-permute-start(bf16[2,4,64,128]{3,2,1,0:T(8,128)(2,1)S(1)} %collective-permute-done.1.refs_4_), channel_id=1, source_target_pairs={{0,4},{4,0},{8,12},{12,8},{1,5},{5,1},{9,13},{13,9},{2,6},{6,2},{1... | collective-permute-start | bytes 393224 | tf_op jit(solution)/shard_map/ppermute | solution.py:406
  11.9 0.0 copy-done.1
  11.9 0.3 collective-permute-start.6
  12.1 0.9 %collective-permute-start.5 = (bf16[2,4,64,128]{3,2,1,0:T(8,128)(2,1)S(1)}, bf16[2,4,64,128]{3,2,1,0:T(8,128)(2,1)S(1)}, u32[]{:S(2)}, u32[]{:S(2)}) collective-permute-start(bf16[2,4,64,128]{3,2,1,0:T(8,128)(2,1)S(1)} %collective-permute-done.1.refs_4_), channel_id=1, source_target_pairs={{0,12},{4,8},{8,4},{12,0},{1,13},{5,9},{9,5},{13,1},{2,14},{6,10},... | collective-permute-start | bytes 393224 | tf_op jit(solution)/shard_map/ppermute | solution.py:406
  13.0 0.2 collective-permute-done.refs_3_
  13.3 1.2 %collective-permute-start.11 = (bf16[2,4,64,128]{3,2,1,0:T(8,128)(2,1)S(1)}, bf16[2,4,64,128]{3,2,1,0:T(8,128)(2,1)S(1)}, u32[]{:S(2)}, u32[]{:S(2)}) collective-permute-start(bf16[2,4,64,128]{3,2,1,0:T(8,128)(2,1)S(1)} %collective-permute-done.3.refs_3_), channel_id=1, source_target_pairs={{0,2},{2,0},{1,3},{3,1},{4,6},{6,4},{5,7},{7,5},{8,10},{10,8},{9,1... | collective-permute-start | bytes 393224 | tf_op jit(solution)/shard_map/ppermute | solution.py:409
  14.5 0.0 collective-permute-done.4.refs_6_
  14.5 1.1 %collective-permute-done.10.refs_4_ = bf16[2,4,64,128]{3,2,1,0:T(8,128)(2,1)S(1)} collective-permute-done((bf16[2,4,64,128]{3,2,1,0:T(8,128)(2,1)S(1)}, bf16[2,4,64,128]{3,2,1,0:T(8,128)(2,1)S(1)}, u32[]{:S(2)}, u32[]{:S(2)}) %collective-permute-start.10) | collective-permute-done | bytes 131104 | tf_op jit(solution)/shard_map/ppermute | solution.py:406
  15.6 1.6 %collective-permute-start.12 = (bf16[2,4,64,128]{3,2,1,0:T(8,128)(2,1)S(1)}, bf16[2,4,64,128]{3,2,1,0:T(8,128)(2,1)S(1)}, u32[]{:S(2)}, u32[]{:S(2)}) collective-permute-start(bf16[2,4,64,128]{3,2,1,0:T(8,128)(2,1)S(1)} %collective-permute-done.10.refs_4_), channel_id=1, source_target_pairs={{0,2},{2,0},{1,3},{3,1},{4,6},{6,4},{5,7},{7,5},{8,10},{10,8},{9,1... | collective-permute-start | bytes 393224 | tf_op jit(solution)/shard_map/ppermute | solution.py:409
  17.1 0.2 collective-permute-done.6.refs_5_
  17.4 1.5 %attend.5 = (f32[2,4,512,128]{3,2,1,0:T(8,128)S(1)}, f32[2,4,512,128]{3,2,1,0:T(8,128)S(1)}, f32[2,4,512,128]{3,2,1,0:T(8,128)S(1)}) custom-call(f32[4,2,32,256]{3,2,1,0:T(8,128)S(1)} %pattern.1.refs_0_, bf16[4,512,128]{2,1,0:T(8,128)(2,1)S(1)} %get-tuple-element.50.refs_1_, bf16[4,512,128]{2,1,0:T(8,128)(2,1)S(1)} %get-tuple-element.51.refs_2_, ...), custom_call_target="tpu_custom_call" | custom-call | flops 1000 | bytes 1000 | tf_op jit(solution)/shard_map/attend/pallas_call | solution.py:304
  18.9 0.0 collective-permute-done.5.refs_4_
  18.9 0.3 collective-permute-start.9
  19.2 1.2 %collective-permute-start.7 = (bf16[2,4,64,128]{3,2,1,0:T(8,128)(2,1)S(1)}, bf16[2,4,64,128]{3,2,1,0:T(8,128)(2,1)S(1)}, u32[]{:S(2)}, u32[]{:S(2)}) collective-permute-start(bf16[2,4,64,128]{3,2,1,0:T(8,128)(2,1)S(1)} %collective-permute-done.refs_3_), channel_id=1, source_target_pairs={{0,2},{2,0},{1,3},{3,1},{4,6},{6,4},{5,7},{7,5},{8,10},{10,8},{9,1... | collective-permute-start | bytes 393224 | tf_op jit(solution)/shard_map/ppermute | solution.py:409
  20.4 0.2 collective-permute-start.8
  20.7 0.0 collective-permute-done.11.refs_5_
  20.7 1.2 %collective-permute-start.13 = (bf16[2,4,64,128]{3,2,1,0:T(8,128)(2,1)S(1)}, bf16[2,4,64,128]{3,2,1,0:T(8,128)(2,1)S(1)}, u32[]{:S(2)}, u32[]{:S(2)}) collective-permute-start(bf16[2,4,64,128]{3,2,1,0:T(8,128)(2,1)S(1)} %collective-permute-done.refs_3_), channel_id=1, source_target_pairs={{0,4},{4,0},{8,12},{12,8},{1,5},{5,1},{9,13},{13,9},{2,6},{6,2},{1... | collective-permute-start | bytes 393224 | tf_op jit(solution)/shard_map/ppermute | solution.py:406
  21.9 1.1 %collective-permute-done.12.refs_6_ = bf16[2,4,64,128]{3,2,1,0:T(8,128)(2,1)S(1)} collective-permute-done((bf16[2,4,64,128]{3,2,1,0:T(8,128)(2,1)S(1)}, bf16[2,4,64,128]{3,2,1,0:T(8,128)(2,1)S(1)}, u32[]{:S(2)}, u32[]{:S(2)}) %collective-permute-start.12) | collective-permute-done | bytes 131104 | tf_op jit(solution)/shard_map/ppermute | solution.py:409
  23.0 1.8 %attend.6 = (f32[2,4,512,128]{3,2,1,0:T(8,128)S(1)}, f32[2,4,512,128]{3,2,1,0:T(8,128)S(1)}, f32[2,4,512,128]{3,2,1,0:T(8,128)S(1)}) custom-call(f32[4,2,32,256]{3,2,1,0:T(8,128)S(1)} %pattern.1.refs_0_, bf16[4,512,128]{2,1,0:T(8,128)(2,1)S(1)} %get-tuple-element.50.refs_1_, bf16[4,512,128]{2,1,0:T(8,128)(2,1)S(1)} %get-tuple-element.51.refs_2_, ...), custom_call_target="tpu_custom_call" | custom-call | flops 1000 | bytes 1000 | tf_op jit(solution)/shard_map/attend/pallas_call | solution.py:304
  24.9 0.0 collective-permute-done.9.refs_4_
  24.9 1.0 %collective-permute-start.15 = (bf16[2,4,64,128]{3,2,1,0:T(8,128)(2,1)S(1)}, bf16[2,4,64,128]{3,2,1,0:T(8,128)(2,1)S(1)}, u32[]{:S(2)}, u32[]{:S(2)}) collective-permute-start(bf16[2,4,64,128]{3,2,1,0:T(8,128)(2,1)S(1)} %collective-permute-done.9.refs_4_), channel_id=1, source_target_pairs={{0,2},{2,0},{1,3},{3,1},{4,6},{6,4},{5,7},{7,5},{8,10},{10,8},{9,1... | collective-permute-start | bytes 393224 | tf_op jit(solution)/shard_map/ppermute | solution.py:409
  25.8 0.0 collective-permute-done.7.refs_5_
  25.8 0.4 %collective-permute-start.14 = (bf16[2,4,64,128]{3,2,1,0:T(8,128)(2,1)S(1)}, bf16[2,4,64,128]{3,2,1,0:T(8,128)(2,1)S(1)}, u32[]{:S(2)}, u32[]{:S(2)}) collective-permute-start(bf16[2,4,64,128]{3,2,1,0:T(8,128)(2,1)S(1)} %collective-permute-done.7.refs_5_), channel_id=1, source_target_pairs={{0,4},{4,0},{8,12},{12,8},{1,5},{5,1},{9,13},{13,9},{2,6},{6,2},{1... | collective-permute-start | bytes 393224 | tf_op jit(solution)/shard_map/ppermute | solution.py:406
  26.2 1.9 %collective-permute-done.8.refs_6_ = bf16[2,4,64,128]{3,2,1,0:T(8,128)(2,1)S(1)} collective-permute-done((bf16[2,4,64,128]{3,2,1,0:T(8,128)(2,1)S(1)}, bf16[2,4,64,128]{3,2,1,0:T(8,128)(2,1)S(1)}, u32[]{:S(2)}, u32[]{:S(2)}) %collective-permute-start.8) | collective-permute-done | bytes 131104 | tf_op jit(solution)/shard_map/ppermute | solution.py:409
  28.1 1.8 %attend.7 = (f32[2,4,512,128]{3,2,1,0:T(8,128)S(1)}, f32[2,4,512,128]{3,2,1,0:T(8,128)S(1)}, f32[2,4,512,128]{3,2,1,0:T(8,128)S(1)}) custom-call(f32[4,2,32,256]{3,2,1,0:T(8,128)S(1)} %pattern.1.refs_0_, bf16[4,512,128]{2,1,0:T(8,128)(2,1)S(1)} %get-tuple-element.50.refs_1_, bf16[4,512,128]{2,1,0:T(8,128)(2,1)S(1)} %get-tuple-element.51.refs_2_, ...), custom_call_target="tpu_custom_call" | custom-call | flops 1000 | bytes 1000 | tf_op jit(solution)/shard_map/attend/pallas_call | solution.py:304
  29.9 0.0 collective-permute-done.13.refs_3_
  29.9 1.0 %collective-permute-done.15.refs_6_ = bf16[2,4,64,128]{3,2,1,0:T(8,128)(2,1)S(1)} collective-permute-done((bf16[2,4,64,128]{3,2,1,0:T(8,128)(2,1)S(1)}, bf16[2,4,64,128]{3,2,1,0:T(8,128)(2,1)S(1)}, u32[]{:S(2)}, u32[]{:S(2)}) %collective-permute-start.15) | collective-permute-done | bytes 131104 | tf_op jit(solution)/shard_map/ppermute | solution.py:409
  30.9 0.0 collective-permute-done.14.refs_5_
  30.9 1.2 %attend.8 = bf16[64,32,128]{2,1,0:T(8,128)(2,1)S(1)} custom-call(f32[4,2,32,256]{3,2,1,0:T(8,128)S(1)} %pattern.1.refs_0_, bf16[4,512,128]{2,1,0:T(8,128)(2,1)S(1)} %get-tuple-element.50.refs_1_, bf16[4,512,128]{2,1,0:T(8,128)(2,1)S(1)} %get-tuple-element.51.refs_2_, bf16[2,4,64,128]{3,2,1,0:T(8,128)(2,1)S(1)} %collective-permute-done.13.refs_3_, ...), custom_call_target="tpu_custom_call" | custom-call | flops 1000 | bytes 1000 | tf_op jit(solution)/shard_map/attend/pallas_call | solution.py:304
  32.0 3.7 %collective-permute-start.16 = (bf16[64,32,128]{2,1,0:T(8,128)(2,1)S(1)}, bf16[64,32,128]{2,1,0:T(8,128)(2,1)S(1)}, u32[]{:S(2)}, u32[]{:S(2)}) collective-permute-start(bf16[64,32,128]{2,1,0:T(8,128)(2,1)S(1)} %attend.8), channel_id=1, source_target_pairs={{0,1},{1,0},{2,3},{3,2},{4,5},{5,4},{6,7},{7,6},{8,9},{9,8},{10,11... | collective-permute-start | bytes 1572872 | tf_op jit(solution)/shard_map/ppermute | solution.py:412
  35.8 2.0 %attend.9.begun_ref = bf16[64,64,128]{2,1,0:T(8,128)(2,1)} custom-call(f32[4,2,32,256]{3,2,1,0:T(8,128)S(1)} %pattern.1.refs_0_, bf16[4,512,128]{2,1,0:T(8,128)(2,1)S(1)} %get-tuple-element.50.refs_1_, bf16[4,512,128]{2,1,0:T(8,128)(2,1)S(1)} %get-tuple-element.51.refs_2_, bf16[2,4,64,128]{3,2,1,0:T(8,128)(2,1)S(1)} %collective-permute-done.13.refs_3_, ...), custom_call_target="tpu_custom_call" | custom-call | flops 1000 | bytes 1000 | tf_op jit(solution)/shard_map/attend/pallas_call | solution.py:304
  37.7 0.0 collective-permute-done.16.other_ref
  37.7 0.8 %join.1 = bf16[64,64,128]{2,1,0:T(8,128)(2,1)} custom-call(s32[1]{0:T(128)} %bitcast.core_ref.refs_10_, bf16[64,32,128]{2,1,0:T(8,128)(2,1)S(1)} %collective-permute-done.16.other_ref, bf16[64,64,128]{2,1,0:T(8,128)(2,1)} %attend.9.begun_ref), custom_call_target="tpu_custom_call", output_to_operand_aliasing={{}: (2, {})} | custom-call | flops 1000 | bytes 1000 | tf_op jit(solution)/shard_map/join/pallas_call | solution.py:386
  (1 shorter events, 0.0 us)
Async XLA Ops:
  0.0 8.8 %collective-permute-start.2 = (bf16[64,64,128]{2,1,0:T(8,128)(2,1)}, bf16[64,64,128]{2,1,0:T(8,128)(2,1)S(1)}, u32[]{:S(2)}, u32[]{:S(2)}) collective-permute-start(bf16[64,64,128]{2,1,0:T(8,128)(2,1)} %q_own.1), channel_id=1, source_target_pairs={{0,1},{1,0},{2,3},{3,2},{4,5},{5,4},{6,7},{7,6},{8,9},{9,8},{10,11... | collective-permute-start | bytes 3145736 | tf_op jit(solution)/shard_map/ppermute | solution.py:412
  1.8 10.1 %copy-start.1 = (bf16[2,4,64,128]{3,2,1,0:T(8,128)(2,1)S(1)}, bf16[2,4,64,128]{3,2,1,0:T(8,128)(2,1)}, u32[]{:S(2)}) copy-start(bf16[2,4,64,128]{3,2,1,0:T(8,128)(2,1)} %get-tuple-element.41.refs_3_) | copy-start | bytes 393220
  1.8 6.9 %collective-permute-start.1 = (bf16[2,4,64,128]{3,2,1,0:T(8,128)(2,1)}, bf16[2,4,64,128]{3,2,1,0:T(8,128)(2,1)S(1)}, u32[]{:S(2)}, u32[]{:S(2)}) collective-permute-start(bf16[2,4,64,128]{3,2,1,0:T(8,128)(2,1)} %get-tuple-element.42), channel_id=1, source_target_pairs={{0,1},{1,0},{2,3},{3,2},{4,5},{5,4},{6,7},{7,6},{8,9},{9,8},{10,11... | collective-permute-start | bytes 393224 | tf_op jit(solution)/shard_map/ppermute | solution.py:412
  2.3 9.1 %collective-permute-start.3 = (bf16[2,4,64,128]{3,2,1,0:T(8,128)(2,1)}, bf16[2,4,64,128]{3,2,1,0:T(8,128)(2,1)S(1)}, u32[]{:S(2)}, u32[]{:S(2)}) collective-permute-start(bf16[2,4,64,128]{3,2,1,0:T(8,128)(2,1)} %get-tuple-element.41.refs_3_), channel_id=1, source_target_pairs={{0,4},{4,0},{8,12},{12,8},{1,5},{5,1},{9,13},{13,9},{2,6},{6,2},{1... | collective-permute-start | bytes 393224 | tf_op jit(solution)/shard_map/ppermute | solution.py:406
  5.6 7.6 %collective-permute-start = (bf16[2,4,64,128]{3,2,1,0:T(8,128)(2,1)}, bf16[2,4,64,128]{3,2,1,0:T(8,128)(2,1)S(1)}, u32[]{:S(2)}, u32[]{:S(2)}) collective-permute-start(bf16[2,4,64,128]{3,2,1,0:T(8,128)(2,1)} %get-tuple-element.41.refs_3_), channel_id=1, source_target_pairs={{0,12},{4,8},{8,4},{12,0},{1,13},{5,9},{9,5},{13,1},{2,14},{6,10},... | collective-permute-start | bytes 393224 | tf_op jit(solution)/shard_map/ppermute | solution.py:406
  8.8 1.2 %copy-start = (bf16[64,64,128]{2,1,0:T(8,128)(2,1)S(1)}, bf16[64,64,128]{2,1,0:T(8,128)(2,1)}, u32[]{:S(2)}) copy-start(bf16[64,64,128]{2,1,0:T(8,128)(2,1)} %q_own.1) | copy-start | bytes 3145732
  10.2 4.3 %collective-permute-start.4 = (bf16[2,4,64,128]{3,2,1,0:T(8,128)(2,1)S(1)}, bf16[2,4,64,128]{3,2,1,0:T(8,128)(2,1)S(1)}, u32[]{:S(2)}, u32[]{:S(2)}) collective-permute-start(bf16[2,4,64,128]{3,2,1,0:T(8,128)(2,1)S(1)} %collective-permute-done.1.refs_4_), channel_id=1, source_target_pairs={{0,2},{2,0},{1,3},{3,1},{4,6},{6,4},{5,7},{7,5},{8,10},{10,8},{9,1... | collective-permute-start | bytes 393224 | tf_op jit(solution)/shard_map/ppermute | solution.py:409
  11.5 4.1 %collective-permute-start.10 = (bf16[2,4,64,128]{3,2,1,0:T(8,128)(2,1)S(1)}, bf16[2,4,64,128]{3,2,1,0:T(8,128)(2,1)S(1)}, u32[]{:S(2)}, u32[]{:S(2)}) collective-permute-start(bf16[2,4,64,128]{3,2,1,0:T(8,128)(2,1)S(1)} %collective-permute-done.1.refs_4_), channel_id=1, source_target_pairs={{0,4},{4,0},{8,12},{12,8},{1,5},{5,1},{9,13},{13,9},{2,6},{6,2},{1... | collective-permute-start | bytes 393224 | tf_op jit(solution)/shard_map/ppermute | solution.py:406
  11.9 5.5 %collective-permute-start.6 = (bf16[2,4,64,128]{3,2,1,0:T(8,128)(2,1)S(1)}, bf16[2,4,64,128]{3,2,1,0:T(8,128)(2,1)S(1)}, u32[]{:S(2)}, u32[]{:S(2)}) collective-permute-start(bf16[2,4,64,128]{3,2,1,0:T(8,128)(2,1)S(1)} %copy-done.1), channel_id=1, source_target_pairs={{0,2},{2,0},{1,3},{3,1},{4,6},{6,4},{5,7},{7,5},{8,10},{10,8},{9,1... | collective-permute-start | bytes 393224 | tf_op jit(solution)/shard_map/ppermute | solution.py:409
  12.1 6.8 %collective-permute-start.5 = (bf16[2,4,64,128]{3,2,1,0:T(8,128)(2,1)S(1)}, bf16[2,4,64,128]{3,2,1,0:T(8,128)(2,1)S(1)}, u32[]{:S(2)}, u32[]{:S(2)}) collective-permute-start(bf16[2,4,64,128]{3,2,1,0:T(8,128)(2,1)S(1)} %collective-permute-done.1.refs_4_), channel_id=1, source_target_pairs={{0,12},{4,8},{8,4},{12,0},{1,13},{5,9},{9,5},{13,1},{2,14},{6,10},... | collective-permute-start | bytes 393224 | tf_op jit(solution)/shard_map/ppermute | solution.py:406
  13.3 7.4 %collective-permute-start.11 = (bf16[2,4,64,128]{3,2,1,0:T(8,128)(2,1)S(1)}, bf16[2,4,64,128]{3,2,1,0:T(8,128)(2,1)S(1)}, u32[]{:S(2)}, u32[]{:S(2)}) collective-permute-start(bf16[2,4,64,128]{3,2,1,0:T(8,128)(2,1)S(1)} %collective-permute-done.3.refs_3_), channel_id=1, source_target_pairs={{0,2},{2,0},{1,3},{3,1},{4,6},{6,4},{5,7},{7,5},{8,10},{10,8},{9,1... | collective-permute-start | bytes 393224 | tf_op jit(solution)/shard_map/ppermute | solution.py:409
  15.6 7.4 %collective-permute-start.12 = (bf16[2,4,64,128]{3,2,1,0:T(8,128)(2,1)S(1)}, bf16[2,4,64,128]{3,2,1,0:T(8,128)(2,1)S(1)}, u32[]{:S(2)}, u32[]{:S(2)}) collective-permute-start(bf16[2,4,64,128]{3,2,1,0:T(8,128)(2,1)S(1)} %collective-permute-done.10.refs_4_), channel_id=1, source_target_pairs={{0,2},{2,0},{1,3},{3,1},{4,6},{6,4},{5,7},{7,5},{8,10},{10,8},{9,1... | collective-permute-start | bytes 393224 | tf_op jit(solution)/shard_map/ppermute | solution.py:409
  18.9 5.9 %collective-permute-start.9 = (bf16[2,4,64,128]{3,2,1,0:T(8,128)(2,1)S(1)}, bf16[2,4,64,128]{3,2,1,0:T(8,128)(2,1)S(1)}, u32[]{:S(2)}, u32[]{:S(2)}) collective-permute-start(bf16[2,4,64,128]{3,2,1,0:T(8,128)(2,1)S(1)} %collective-permute-done.5.refs_4_), channel_id=1, source_target_pairs={{0,4},{4,0},{8,12},{12,8},{1,5},{5,1},{9,13},{13,9},{2,6},{6,2},{1... | collective-permute-start | bytes 393224 | tf_op jit(solution)/shard_map/ppermute | solution.py:406
  19.2 6.6 %collective-permute-start.7 = (bf16[2,4,64,128]{3,2,1,0:T(8,128)(2,1)S(1)}, bf16[2,4,64,128]{3,2,1,0:T(8,128)(2,1)S(1)}, u32[]{:S(2)}, u32[]{:S(2)}) collective-permute-start(bf16[2,4,64,128]{3,2,1,0:T(8,128)(2,1)S(1)} %collective-permute-done.refs_3_), channel_id=1, source_target_pairs={{0,2},{2,0},{1,3},{3,1},{4,6},{6,4},{5,7},{7,5},{8,10},{10,8},{9,1... | collective-permute-start | bytes 393224 | tf_op jit(solution)/shard_map/ppermute | solution.py:409
  20.4 7.6 %collective-permute-start.8 = (bf16[2,4,64,128]{3,2,1,0:T(8,128)(2,1)S(1)}, bf16[2,4,64,128]{3,2,1,0:T(8,128)(2,1)S(1)}, u32[]{:S(2)}, u32[]{:S(2)}) collective-permute-start(bf16[2,4,64,128]{3,2,1,0:T(8,128)(2,1)S(1)} %collective-permute-done.5.refs_4_), channel_id=1, source_target_pairs={{0,2},{2,0},{1,3},{3,1},{4,6},{6,4},{5,7},{7,5},{8,10},{10,8},{9,1... | collective-permute-start | bytes 393224 | tf_op jit(solution)/shard_map/ppermute | solution.py:409
  20.7 9.2 %collective-permute-start.13 = (bf16[2,4,64,128]{3,2,1,0:T(8,128)(2,1)S(1)}, bf16[2,4,64,128]{3,2,1,0:T(8,128)(2,1)S(1)}, u32[]{:S(2)}, u32[]{:S(2)}) collective-permute-start(bf16[2,4,64,128]{3,2,1,0:T(8,128)(2,1)S(1)} %collective-permute-done.refs_3_), channel_id=1, source_target_pairs={{0,4},{4,0},{8,12},{12,8},{1,5},{5,1},{9,13},{13,9},{2,6},{6,2},{1... | collective-permute-start | bytes 393224 | tf_op jit(solution)/shard_map/ppermute | solution.py:406
  24.9 6.0 %collective-permute-start.15 = (bf16[2,4,64,128]{3,2,1,0:T(8,128)(2,1)S(1)}, bf16[2,4,64,128]{3,2,1,0:T(8,128)(2,1)S(1)}, u32[]{:S(2)}, u32[]{:S(2)}) collective-permute-start(bf16[2,4,64,128]{3,2,1,0:T(8,128)(2,1)S(1)} %collective-permute-done.9.refs_4_), channel_id=1, source_target_pairs={{0,2},{2,0},{1,3},{3,1},{4,6},{6,4},{5,7},{7,5},{8,10},{10,8},{9,1... | collective-permute-start | bytes 393224 | tf_op jit(solution)/shard_map/ppermute | solution.py:409
  25.8 5.1 %collective-permute-start.14 = (bf16[2,4,64,128]{3,2,1,0:T(8,128)(2,1)S(1)}, bf16[2,4,64,128]{3,2,1,0:T(8,128)(2,1)S(1)}, u32[]{:S(2)}, u32[]{:S(2)}) collective-permute-start(bf16[2,4,64,128]{3,2,1,0:T(8,128)(2,1)S(1)} %collective-permute-done.7.refs_5_), channel_id=1, source_target_pairs={{0,4},{4,0},{8,12},{12,8},{1,5},{5,1},{9,13},{13,9},{2,6},{6,2},{1... | collective-permute-start | bytes 393224 | tf_op jit(solution)/shard_map/ppermute | solution.py:406
  32.0 5.7 %collective-permute-start.16 = (bf16[64,32,128]{2,1,0:T(8,128)(2,1)S(1)}, bf16[64,32,128]{2,1,0:T(8,128)(2,1)S(1)}, u32[]{:S(2)}, u32[]{:S(2)}) collective-permute-start(bf16[64,32,128]{2,1,0:T(8,128)(2,1)S(1)} %attend.8), channel_id=1, source_target_pairs={{0,1},{1,0},{2,3},{3,2},{4,5},{5,4},{6,7},{7,6},{8,9},{9,8},{10,11... | collective-permute-start | bytes 1572872 | tf_op jit(solution)/shard_map/ppermute | solution.py:412

commit v3 on v2

--- a/solution.py
+++ b/solution.py
@@ -179,55 +179,49 @@
     hit = (entries == wanted) & (row < live_count)
     return jnp.sum(jnp.where(hit, 1.0, 0.0), axis=0, keepdims=True)
 
-def pattern_body(stages, vert_rows, slash_rows, ids, lists, out_ref, taken_ref):
+def pattern_body(vert_rows, slash_rows, ids, lists, out_ref, taken_ref):
     vert, vcount = lists[:vert_rows], lists[vert_rows:vert_rows + 1]
     slash, scount = lists[vert_rows + 1:vert_rows + 1 + slash_rows], lists[vert_rows + 1 + slash_rows:]
-    half = out_ref.shape[2]
-    slots = out_ref.shape[3] // BLOCK
+    half, width = out_ref.shape[1:]
+    slots = width // BLOCK
     lo = pl.multiple_of(ids[0] * half, half)
     spread = (
-        lax.broadcasted_iota(jnp.int32, (8, slots * BLOCK), 0)
-        == lax.broadcasted_iota(jnp.int32, (8, slots * BLOCK), 1) // BLOCK
+        lax.broadcasted_iota(jnp.int32, (slots, width), 0) == lax.broadcasted_iota(jnp.int32, (slots, width), 1) // BLOCK
     )
     spread = jnp.where(spread, 1.0, 0.0)
-    pad = jnp.zeros((8 - slots, lists.shape[1]), jnp.float32)
-    for stage in range(stages):
-        for b in range(2):
-            rows = []
-            for slot in range(slots):
-                key_block, query_block = ids[3 + stage * slots + slot], ids[1 + b]
-                n = listed(vert, vcount, key_block) + listed(slash, scount, query_block - key_block)
-                rows.append(n * jnp.where((key_block >= 0) & (key_block <= query_block), 1.0, 0.0))
-            taken = lax.dot_general(
-                jnp.concatenate(rows + [pad], axis=0),
-                spread,
-                (((0,), (0,)), ((), ())),
-                preferred_element_type=jnp.float32,
-            )
-            taken_ref[...] = jnp.where(taken > 0.5, 0.0, NEG)
-            out_ref[stage, b] = taken_ref[pl.ds(lo, half), :]
-
-
-def pattern_bias(ids, stages, slots, vert_rows, slash_rows, lists):
+    for b in range(2):
+        rows = []
+        for slot in range(slots):
+            key_block, query_block = ids[3 + slot], ids[1 + b]
+            n = listed(vert, vcount, key_block) + listed(slash, scount, query_block - key_block)
+            rows.append(n * jnp.where((key_block >= 0) & (key_block <= query_block), 1.0, 0.0))
+        taken_ref[...] = lax.dot_general(
+            jnp.concatenate(rows, axis=0), spread, (((0,), (0,)), ((), ())), preferred_element_type=jnp.float32
+        )
+        out_ref[b] = jnp.where(taken_ref[pl.ds(lo, half), :] > 0.5, 0.0, NEG)
+
+
+def pattern_bias(ids, slots, vert_rows, slash_rows, lists):
     heads = lists.shape[1]
     vm = pl.BlockSpec(memory_space=pltpu.VMEM)
     return pl.pallas_call(
-        functools.partial(pattern_body, stages, vert_rows, slash_rows),
-        out_shape=jax.ShapeDtypeStruct((stages, 2, heads // 2, slots * BLOCK), jnp.float32),
+        functools.partial(pattern_body, vert_rows, slash_rows),
+        out_shape=jax.ShapeDtypeStruct((2, heads // 2, slots * BLOCK), jnp.float32),
         in_specs=[pl.BlockSpec(memory_space=pltpu.SMEM), vm],
         out_specs=vm,
         scratch_shapes=[pltpu.VMEM((heads, slots * BLOCK), jnp.float32)],
         compiler_params=pltpu.CompilerParams(vmem_limit_bytes=8 * 1024 * 1024),
-        cost_estimate=pl.CostEstimate(flops=1000, bytes_accessed=1000, transcendentals=0),
+        cost_estimate=pl.CostEstimate(flops=0, bytes_accessed=16 << 20, transcendentals=0),
         name="pattern",
     )(ids, lists)
 
 
-def stage_body(stage, rows_of, slots, group, scale, *refs):
+def stage_body(first_slot, rows_of, slots, group, scale, *refs):
     last = rows_of is not None
     (bias, q_own, q_sib), refs = refs[:3], refs[3:]
     tiles, refs = refs[:slots], refs[slots:]
-    first = stage == 0
+    first = first_slot == 0
+    keys = slice(first_slot * BLOCK, (first_slot + slots) * BLOCK)
     if not first:
         acc_in, top_in, sum_in = refs[:3]
         refs = refs[3:]
@@ -248,7 +242,7 @@
             k = jnp.concatenate([t[0, g] for t in tiles], axis=0)
             v = jnp.concatenate([t[1, g] for t in tiles], axis=0)
             s = lax.dot_general(q_ref[g], k, (((1,), (1,)), ((), ())), preferred_element_type=jnp.float32)
-            s = s.reshape(BLOCK, group, width) + bias[stage, b, g * group:(g + 1) * group, :][None]
+            s = s.reshape(BLOCK, group, width) + bias[b, g * group:(g + 1) * group, keys][None]
             if first:
                 offset = key - b * BLOCK
                 causal = jnp.where((offset > pos) & (offset < BLOCK), NEG, 0.0)
@@ -283,7 +277,7 @@
         send.wait()
 
 
-def attend_stage(stage, bias, q_own, q_sib, tiles, state, rows_of=None, core=None):
+def attend_stage(first_slot, bias, q_own, q_sib, tiles, state, rows_of=None, core=None):
     kv_heads, rows, head_width = q_own.shape
     group = rows // BLOCK
     scale = 1.0 / math.sqrt(head_width) * math.log2(math.e)
@@ -302,7 +296,7 @@
             out_specs = pl.BlockSpec(memory_space=pl.ANY)
             scratch = [pltpu.VMEM(half, jnp.bfloat16), pltpu.SemaphoreType.DMA]
     return pl.pallas_call(
-        functools.partial(stage_body, stage, rows_of, len(tiles), group, scale),
+        functools.partial(stage_body, first_slot, rows_of, len(tiles), group, scale),
         out_shape=out,
         in_specs=specs,
         out_specs=out_specs,
@@ -335,7 +329,7 @@
         in_specs=[pl.BlockSpec(memory_space=pltpu.SMEM), vm, vm],
         out_specs=[vm, vm],
         compiler_params=pltpu.CompilerParams(vmem_limit_bytes=8 * 1024 * 1024),
-        cost_estimate=pl.CostEstimate(flops=1000, bytes_accessed=1000, transcendentals=0),
+        cost_estimate=pl.CostEstimate(flops=0, bytes_accessed=16 << 20, transcendentals=0),
         name="turn",
     )(core, own, sib)
 
@@ -420,38 +414,38 @@
         + [(plane ^ step) * 4 + slots for step in (0, 1, 3, 2)]
     )
     a, b = keep, sibling(give)
-    far_a, x_a, near_a = trade(a, 3), across(a), trade(a, 1)
-    b, queries_b = lax.optimization_barrier((b, sibling_queries))
-    far_b = trade(b, 3)
-    q_keep, q_sib = turn_queries(core_id, queries, queries_b, 2 * give.shape[1])
-    lists = jnp.concatenate([vert_blocks.T, vert_count[None], slash_offsets.T, slash_count[None]])
-    bias = pattern_bias(ids, planes, 4, vert_blocks.shape[1], slash_offsets.shape[1], lists)
-    x_b = across(b)
+    far_a, near_a = trade(a, 3), trade(a, 1)
+    late_a, b, sibling_queries = lax.optimization_barrier((a, b, sibling_queries))
+    far_b, x_a, x_b = trade(b, 3), across(late_a), across(b)
+    vert_lists = vert_blocks
+    q_keep, q_sib = turn_queries(core_id, queries, sibling_queries, 2 * give.shape[1])
+    lists = jnp.concatenate([vert_lists.T, vert_count[None], slash_offsets.T, slash_count[None]])
+    bias = pattern_bias(ids, 4 * planes, vert_blocks.shape[1], slash_offsets.shape[1], lists)
     late_b, near_a, bias, q_keep, q_sib = lax.optimization_barrier((b, near_a, bias, q_keep, q_sib))
-    near_b = trade(late_b, 1)
-    x_near_a = across(near_a)
-    far_a, q_sib, bias, x_b = lax.optimization_barrier((far_a, q_sib, bias, x_b))
-    last_a = trade(far_a, 1)
-    x_far_a = across(far_a)
+    near_b, x_near_a = trade(late_b, 1), across(near_a)
+    state = attend_stage(0, bias, q_keep, q_sib, [a, b, x_a, x_b], ())
+    early_a, state = lax.optimization_barrier((far_a, state))
+    last_a = trade(early_a, 1)
+    x_far_b = across(far_b)
+    late_far_b = far_b
+    last_b = trade(late_far_b, 1)
+    late_far_a, x_near_a = lax.optimization_barrier((far_a, x_near_a))
+    x_far_a = across(late_far_a)
     x_near_b = across(near_b)
-    state = attend_stage(0, bias, q_keep, q_sib, [a, b, x_a, x_b], ())
-    far_b, state = lax.optimization_barrier((far_b, state))
-    last_b = trade(far_b, 1)
-    x_far_b = across(far_b)
-    state = attend_stage(1, bias, q_keep, q_sib, [near_a, near_b, x_near_a, x_near_b], state)
-    go_b, state = lax.optimization_barrier((last_b, state))
-    x_last_a, x_last_b = trade(x_far_a, 1), across(go_b)
-    state = attend_stage(2, bias, q_keep, q_sib, [far_a, far_b, x_far_a, x_far_b], state)
+    x_last_a, x_last_b = across(last_a), trade(x_far_b, 1)
+    state = attend_stage(4, bias, q_keep, q_sib, [near_a, near_b, x_near_a, x_near_b], state)
+    state = attend_stage(8, bias, q_keep, q_sib, [far_a, far_b, x_far_a, x_far_b], state)
     tiles = [last_a, last_b, x_last_a, x_last_b]
-    sibling_rows = attend_stage(3, bias, q_keep, q_sib, tiles, state, "sibling", core_id)
+    sibling_rows = attend_stage(12, bias, q_keep, q_sib, tiles, state, "sibling", core_id)
     state, sibling_rows = lax.optimization_barrier((state, sibling_rows))
-    own_rows = attend_stage(3, bias, q_keep, q_sib, tiles, state, "own", core_id)
+    own_rows = attend_stage(12, bias, q_keep, q_sib, tiles, state, "own", core_id)
     return join_heads(core_id, sibling(sibling_rows), own_rows)
 
 
 def on_device(queries, keys, values, vert_blocks, vert_count, slash_offsets, slash_count):
     gathered = 2 * keys.size * keys.dtype.itemsize * lax.axis_size("seq") * lax.axis_size("blk")
-    fits = gathered <= GATHER_BYTES and keys.shape[0] == BLOCK and lax.axis_size("blk") == 4
+    shape = (keys.shape[0], lax.axis_size("seq"), lax.axis_size("blk"))
+    fits = gathered <= GATHER_BYTES and shape == (BLOCK, 4, 4)
     plan = by_key_block if fits else by_head_owner
     return plan(queries, keys, values, vert_blocks, vert_count, slash_offsets, slash_count)
 

time: 38.8 us -> 36.7 us (0.946)
  waiting for transfers between devices: 5.52 us -> 0.6 us
  starting transfers between devices: 18.9 us -> 21.7 us
    ppermute x7, waiting for transfers between devices: 4.17 us -> 0.57 us  [across(): return lax.ppermute(tile, 'blk', [(0, 2), (2, 0), (1, 3), (3, 1)])]
    ppermute x7, starting transfers between devices: 7.86 us -> 10.6 us  [trade(): return lax.ppermute(tile, 'seq', [(i, i ^ step) for i in range(planes)])]
    ppermute x7, waiting for transfers between devices: 1.34 us -> 0.02 us  [trade(): return lax.ppermute(tile, 'seq', [(i, i ^ step) for i in range(planes)])]
    ppermute x3, starting transfers between devices: 4.29 us -> 5.02 us  [sibling(): return lax.ppermute(tile, 'blk', [(0, 1), (1, 0), (2, 3), (3, 2)])]
    ppermute x7, starting transfers between devices: 6.72 us -> 6.08 us  [across(): return lax.ppermute(tile, 'blk', [(0, 2), (2, 0), (1, 3), (3, 1)])]
  transfers between devices with their start and end apart: 17 -> 17, of which waited for: 6 -> 1; matrix products, arithmetic and copies ran while one was open for 2% -> 3% of each run, Pallas kernels for 26% -> 27%
where the time goes in v3:
time: 36.7 us; the launch traced here: 36.5 us
  starting transfers between devices  21.7 us (59%)
  Pallas kernels  11.9 us (32%)
  local copies, waits for them, and re-layouts  1.3 us (4%)
  other arithmetic  0.85 us (2%)
  waiting for transfers between devices  0.6 us (2%)
    ppermute x7, starting transfers between devices, trade(): return lax.ppermute(tile, 'seq', [(i, i ^ step) for i in range(planes)])  10.6 us
    pallas_call x5, Pallas kernels, attend_stage(): pl.pallas_call(functools.partial(stage_body, first_slot, rows_of, len(til...  8.25 us
    ppermute x7, starting transfers between devices, across(): return lax.ppermute(tile, 'blk', [(0, 2), (2, 0), (1, 3), (3, 1)])  6.08 us
    ppermute x3, starting transfers between devices, sibling(): return lax.ppermute(tile, 'blk', [(0, 1), (1, 0), (2, 3), (3, 2)])  5.02 us
    pallas_call x1, Pallas kernels, split_heads(): pl.pallas_call(split_body, out_shape=[half, half], in_specs=[pl.BlockSpec...  1.74 us
    unnamed x4, local copies, waits for them, and re-layouts  1.23 us
    pallas_call x1, Pallas kernels, pattern_bias(): pl.pallas_call(functools.partial(pattern_body, vert_rows, slash_rows), ou...  0.92 us
    pallas_call x1, Pallas kernels, join_heads(): pl.pallas_call(join_body, out_shape=jax.ShapeDtypeStruct(begun.shape, beg...  0.81 us
  transfers between devices with their start and end apart: 17, of which 1 were waited for; matrix products, arithmetic and copies ran while one was open for 3% of the time, Pallas kernels for 27%

profile of v3, /device:TPU:1, one launch (start us, length us, event | category | flops | bytes accessed | tf_op | source)
XLA Modules:
  0.0 36.5 jit_solution(6385272426189335640)
XLA Ops:
  0.0 0.1 collective-permute-start.1
  0.1 1.7 %split.1 = (bf16[2,4,64,128]{3,2,1,0:T(8,128)(2,1)}, bf16[2,4,64,128]{3,2,1,0:T(8,128)(2,1)}) custom-call(s32[1]{0:T(128)} %bitcast.core_ref.refs_10_, bf16[64,8,128]{2,1,0:T(8,128)(2,1)} %k_hbm.1, bf16[64,8,128]{2,1,0:T(8,128)(2,1)} %v_hbm.1), custom_call_target="tpu_custom_call" | custom-call | flops 1000 | bytes 1000 | tf_op jit(solution)/shard_map/split/pallas_call | solution.py:354
  1.8 0.0 copy-start.1
  1.8 0.5 %collective-permute-start = (bf16[2,4,64,128]{3,2,1,0:T(8,128)(2,1)}, bf16[2,4,64,128]{3,2,1,0:T(8,128)(2,1)S(1)}, u32[]{:S(2)}, u32[]{:S(2)}) collective-permute-start(bf16[2,4,64,128]{3,2,1,0:T(8,128)(2,1)} %get-tuple-element.37), channel_id=1, source_target_pairs={{0,1},{1,0},{2,3},{3,2},{4,5},{5,4},{6,7},{7,6},{8,9},{9,8},{10,11... | collective-permute-start | bytes 393224 | tf_op jit(solution)/shard_map/ppermute | solution.py:406
  2.3 2.4 %collective-permute-start.2 = (bf16[2,4,64,128]{3,2,1,0:T(8,128)(2,1)}, bf16[2,4,64,128]{3,2,1,0:T(8,128)(2,1)S(1)}, u32[]{:S(2)}, u32[]{:S(2)}) collective-permute-start(bf16[2,4,64,128]{3,2,1,0:T(8,128)(2,1)} %get-tuple-element.49.refs_3_), channel_id=1, source_target_pairs={{0,4},{4,0},{8,12},{12,8},{1,5},{5,1},{9,13},{13,9},{2,6},{6,2},{1... | collective-permute-start | bytes 393224 | tf_op jit(solution)/shard_map/ppermute | solution.py:400
  4.7 2.2 %collective-permute-start.3 = (bf16[2,4,64,128]{3,2,1,0:T(8,128)(2,1)}, bf16[2,4,64,128]{3,2,1,0:T(8,128)(2,1)S(1)}, u32[]{:S(2)}, u32[]{:S(2)}) collective-permute-start(bf16[2,4,64,128]{3,2,1,0:T(8,128)(2,1)} %get-tuple-element.49.refs_3_), channel_id=1, source_target_pairs={{0,12},{4,8},{8,4},{12,0},{1,13},{5,9},{9,5},{13,1},{2,14},{6,10},... | collective-permute-start | bytes 393224 | tf_op jit(solution)/shard_map/ppermute | solution.py:400
  6.9 0.1 broadcast_add_fusion
  7.0 0.0 collective-permute-done.refs_4_
  7.0 0.0 collective-permute-done.1.q_sib
  7.0 1.3 %collective-permute-start.11 = (bf16[2,4,64,128]{3,2,1,0:T(8,128)(2,1)S(1)}, bf16[2,4,64,128]{3,2,1,0:T(8,128)(2,1)S(1)}, u32[]{:S(2)}, u32[]{:S(2)}) collective-permute-start(bf16[2,4,64,128]{3,2,1,0:T(8,128)(2,1)S(1)} %collective-permute-done.refs_4_), channel_id=1, source_target_pairs={{0,2},{2,0},{1,3},{3,1},{4,6},{6,4},{5,7},{7,5},{8,10},{10,8},{9,1... | collective-permute-start | bytes 393224 | tf_op jit(solution)/shard_map/ppermute | solution.py:403
  8.3 1.2 %collective-permute-start.4 = (bf16[2,4,64,128]{3,2,1,0:T(8,128)(2,1)S(1)}, bf16[2,4,64,128]{3,2,1,0:T(8,128)(2,1)S(1)}, u32[]{:S(2)}, u32[]{:S(2)}) collective-permute-start(bf16[2,4,64,128]{3,2,1,0:T(8,128)(2,1)S(1)} %collective-permute-done.refs_4_), channel_id=1, source_target_pairs={{0,12},{4,8},{8,4},{12,0},{1,13},{5,9},{9,5},{13,1},{2,14},{6,10},... | collective-permute-start | bytes 393224 | tf_op jit(solution)/shard_map/ppermute | solution.py:400
  9.4 0.3 collective-permute-start.10
  9.7 0.1 concatenate.6.ids
  9.8 0.8 %pad_add_fusion.lists = s32[32,64]{1,0:T(8,128)S(1)} fusion(s32[1,64]{1,0:T(1,128)} %bitcast.13, s32[14,64]{1,0:T(8,128)} %bitcast.11, s32[1,64]{1,0:T(1,128)} %bitcast.14, s32[16,64]{1,0:T(8,128)} %bitcast.12), kind=kLoop, calls=%fused_computation | loop fusion | flops 6144 | bytes 16384 | tf_op jit(solution)/shard_map/concatenate | solution.py:422
  10.5 0.9 %pattern.1.refs_0_ = f32[2,32,1024]{2,1,0:T(8,128)S(1)} custom-call(s32[19]{0:T(128)S(1)} %concatenate.6.ids, s32[32,64]{1,0:T(8,128)S(1)} %pad_add_fusion.lists), custom_call_target="tpu_custom_call" | custom-call | bytes 16777216 | tf_op jit(solution)/shard_map/pattern/pallas_call | solution.py:207
  11.5 0.0 copy-start
  11.5 1.2 %copy-done = bf16[64,64,128]{2,1,0:T(8,128)(2,1)S(1)} copy-done((bf16[64,64,128]{2,1,0:T(8,128)(2,1)S(1)}, bf16[64,64,128]{2,1,0:T(8,128)(2,1)}, u32[]{:S(2)}) %copy-start) | copy-done | bytes 1048600
  12.7 0.2 turn.1
  12.9 0.0 collective-permute-done.2.refs_3_
  12.9 1.3 %collective-permute-start.5 = (bf16[2,4,64,128]{3,2,1,0:T(8,128)(2,1)S(1)}, bf16[2,4,64,128]{3,2,1,0:T(8,128)(2,1)S(1)}, u32[]{:S(2)}, u32[]{:S(2)}) collective-permute-start(bf16[2,4,64,128]{3,2,1,0:T(8,128)(2,1)S(1)} %collective-permute-done.2.refs_3_), channel_id=1, source_target_pairs={{0,2},{2,0},{1,3},{3,1},{4,6},{6,4},{5,7},{7,5},{8,10},{10,8},{9,1... | collective-permute-start | bytes 393224 | tf_op jit(solution)/shard_map/ppermute | solution.py:403
  14.2 0.0 collective-permute-done.10.refs_5_
  14.2 0.3 collective-permute-start.8
  14.4 0.0 collective-permute-done.11.refs_6_
  14.4 0.0 copy-done.1
  14.4 1.5 %attend.5 = (f32[2,4,512,128]{3,2,1,0:T(8,128)S(1)}, f32[2,4,512,128]{3,2,1,0:T(8,128)S(1)}, f32[2,4,512,128]{3,2,1,0:T(8,128)S(1)}) custom-call(f32[2,32,1024]{2,1,0:T(8,128)S(1)} %pattern.1.refs_0_, bf16[4,512,128]{2,1,0:T(8,128)(2,1)S(1)} %get-tuple-element.43.refs_1_, bf16[4,512,128]{2,1,0:T(8,128)(2,1)S(1)} %get-tuple-element.44.refs_2_, ...), custom_call_target="tpu_custom_call" | custom-call | flops 1000 | bytes 1000 | tf_op jit(solution)/shard_map/attend/pallas_call | solution.py:298
  16.0 0.0 collective-permute-done.3.refs_3_
  16.0 1.3 %collective-permute-start.12 = (bf16[2,4,64,128]{3,2,1,0:T(8,128)(2,1)S(1)}, bf16[2,4,64,128]{3,2,1,0:T(8,128)(2,1)S(1)}, u32[]{:S(2)}, u32[]{:S(2)}) collective-permute-start(bf16[2,4,64,128]{3,2,1,0:T(8,128)(2,1)S(1)} %collective-permute-done.3.refs_3_), channel_id=1, source_target_pairs={{0,4},{4,0},{8,12},{12,8},{1,5},{5,1},{9,13},{13,9},{2,6},{6,2},{1... | collective-permute-start | bytes 393224 | tf_op jit(solution)/shard_map/ppermute | solution.py:400
  17.2 0.0 collective-permute-done.4.refs_4_
  17.2 1.2 %collective-permute-start.7 = (bf16[2,4,64,128]{3,2,1,0:T(8,128)(2,1)S(1)}, bf16[2,4,64,128]{3,2,1,0:T(8,128)(2,1)S(1)}, u32[]{:S(2)}, u32[]{:S(2)}) collective-permute-start(bf16[2,4,64,128]{3,2,1,0:T(8,128)(2,1)S(1)} %collective-permute-done.4.refs_4_), channel_id=1, source_target_pairs={{0,2},{2,0},{1,3},{3,1},{4,6},{6,4},{5,7},{7,5},{8,10},{10,8},{9,1... | collective-permute-start | bytes 393224 | tf_op jit(solution)/shard_map/ppermute | solution.py:403
  18.5 0.0 collective-permute-done.8.refs_4_
  18.5 1.0 %collective-permute-start.9 = (bf16[2,4,64,128]{3,2,1,0:T(8,128)(2,1)S(1)}, bf16[2,4,64,128]{3,2,1,0:T(8,128)(2,1)S(1)}, u32[]{:S(2)}, u32[]{:S(2)}) collective-permute-start(bf16[2,4,64,128]{3,2,1,0:T(8,128)(2,1)S(1)} %collective-permute-done.8.refs_4_), channel_id=1, source_target_pairs={{0,2},{2,0},{1,3},{3,1},{4,6},{6,4},{5,7},{7,5},{8,10},{10,8},{9,1... | collective-permute-start | bytes 393224 | tf_op jit(solution)/shard_map/ppermute | solution.py:403
  19.5 0.0 collective-permute-done.5.refs_5_
  19.5 0.4 %collective-permute-start.6 = (bf16[2,4,64,128]{3,2,1,0:T(8,128)(2,1)S(1)}, bf16[2,4,64,128]{3,2,1,0:T(8,128)(2,1)S(1)}, u32[]{:S(2)}, u32[]{:S(2)}) collective-permute-start(bf16[2,4,64,128]{3,2,1,0:T(8,128)(2,1)S(1)} %collective-permute-done.3.refs_3_), channel_id=1, source_target_pairs={{0,2},{2,0},{1,3},{3,1},{4,6},{6,4},{5,7},{7,5},{8,10},{10,8},{9,1... | collective-permute-start | bytes 393224 | tf_op jit(solution)/shard_map/ppermute | solution.py:403
  20.0 1.9 %collective-permute-start.13 = (bf16[2,4,64,128]{3,2,1,0:T(8,128)(2,1)S(1)}, bf16[2,4,64,128]{3,2,1,0:T(8,128)(2,1)S(1)}, u32[]{:S(2)}, u32[]{:S(2)}) collective-permute-start(bf16[2,4,64,128]{3,2,1,0:T(8,128)(2,1)S(1)} %collective-permute-done.4.refs_4_), channel_id=1, source_target_pairs={{0,4},{4,0},{8,12},{12,8},{1,5},{5,1},{9,13},{13,9},{2,6},{6,2},{1... | collective-permute-start | bytes 393224 | tf_op jit(solution)/shard_map/ppermute | solution.py:400
  21.8 0.0 collective-permute-done.12.refs_3_
  21.8 0.6 %collective-permute-start.14 = (bf16[2,4,64,128]{3,2,1,0:T(8,128)(2,1)S(1)}, bf16[2,4,64,128]{3,2,1,0:T(8,128)(2,1)S(1)}, u32[]{:S(2)}, u32[]{:S(2)}) collective-permute-start(bf16[2,4,64,128]{3,2,1,0:T(8,128)(2,1)S(1)} %collective-permute-done.12.refs_3_), channel_id=1, source_target_pairs={{0,2},{2,0},{1,3},{3,1},{4,6},{6,4},{5,7},{7,5},{8,10},{10,8},{9,1... | collective-permute-start | bytes 393224 | tf_op jit(solution)/shard_map/ppermute | solution.py:403
  22.4 0.0 collective-permute-done.7.refs_6_
  22.4 1.4 %collective-permute-start.15 = (bf16[2,4,64,128]{3,2,1,0:T(8,128)(2,1)S(1)}, bf16[2,4,64,128]{3,2,1,0:T(8,128)(2,1)S(1)}, u32[]{:S(2)}, u32[]{:S(2)}) collective-permute-start(bf16[2,4,64,128]{3,2,1,0:T(8,128)(2,1)S(1)} %collective-permute-done.7.refs_6_), channel_id=1, source_target_pairs={{0,4},{4,0},{8,12},{12,8},{1,5},{5,1},{9,13},{13,9},{2,6},{6,2},{1... | collective-permute-start | bytes 393224 | tf_op jit(solution)/shard_map/ppermute | solution.py:400
  23.9 0.0 collective-permute-done.9.refs_6_
  23.9 1.8 %attend.6 = (f32[2,4,512,128]{3,2,1,0:T(8,128)S(1)}, f32[2,4,512,128]{3,2,1,0:T(8,128)S(1)}, f32[2,4,512,128]{3,2,1,0:T(8,128)S(1)}) custom-call(f32[2,32,1024]{2,1,0:T(8,128)S(1)} %pattern.1.refs_0_, bf16[4,512,128]{2,1,0:T(8,128)(2,1)S(1)} %get-tuple-element.43.refs_1_, bf16[4,512,128]{2,1,0:T(8,128)(2,1)S(1)} %get-tuple-element.44.refs_2_, ...), custom_call_target="tpu_custom_call" | custom-call | flops 1000 | bytes 1000 | tf_op jit(solution)/shard_map/attend/pallas_call | solution.py:298
  25.7 0.0 collective-permute-done.6.refs_5_
  25.7 1.8 %attend.7 = (f32[2,4,512,128]{3,2,1,0:T(8,128)S(1)}, f32[2,4,512,128]{3,2,1,0:T(8,128)S(1)}, f32[2,4,512,128]{3,2,1,0:T(8,128)S(1)}) custom-call(f32[2,32,1024]{2,1,0:T(8,128)S(1)} %pattern.1.refs_0_, bf16[4,512,128]{2,1,0:T(8,128)(2,1)S(1)} %get-tuple-element.43.refs_1_, bf16[4,512,128]{2,1,0:T(8,128)(2,1)S(1)} %get-tuple-element.44.refs_2_, ...), custom_call_target="tpu_custom_call" | custom-call | flops 1000 | bytes 1000 | tf_op jit(solution)/shard_map/attend/pallas_call | solution.py:298
  27.5 0.0 collective-permute-done.13.refs_4_
  27.5 0.6 %collective-permute-done.14.refs_5_ = bf16[2,4,64,128]{3,2,1,0:T(8,128)(2,1)S(1)} collective-permute-done((bf16[2,4,64,128]{3,2,1,0:T(8,128)(2,1)S(1)}, bf16[2,4,64,128]{3,2,1,0:T(8,128)(2,1)S(1)}, u32[]{:S(2)}, u32[]{:S(2)}) %collective-permute-start.14) | collective-permute-done | bytes 131104 | tf_op jit(solution)/shard_map/ppermute | solution.py:403
  28.1 0.0 collective-permute-done.15.refs_6_
  28.1 1.2 %attend.8 = bf16[64,32,128]{2,1,0:T(8,128)(2,1)S(1)} custom-call(f32[2,32,1024]{2,1,0:T(8,128)S(1)} %pattern.1.refs_0_, bf16[4,512,128]{2,1,0:T(8,128)(2,1)S(1)} %get-tuple-element.43.refs_1_, bf16[4,512,128]{2,1,0:T(8,128)(2,1)S(1)} %get-tuple-element.44.refs_2_, bf16[2,4,64,128]{3,2,1,0:T(8,128)(2,1)S(1)} %collective-permute-done.12.refs_3_, ...), custom_call_target="tpu_custom_call" | custom-call | flops 1000 | bytes 1000 | tf_op jit(solution)/shard_map/attend/pallas_call | solution.py:298
  29.2 4.4 %collective-permute-start.16 = (bf16[64,32,128]{2,1,0:T(8,128)(2,1)S(1)}, bf16[64,32,128]{2,1,0:T(8,128)(2,1)S(1)}, u32[]{:S(2)}, u32[]{:S(2)}) collective-permute-start(bf16[64,32,128]{2,1,0:T(8,128)(2,1)S(1)} %attend.8), channel_id=1, source_target_pairs={{0,1},{1,0},{2,3},{3,2},{4,5},{5,4},{6,7},{7,6},{8,9},{9,8},{10,11... | collective-permute-start | bytes 1572872 | tf_op jit(solution)/shard_map/ppermute | solution.py:406
  33.7 2.0 %attend.9.begun_ref = bf16[64,64,128]{2,1,0:T(8,128)(2,1)} custom-call(f32[2,32,1024]{2,1,0:T(8,128)S(1)} %pattern.1.refs_0_, bf16[4,512,128]{2,1,0:T(8,128)(2,1)S(1)} %get-tuple-element.43.refs_1_, bf16[4,512,128]{2,1,0:T(8,128)(2,1)S(1)} %get-tuple-element.44.refs_2_, bf16[2,4,64,128]{3,2,1,0:T(8,128)(2,1)S(1)} %collective-permute-done.12.refs_3_, ...), custom_call_target="tpu_custom_call" | custom-call | flops 1000 | bytes 1000 | tf_op jit(solution)/shard_map/attend/pallas_call | solution.py:298
  35.6 0.0 collective-permute-done.16.other_ref
  35.7 0.8 %join.1 = bf16[64,64,128]{2,1,0:T(8,128)(2,1)} custom-call(s32[1]{0:T(128)} %bitcast.core_ref.refs_10_, bf16[64,32,128]{2,1,0:T(8,128)(2,1)S(1)} %collective-permute-done.16.other_ref, bf16[64,64,128]{2,1,0:T(8,128)(2,1)} %attend.9.begun_ref), custom_call_target="tpu_custom_call", output_to_operand_aliasing={{}: (2, {})} | custom-call | flops 1000 | bytes 1000 | tf_op jit(solution)/shard_map/join/pallas_call | solution.py:380
  (1 shorter events, 0.0 us)
Async XLA Ops:
  0.0 7.0 %collective-permute-start.1 = (bf16[64,64,128]{2,1,0:T(8,128)(2,1)}, bf16[64,64,128]{2,1,0:T(8,128)(2,1)S(1)}, u32[]{:S(2)}, u32[]{:S(2)}) collective-permute-start(bf16[64,64,128]{2,1,0:T(8,128)(2,1)} %q_own.1), channel_id=1, source_target_pairs={{0,1},{1,0},{2,3},{3,2},{4,5},{5,4},{6,7},{7,6},{8,9},{9,8},{10,11... | collective-permute-start | bytes 3145736 | tf_op jit(solution)/shard_map/ppermute | solution.py:406
  1.8 12.6 %copy-start.1 = (bf16[2,4,64,128]{3,2,1,0:T(8,128)(2,1)S(1)}, bf16[2,4,64,128]{3,2,1,0:T(8,128)(2,1)}, u32[]{:S(2)}) copy-start(bf16[2,4,64,128]{3,2,1,0:T(8,128)(2,1)} %get-tuple-element.49.refs_3_) | copy-start | bytes 393220
  1.8 5.2 %collective-permute-start = (bf16[2,4,64,128]{3,2,1,0:T(8,128)(2,1)}, bf16[2,4,64,128]{3,2,1,0:T(8,128)(2,1)S(1)}, u32[]{:S(2)}, u32[]{:S(2)}) collective-permute-start(bf16[2,4,64,128]{3,2,1,0:T(8,128)(2,1)} %get-tuple-element.37), channel_id=1, source_target_pairs={{0,1},{1,0},{2,3},{3,2},{4,5},{5,4},{6,7},{7,6},{8,9},{9,8},{10,11... | collective-permute-start | bytes 393224 | tf_op jit(solution)/shard_map/ppermute | solution.py:406
  2.3 10.5 %collective-permute-start.2 = (bf16[2,4,64,128]{3,2,1,0:T(8,128)(2,1)}, bf16[2,4,64,128]{3,2,1,0:T(8,128)(2,1)S(1)}, u32[]{:S(2)}, u32[]{:S(2)}) collective-permute-start(bf16[2,4,64,128]{3,2,1,0:T(8,128)(2,1)} %get-tuple-element.49.refs_3_), channel_id=1, source_target_pairs={{0,4},{4,0},{8,12},{12,8},{1,5},{5,1},{9,13},{13,9},{2,6},{6,2},{1... | collective-permute-start | bytes 393224 | tf_op jit(solution)/shard_map/ppermute | solution.py:400
  4.7 11.2 %collective-permute-start.3 = (bf16[2,4,64,128]{3,2,1,0:T(8,128)(2,1)}, bf16[2,4,64,128]{3,2,1,0:T(8,128)(2,1)S(1)}, u32[]{:S(2)}, u32[]{:S(2)}) collective-permute-start(bf16[2,4,64,128]{3,2,1,0:T(8,128)(2,1)} %get-tuple-element.49.refs_3_), channel_id=1, source_target_pairs={{0,12},{4,8},{8,4},{12,0},{1,13},{5,9},{9,5},{13,1},{2,14},{6,10},... | collective-permute-start | bytes 393224 | tf_op jit(solution)/shard_map/ppermute | solution.py:400
  7.0 7.4 %collective-permute-start.11 = (bf16[2,4,64,128]{3,2,1,0:T(8,128)(2,1)S(1)}, bf16[2,4,64,128]{3,2,1,0:T(8,128)(2,1)S(1)}, u32[]{:S(2)}, u32[]{:S(2)}) collective-permute-start(bf16[2,4,64,128]{3,2,1,0:T(8,128)(2,1)S(1)} %collective-permute-done.refs_4_), channel_id=1, source_target_pairs={{0,2},{2,0},{1,3},{3,1},{4,6},{6,4},{5,7},{7,5},{8,10},{10,8},{9,1... | collective-permute-start | bytes 393224 | tf_op jit(solution)/shard_map/ppermute | solution.py:403
  8.3 9.0 %collective-permute-start.4 = (bf16[2,4,64,128]{3,2,1,0:T(8,128)(2,1)S(1)}, bf16[2,4,64,128]{3,2,1,0:T(8,128)(2,1)S(1)}, u32[]{:S(2)}, u32[]{:S(2)}) collective-permute-start(bf16[2,4,64,128]{3,2,1,0:T(8,128)(2,1)S(1)} %collective-permute-done.refs_4_), channel_id=1, source_target_pairs={{0,12},{4,8},{8,4},{12,0},{1,13},{5,9},{9,5},{13,1},{2,14},{6,10},... | collective-permute-start | bytes 393224 | tf_op jit(solution)/shard_map/ppermute | solution.py:400
  9.4 4.7 %collective-permute-start.10 = (bf16[2,4,64,128]{3,2,1,0:T(8,128)(2,1)}, bf16[2,4,64,128]{3,2,1,0:T(8,128)(2,1)S(1)}, u32[]{:S(2)}, u32[]{:S(2)}) collective-permute-start(bf16[2,4,64,128]{3,2,1,0:T(8,128)(2,1)} %get-tuple-element.49.refs_3_), channel_id=1, source_target_pairs={{0,2},{2,0},{1,3},{3,1},{4,6},{6,4},{5,7},{7,5},{8,10},{10,8},{9,1... | collective-permute-start | bytes 393224 | tf_op jit(solution)/shard_map/ppermute | solution.py:403
  11.5 1.2 %copy-start = (bf16[64,64,128]{2,1,0:T(8,128)(2,1)S(1)}, bf16[64,64,128]{2,1,0:T(8,128)(2,1)}, u32[]{:S(2)}) copy-start(bf16[64,64,128]{2,1,0:T(8,128)(2,1)} %q_own.1) | copy-start | bytes 3145732
  12.9 6.6 %collective-permute-start.5 = (bf16[2,4,64,128]{3,2,1,0:T(8,128)(2,1)S(1)}, bf16[2,4,64,128]{3,2,1,0:T(8,128)(2,1)S(1)}, u32[]{:S(2)}, u32[]{:S(2)}) collective-permute-start(bf16[2,4,64,128]{3,2,1,0:T(8,128)(2,1)S(1)} %collective-permute-done.2.refs_3_), channel_id=1, source_target_pairs={{0,2},{2,0},{1,3},{3,1},{4,6},{6,4},{5,7},{7,5},{8,10},{10,8},{9,1... | collective-permute-start | bytes 393224 | tf_op jit(solution)/shard_map/ppermute | solution.py:403
  14.2 4.3 %collective-permute-start.8 = (bf16[2,4,64,128]{3,2,1,0:T(8,128)(2,1)S(1)}, bf16[2,4,64,128]{3,2,1,0:T(8,128)(2,1)S(1)}, u32[]{:S(2)}, u32[]{:S(2)}) collective-permute-start(bf16[2,4,64,128]{3,2,1,0:T(8,128)(2,1)S(1)} %collective-permute-done.refs_4_), channel_id=1, source_target_pairs={{0,4},{4,0},{8,12},{12,8},{1,5},{5,1},{9,13},{13,9},{2,6},{6,2},{1... | collective-permute-start | bytes 393224 | tf_op jit(solution)/shard_map/ppermute | solution.py:400
  16.0 5.9 %collective-permute-start.12 = (bf16[2,4,64,128]{3,2,1,0:T(8,128)(2,1)S(1)}, bf16[2,4,64,128]{3,2,1,0:T(8,128)(2,1)S(1)}, u32[]{:S(2)}, u32[]{:S(2)}) collective-permute-start(bf16[2,4,64,128]{3,2,1,0:T(8,128)(2,1)S(1)} %collective-permute-done.3.refs_3_), channel_id=1, source_target_pairs={{0,4},{4,0},{8,12},{12,8},{1,5},{5,1},{9,13},{13,9},{2,6},{6,2},{1... | collective-permute-start | bytes 393224 | tf_op jit(solution)/shard_map/ppermute | solution.py:400
  17.2 5.2 %collective-permute-start.7 = (bf16[2,4,64,128]{3,2,1,0:T(8,128)(2,1)S(1)}, bf16[2,4,64,128]{3,2,1,0:T(8,128)(2,1)S(1)}, u32[]{:S(2)}, u32[]{:S(2)}) collective-permute-start(bf16[2,4,64,128]{3,2,1,0:T(8,128)(2,1)S(1)} %collective-permute-done.4.refs_4_), channel_id=1, source_target_pairs={{0,2},{2,0},{1,3},{3,1},{4,6},{6,4},{5,7},{7,5},{8,10},{10,8},{9,1... | collective-permute-start | bytes 393224 | tf_op jit(solution)/shard_map/ppermute | solution.py:403
  18.5 5.4 %collective-permute-start.9 = (bf16[2,4,64,128]{3,2,1,0:T(8,128)(2,1)S(1)}, bf16[2,4,64,128]{3,2,1,0:T(8,128)(2,1)S(1)}, u32[]{:S(2)}, u32[]{:S(2)}) collective-permute-start(bf16[2,4,64,128]{3,2,1,0:T(8,128)(2,1)S(1)} %collective-permute-done.8.refs_4_), channel_id=1, source_target_pairs={{0,2},{2,0},{1,3},{3,1},{4,6},{6,4},{5,7},{7,5},{8,10},{10,8},{9,1... | collective-permute-start | bytes 393224 | tf_op jit(solution)/shard_map/ppermute | solution.py:403
  19.5 6.2 %collective-permute-start.6 = (bf16[2,4,64,128]{3,2,1,0:T(8,128)(2,1)S(1)}, bf16[2,4,64,128]{3,2,1,0:T(8,128)(2,1)S(1)}, u32[]{:S(2)}, u32[]{:S(2)}) collective-permute-start(bf16[2,4,64,128]{3,2,1,0:T(8,128)(2,1)S(1)} %collective-permute-done.3.refs_3_), channel_id=1, source_target_pairs={{0,2},{2,0},{1,3},{3,1},{4,6},{6,4},{5,7},{7,5},{8,10},{10,8},{9,1... | collective-permute-start | bytes 393224 | tf_op jit(solution)/shard_map/ppermute | solution.py:403
  20.0 7.6 %collective-permute-start.13 = (bf16[2,4,64,128]{3,2,1,0:T(8,128)(2,1)S(1)}, bf16[2,4,64,128]{3,2,1,0:T(8,128)(2,1)S(1)}, u32[]{:S(2)}, u32[]{:S(2)}) collective-permute-start(bf16[2,4,64,128]{3,2,1,0:T(8,128)(2,1)S(1)} %collective-permute-done.4.refs_4_), channel_id=1, source_target_pairs={{0,4},{4,0},{8,12},{12,8},{1,5},{5,1},{9,13},{13,9},{2,6},{6,2},{1... | collective-permute-start | bytes 393224 | tf_op jit(solution)/shard_map/ppermute | solution.py:400
  21.8 6.2 %collective-permute-start.14 = (bf16[2,4,64,128]{3,2,1,0:T(8,128)(2,1)S(1)}, bf16[2,4,64,128]{3,2,1,0:T(8,128)(2,1)S(1)}, u32[]{:S(2)}, u32[]{:S(2)}) collective-permute-start(bf16[2,4,64,128]{3,2,1,0:T(8,128)(2,1)S(1)} %collective-permute-done.12.refs_3_), channel_id=1, source_target_pairs={{0,2},{2,0},{1,3},{3,1},{4,6},{6,4},{5,7},{7,5},{8,10},{10,8},{9,1... | collective-permute-start | bytes 393224 | tf_op jit(solution)/shard_map/ppermute | solution.py:403
  22.4 5.7 %collective-permute-start.15 = (bf16[2,4,64,128]{3,2,1,0:T(8,128)(2,1)S(1)}, bf16[2,4,64,128]{3,2,1,0:T(8,128)(2,1)S(1)}, u32[]{:S(2)}, u32[]{:S(2)}) collective-permute-start(bf16[2,4,64,128]{3,2,1,0:T(8,128)(2,1)S(1)} %collective-permute-done.7.refs_6_), channel_id=1, source_target_pairs={{0,4},{4,0},{8,12},{12,8},{1,5},{5,1},{9,13},{13,9},{2,6},{6,2},{1... | collective-permute-start | bytes 393224 | tf_op jit(solution)/shard_map/ppermute | solution.py:400
  29.2 6.4 %collective-permute-start.16 = (bf16[64,32,128]{2,1,0:T(8,128)(2,1)S(1)}, bf16[64,32,128]{2,1,0:T(8,128)(2,1)S(1)}, u32[]{:S(2)}, u32[]{:S(2)}) collective-permute-start(bf16[64,32,128]{2,1,0:T(8,128)(2,1)S(1)} %attend.8), channel_id=1, source_target_pairs={{0,1},{1,0},{2,3},{3,2},{4,5},{5,4},{6,7},{7,6},{8,9},{9,8},{10,11... | collective-permute-start | bytes 1572872 | tf_op jit(solution)/shard_map/ppermute | solution.py:406

commit v4 on v3

--- a/solution.py
+++ b/solution.py
@@ -232,6 +232,7 @@
         acc_out, top_out, sum_out = refs
     kv_heads, rows, head_width = q_own.shape
     width = slots * BLOCK
+    sends = []
     if first:
         pos = lax.broadcasted_iota(jnp.int32, (BLOCK, 1, 2 * BLOCK), 0)
         key = lax.broadcasted_iota(jnp.int32, (BLOCK, 1, 2 * BLOCK), 2)
@@ -267,13 +268,17 @@
             outs.append((acc / total).reshape(BLOCK, group, head_width))
             if g % 2:
                 pair = jnp.concatenate(outs, axis=1).astype(jnp.bfloat16)
-                done_ref[:, (g - 1) * group:(g + 1) * group, :] = pair
+                part = pl.ds((g - 1) * group, 2 * group)
+                done_ref[:, part, :] = pair
                 outs = []
-    if last and rows_of == "own":
-        half = kv_heads * group
-        place = pl.ds(pl.multiple_of(core[0] * half, half), half)
-        send = pltpu.make_async_copy(done_ref, out.at[:, place, :], sems[0])
-        send.start()
+                if rows_of == "own":
+                    place = pl.ds(pl.multiple_of((core[0] * kv_heads + g - 1) * group, 2 * group), 2 * group)
+                    for n in range(2):
+                        at = pl.ds(n * BLOCK // 2, BLOCK // 2)
+                        send = pltpu.make_async_copy(done_ref.at[at, part, :], out.at[at, place, :], sems[0].at[g - 1 + n])
+                        send.start()
+                        sends.append(send)
+    for send in sends:
         send.wait()
 
 
@@ -294,7 +299,7 @@
         if rows_of == "own":
             out = jax.ShapeDtypeStruct((BLOCK, 2 * half[1], head_width), jnp.bfloat16)
             out_specs = pl.BlockSpec(memory_space=pl.ANY)
-            scratch = [pltpu.VMEM(half, jnp.bfloat16), pltpu.SemaphoreType.DMA]
+            scratch = [pltpu.VMEM(half, jnp.bfloat16), pltpu.SemaphoreType.DMA((kv_heads,))]
     return pl.pallas_call(
         functools.partial(stage_body, first_slot, rows_of, len(tiles), group, scale),
         out_shape=out,
@@ -367,12 +372,19 @@
     )(core, keys, values)
 
 
-def join_body(core_ref, other_ref, begun_ref, out_ref, sem):
+def join_body(core_ref, other_ref, begun_ref, out_ref, sems):
     half = other_ref.shape[1]
     place = pl.ds(pl.multiple_of((1 - core_ref[0]) * half, half), half)
-    send = pltpu.make_async_copy(other_ref, out_ref.at[:, place, :], sem)
-    send.start()
-    send.wait()
+    parts = sems.shape[0]
+    step = other_ref.shape[0] // parts
+    sends = [
+        pltpu.make_async_copy(other_ref.at[pl.ds(n * step, step)], out_ref.at[pl.ds(n * step, step), place, :], sems.at[n])
+        for n in range(parts)
+    ]
+    for send in sends:
+        send.start()
+    for send in sends:
+        send.wait()
 
 
 def join_heads(core, other, begun):
@@ -382,7 +394,7 @@
         out_shape=jax.ShapeDtypeStruct(begun.shape, begun.dtype),
         in_specs=[pl.BlockSpec(memory_space=pltpu.SMEM), pl.BlockSpec(memory_space=pltpu.VMEM), somewhere],
         out_specs=somewhere,
-        scratch_shapes=[pltpu.SemaphoreType.DMA],
+        scratch_shapes=[pltpu.SemaphoreType.DMA((4,))],
         input_output_aliases={2: 0},
         compiler_params=pltpu.CompilerParams(vmem_limit_bytes=8 * 1024 * 1024),
         cost_estimate=pl.CostEstimate(flops=1000, bytes_accessed=1000, transcendentals=0),

time: 36.7 us -> 36.6 us (level)
  no operation moved by 1% of the time
where the time goes in v4:
time: 36.6 us; the launch traced here: 36.4 us
  starting transfers between devices  21.7 us (59%)
  Pallas kernels  11.9 us (33%)
  local copies, waits for them, and re-layouts  1.3 us (4%)
  other arithmetic  0.85 us (2%)
  waiting for transfers between devices  0.6 us (2%)
    ppermute x7, starting transfers between devices, trade(): return lax.ppermute(tile, 'seq', [(i, i ^ step) for i in range(planes)])  10.6 us
    pallas_call x5, Pallas kernels, attend_stage(): pl.pallas_call(functools.partial(stage_body, first_slot, rows_of, len(til...  8.2 us
    ppermute x7, starting transfers between devices, across(): return lax.ppermute(tile, 'blk', [(0, 2), (2, 0), (1, 3), (3, 1)])  6.08 us
    ppermute x3, starting transfers between devices, sibling(): return lax.ppermute(tile, 'blk', [(0, 1), (1, 0), (2, 3), (3, 2)])  5.02 us
    pallas_call x1, Pallas kernels, split_heads(): pl.pallas_call(split_body, out_shape=[half, half], in_specs=[pl.BlockSpec...  1.74 us
    unnamed x4, local copies, waits for them, and re-layouts  1.23 us
    pallas_call x1, Pallas kernels, pattern_bias(): pl.pallas_call(functools.partial(pattern_body, vert_rows, slash_rows), ou...  0.92 us
    pallas_call x1, Pallas kernels, join_heads(): pl.pallas_call(join_body, out_shape=jax.ShapeDtypeStruct(begun.shape, beg...  0.82 us
  transfers between devices with their start and end apart: 17, of which 1 were waited for; matrix products, arithmetic and copies ran while one was open for 3% of the time, Pallas kernels for 27%

profile of v4, /device:TPU:1, one launch (start us, length us, event | category | flops | bytes accessed | tf_op | source)
XLA Modules:
  0.0 36.4 jit_solution(11499965188579789247)
XLA Ops:
  0.0 0.1 collective-permute-start.1
  0.1 1.7 %split.1 = (bf16[2,4,64,128]{3,2,1,0:T(8,128)(2,1)}, bf16[2,4,64,128]{3,2,1,0:T(8,128)(2,1)}) custom-call(s32[1]{0:T(128)} %bitcast.core_ref.refs_10_, bf16[64,8,128]{2,1,0:T(8,128)(2,1)} %k_hbm.1, bf16[64,8,128]{2,1,0:T(8,128)(2,1)} %v_hbm.1), custom_call_target="tpu_custom_call" | custom-call | flops 1000 | bytes 1000 | tf_op jit(solution)/shard_map/split/pallas_call | solution.py:359
  1.8 0.0 copy-start.1
  1.8 0.5 %collective-permute-start = (bf16[2,4,64,128]{3,2,1,0:T(8,128)(2,1)}, bf16[2,4,64,128]{3,2,1,0:T(8,128)(2,1)S(1)}, u32[]{:S(2)}, u32[]{:S(2)}) collective-permute-start(bf16[2,4,64,128]{3,2,1,0:T(8,128)(2,1)} %get-tuple-element.37), channel_id=1, source_target_pairs={{0,1},{1,0},{2,3},{3,2},{4,5},{5,4},{6,7},{7,6},{8,9},{9,8},{10,11... | collective-permute-start | bytes 393224 | tf_op jit(solution)/shard_map/ppermute | solution.py:418
  2.3 2.4 %collective-permute-start.2 = (bf16[2,4,64,128]{3,2,1,0:T(8,128)(2,1)}, bf16[2,4,64,128]{3,2,1,0:T(8,128)(2,1)S(1)}, u32[]{:S(2)}, u32[]{:S(2)}) collective-permute-start(bf16[2,4,64,128]{3,2,1,0:T(8,128)(2,1)} %get-tuple-element.49.refs_3_), channel_id=1, source_target_pairs={{0,4},{4,0},{8,12},{12,8},{1,5},{5,1},{9,13},{13,9},{2,6},{6,2},{1... | collective-permute-start | bytes 393224 | tf_op jit(solution)/shard_map/ppermute | solution.py:412
  4.7 2.2 %collective-permute-start.3 = (bf16[2,4,64,128]{3,2,1,0:T(8,128)(2,1)}, bf16[2,4,64,128]{3,2,1,0:T(8,128)(2,1)S(1)}, u32[]{:S(2)}, u32[]{:S(2)}) collective-permute-start(bf16[2,4,64,128]{3,2,1,0:T(8,128)(2,1)} %get-tuple-element.49.refs_3_), channel_id=1, source_target_pairs={{0,12},{4,8},{8,4},{12,0},{1,13},{5,9},{9,5},{13,1},{2,14},{6,10},... | collective-permute-start | bytes 393224 | tf_op jit(solution)/shard_map/ppermute | solution.py:412
  6.9 0.1 broadcast_add_fusion
  7.0 0.0 collective-permute-done.refs_4_
  7.0 0.0 collective-permute-done.1.q_sib
  7.0 1.3 %collective-permute-start.11 = (bf16[2,4,64,128]{3,2,1,0:T(8,128)(2,1)S(1)}, bf16[2,4,64,128]{3,2,1,0:T(8,128)(2,1)S(1)}, u32[]{:S(2)}, u32[]{:S(2)}) collective-permute-start(bf16[2,4,64,128]{3,2,1,0:T(8,128)(2,1)S(1)} %collective-permute-done.refs_4_), channel_id=1, source_target_pairs={{0,2},{2,0},{1,3},{3,1},{4,6},{6,4},{5,7},{7,5},{8,10},{10,8},{9,1... | collective-permute-start | bytes 393224 | tf_op jit(solution)/shard_map/ppermute | solution.py:415
  8.3 1.2 %collective-permute-start.4 = (bf16[2,4,64,128]{3,2,1,0:T(8,128)(2,1)S(1)}, bf16[2,4,64,128]{3,2,1,0:T(8,128)(2,1)S(1)}, u32[]{:S(2)}, u32[]{:S(2)}) collective-permute-start(bf16[2,4,64,128]{3,2,1,0:T(8,128)(2,1)S(1)} %collective-permute-done.refs_4_), channel_id=1, source_target_pairs={{0,12},{4,8},{8,4},{12,0},{1,13},{5,9},{9,5},{13,1},{2,14},{6,10},... | collective-permute-start | bytes 393224 | tf_op jit(solution)/shard_map/ppermute | solution.py:412
  9.4 0.3 collective-permute-start.10
  9.7 0.1 concatenate.6.ids
  9.8 0.8 %pad_add_fusion.lists = s32[32,64]{1,0:T(8,128)S(1)} fusion(s32[1,64]{1,0:T(1,128)} %bitcast.13, s32[14,64]{1,0:T(8,128)} %bitcast.11, s32[1,64]{1,0:T(1,128)} %bitcast.14, s32[16,64]{1,0:T(8,128)} %bitcast.12), kind=kLoop, calls=%fused_computation | loop fusion | flops 6144 | bytes 16384 | tf_op jit(solution)/shard_map/concatenate | solution.py:434
  10.5 0.9 %pattern.1.refs_0_ = f32[2,32,1024]{2,1,0:T(8,128)S(1)} custom-call(s32[19]{0:T(128)S(1)} %concatenate.6.ids, s32[32,64]{1,0:T(8,128)S(1)} %pad_add_fusion.lists), custom_call_target="tpu_custom_call" | custom-call | bytes 16777216 | tf_op jit(solution)/shard_map/pattern/pallas_call | solution.py:207
  11.5 0.0 copy-start
  11.5 1.2 %copy-done = bf16[64,64,128]{2,1,0:T(8,128)(2,1)S(1)} copy-done((bf16[64,64,128]{2,1,0:T(8,128)(2,1)S(1)}, bf16[64,64,128]{2,1,0:T(8,128)(2,1)}, u32[]{:S(2)}) %copy-start) | copy-done | bytes 1048600
  12.7 0.2 turn.1
  12.9 0.0 collective-permute-done.2.refs_3_
  12.9 1.3 %collective-permute-start.5 = (bf16[2,4,64,128]{3,2,1,0:T(8,128)(2,1)S(1)}, bf16[2,4,64,128]{3,2,1,0:T(8,128)(2,1)S(1)}, u32[]{:S(2)}, u32[]{:S(2)}) collective-permute-start(bf16[2,4,64,128]{3,2,1,0:T(8,128)(2,1)S(1)} %collective-permute-done.2.refs_3_), channel_id=1, source_target_pairs={{0,2},{2,0},{1,3},{3,1},{4,6},{6,4},{5,7},{7,5},{8,10},{10,8},{9,1... | collective-permute-start | bytes 393224 | tf_op jit(solution)/shard_map/ppermute | solution.py:415
  14.2 0.0 collective-permute-done.10.refs_5_
  14.2 0.3 collective-permute-start.8
  14.4 0.0 collective-permute-done.11.refs_6_
  14.4 0.0 copy-done.1
  14.4 1.5 %attend.5 = (f32[2,4,512,128]{3,2,1,0:T(8,128)S(1)}, f32[2,4,512,128]{3,2,1,0:T(8,128)S(1)}, f32[2,4,512,128]{3,2,1,0:T(8,128)S(1)}) custom-call(f32[2,32,1024]{2,1,0:T(8,128)S(1)} %pattern.1.refs_0_, bf16[4,512,128]{2,1,0:T(8,128)(2,1)S(1)} %get-tuple-element.43.refs_1_, bf16[4,512,128]{2,1,0:T(8,128)(2,1)S(1)} %get-tuple-element.44.refs_2_, ...), custom_call_target="tpu_custom_call" | custom-call | flops 1000 | bytes 1000 | tf_op jit(solution)/shard_map/attend/pallas_call | solution.py:303
  16.0 0.0 collective-permute-done.3.refs_3_
  16.0 1.3 %collective-permute-start.12 = (bf16[2,4,64,128]{3,2,1,0:T(8,128)(2,1)S(1)}, bf16[2,4,64,128]{3,2,1,0:T(8,128)(2,1)S(1)}, u32[]{:S(2)}, u32[]{:S(2)}) collective-permute-start(bf16[2,4,64,128]{3,2,1,0:T(8,128)(2,1)S(1)} %collective-permute-done.3.refs_3_), channel_id=1, source_target_pairs={{0,4},{4,0},{8,12},{12,8},{1,5},{5,1},{9,13},{13,9},{2,6},{6,2},{1... | collective-permute-start | bytes 393224 | tf_op jit(solution)/shard_map/ppermute | solution.py:412
  17.2 0.0 collective-permute-done.4.refs_4_
  17.2 1.2 %collective-permute-start.7 = (bf16[2,4,64,128]{3,2,1,0:T(8,128)(2,1)S(1)}, bf16[2,4,64,128]{3,2,1,0:T(8,128)(2,1)S(1)}, u32[]{:S(2)}, u32[]{:S(2)}) collective-permute-start(bf16[2,4,64,128]{3,2,1,0:T(8,128)(2,1)S(1)} %collective-permute-done.4.refs_4_), channel_id=1, source_target_pairs={{0,2},{2,0},{1,3},{3,1},{4,6},{6,4},{5,7},{7,5},{8,10},{10,8},{9,1... | collective-permute-start | bytes 393224 | tf_op jit(solution)/shard_map/ppermute | solution.py:415
  18.5 0.0 collective-permute-done.8.refs_4_
  18.5 1.0 %collective-permute-start.9 = (bf16[2,4,64,128]{3,2,1,0:T(8,128)(2,1)S(1)}, bf16[2,4,64,128]{3,2,1,0:T(8,128)(2,1)S(1)}, u32[]{:S(2)}, u32[]{:S(2)}) collective-permute-start(bf16[2,4,64,128]{3,2,1,0:T(8,128)(2,1)S(1)} %collective-permute-done.8.refs_4_), channel_id=1, source_target_pairs={{0,2},{2,0},{1,3},{3,1},{4,6},{6,4},{5,7},{7,5},{8,10},{10,8},{9,1... | collective-permute-start | bytes 393224 | tf_op jit(solution)/shard_map/ppermute | solution.py:415
  19.5 0.0 collective-permute-done.5.refs_5_
  19.5 0.4 %collective-permute-start.6 = (bf16[2,4,64,128]{3,2,1,0:T(8,128)(2,1)S(1)}, bf16[2,4,64,128]{3,2,1,0:T(8,128)(2,1)S(1)}, u32[]{:S(2)}, u32[]{:S(2)}) collective-permute-start(bf16[2,4,64,128]{3,2,1,0:T(8,128)(2,1)S(1)} %collective-permute-done.3.refs_3_), channel_id=1, source_target_pairs={{0,2},{2,0},{1,3},{3,1},{4,6},{6,4},{5,7},{7,5},{8,10},{10,8},{9,1... | collective-permute-start | bytes 393224 | tf_op jit(solution)/shard_map/ppermute | solution.py:415
  20.0 1.9 %collective-permute-start.13 = (bf16[2,4,64,128]{3,2,1,0:T(8,128)(2,1)S(1)}, bf16[2,4,64,128]{3,2,1,0:T(8,128)(2,1)S(1)}, u32[]{:S(2)}, u32[]{:S(2)}) collective-permute-start(bf16[2,4,64,128]{3,2,1,0:T(8,128)(2,1)S(1)} %collective-permute-done.4.refs_4_), channel_id=1, source_target_pairs={{0,4},{4,0},{8,12},{12,8},{1,5},{5,1},{9,13},{13,9},{2,6},{6,2},{1... | collective-permute-start | bytes 393224 | tf_op jit(solution)/shard_map/ppermute | solution.py:412
  21.8 0.0 collective-permute-done.12.refs_3_
  21.8 0.6 %collective-permute-start.14 = (bf16[2,4,64,128]{3,2,1,0:T(8,128)(2,1)S(1)}, bf16[2,4,64,128]{3,2,1,0:T(8,128)(2,1)S(1)}, u32[]{:S(2)}, u32[]{:S(2)}) collective-permute-start(bf16[2,4,64,128]{3,2,1,0:T(8,128)(2,1)S(1)} %collective-permute-done.12.refs_3_), channel_id=1, source_target_pairs={{0,2},{2,0},{1,3},{3,1},{4,6},{6,4},{5,7},{7,5},{8,10},{10,8},{9,1... | collective-permute-start | bytes 393224 | tf_op jit(solution)/shard_map/ppermute | solution.py:415
  22.4 0.0 collective-permute-done.7.refs_6_
  22.4 1.4 %collective-permute-start.15 = (bf16[2,4,64,128]{3,2,1,0:T(8,128)(2,1)S(1)}, bf16[2,4,64,128]{3,2,1,0:T(8,128)(2,1)S(1)}, u32[]{:S(2)}, u32[]{:S(2)}) collective-permute-start(bf16[2,4,64,128]{3,2,1,0:T(8,128)(2,1)S(1)} %collective-permute-done.7.refs_6_), channel_id=1, source_target_pairs={{0,4},{4,0},{8,12},{12,8},{1,5},{5,1},{9,13},{13,9},{2,6},{6,2},{1... | collective-permute-start | bytes 393224 | tf_op jit(solution)/shard_map/ppermute | solution.py:412
  23.9 0.0 collective-permute-done.9.refs_6_
  23.9 1.8 %attend.6 = (f32[2,4,512,128]{3,2,1,0:T(8,128)S(1)}, f32[2,4,512,128]{3,2,1,0:T(8,128)S(1)}, f32[2,4,512,128]{3,2,1,0:T(8,128)S(1)}) custom-call(f32[2,32,1024]{2,1,0:T(8,128)S(1)} %pattern.1.refs_0_, bf16[4,512,128]{2,1,0:T(8,128)(2,1)S(1)} %get-tuple-element.43.refs_1_, bf16[4,512,128]{2,1,0:T(8,128)(2,1)S(1)} %get-tuple-element.44.refs_2_, ...), custom_call_target="tpu_custom_call" | custom-call | flops 1000 | bytes 1000 | tf_op jit(solution)/shard_map/attend/pallas_call | solution.py:303
  25.7 0.0 collective-permute-done.6.refs_5_
  25.7 1.8 %attend.7 = (f32[2,4,512,128]{3,2,1,0:T(8,128)S(1)}, f32[2,4,512,128]{3,2,1,0:T(8,128)S(1)}, f32[2,4,512,128]{3,2,1,0:T(8,128)S(1)}) custom-call(f32[2,32,1024]{2,1,0:T(8,128)S(1)} %pattern.1.refs_0_, bf16[4,512,128]{2,1,0:T(8,128)(2,1)S(1)} %get-tuple-element.43.refs_1_, bf16[4,512,128]{2,1,0:T(8,128)(2,1)S(1)} %get-tuple-element.44.refs_2_, ...), custom_call_target="tpu_custom_call" | custom-call | flops 1000 | bytes 1000 | tf_op jit(solution)/shard_map/attend/pallas_call | solution.py:303
  27.5 0.0 collective-permute-done.13.refs_4_
  27.5 0.6 %collective-permute-done.14.refs_5_ = bf16[2,4,64,128]{3,2,1,0:T(8,128)(2,1)S(1)} collective-permute-done((bf16[2,4,64,128]{3,2,1,0:T(8,128)(2,1)S(1)}, bf16[2,4,64,128]{3,2,1,0:T(8,128)(2,1)S(1)}, u32[]{:S(2)}, u32[]{:S(2)}) %collective-permute-start.14) | collective-permute-done | bytes 131104 | tf_op jit(solution)/shard_map/ppermute | solution.py:415
  28.1 0.0 collective-permute-done.15.refs_6_
  28.1 1.2 %attend.8 = bf16[64,32,128]{2,1,0:T(8,128)(2,1)S(1)} custom-call(f32[2,32,1024]{2,1,0:T(8,128)S(1)} %pattern.1.refs_0_, bf16[4,512,128]{2,1,0:T(8,128)(2,1)S(1)} %get-tuple-element.43.refs_1_, bf16[4,512,128]{2,1,0:T(8,128)(2,1)S(1)} %get-tuple-element.44.refs_2_, bf16[2,4,64,128]{3,2,1,0:T(8,128)(2,1)S(1)} %collective-permute-done.12.refs_3_, ...), custom_call_target="tpu_custom_call" | custom-call | flops 1000 | bytes 1000 | tf_op jit(solution)/shard_map/attend/pallas_call | solution.py:303
  29.2 4.4 %collective-permute-start.16 = (bf16[64,32,128]{2,1,0:T(8,128)(2,1)S(1)}, bf16[64,32,128]{2,1,0:T(8,128)(2,1)S(1)}, u32[]{:S(2)}, u32[]{:S(2)}) collective-permute-start(bf16[64,32,128]{2,1,0:T(8,128)(2,1)S(1)} %attend.8), channel_id=1, source_target_pairs={{0,1},{1,0},{2,3},{3,2},{4,5},{5,4},{6,7},{7,6},{8,9},{9,8},{10,11... | collective-permute-start | bytes 1572872 | tf_op jit(solution)/shard_map/ppermute | solution.py:418
  33.7 1.9 %attend.9.begun_ref = bf16[64,64,128]{2,1,0:T(8,128)(2,1)} custom-call(f32[2,32,1024]{2,1,0:T(8,128)S(1)} %pattern.1.refs_0_, bf16[4,512,128]{2,1,0:T(8,128)(2,1)S(1)} %get-tuple-element.43.refs_1_, bf16[4,512,128]{2,1,0:T(8,128)(2,1)S(1)} %get-tuple-element.44.refs_2_, bf16[2,4,64,128]{3,2,1,0:T(8,128)(2,1)S(1)} %collective-permute-done.12.refs_3_, ...), custom_call_target="tpu_custom_call" | custom-call | flops 1000 | bytes 1000 | tf_op jit(solution)/shard_map/attend/pallas_call | solution.py:303
  35.6 0.0 collective-permute-done.16.other_ref
  35.6 0.8 %join.1 = bf16[64,64,128]{2,1,0:T(8,128)(2,1)} custom-call(s32[1]{0:T(128)} %bitcast.core_ref.refs_10_, bf16[64,32,128]{2,1,0:T(8,128)(2,1)S(1)} %collective-permute-done.16.other_ref, bf16[64,64,128]{2,1,0:T(8,128)(2,1)} %attend.9.begun_ref), custom_call_target="tpu_custom_call", output_to_operand_aliasing={{}: (2, {})} | custom-call | flops 1000 | bytes 1000 | tf_op jit(solution)/shard_map/join/pallas_call | solution.py:392
  (1 shorter events, 0.0 us)
Async XLA Ops:
  0.0 7.0 %collective-permute-start.1 = (bf16[64,64,128]{2,1,0:T(8,128)(2,1)}, bf16[64,64,128]{2,1,0:T(8,128)(2,1)S(1)}, u32[]{:S(2)}, u32[]{:S(2)}) collective-permute-start(bf16[64,64,128]{2,1,0:T(8,128)(2,1)} %q_own.1), channel_id=1, source_target_pairs={{0,1},{1,0},{2,3},{3,2},{4,5},{5,4},{6,7},{7,6},{8,9},{9,8},{10,11... | collective-permute-start | bytes 3145736 | tf_op jit(solution)/shard_map/ppermute | solution.py:418
  1.8 12.6 %copy-start.1 = (bf16[2,4,64,128]{3,2,1,0:T(8,128)(2,1)S(1)}, bf16[2,4,64,128]{3,2,1,0:T(8,128)(2,1)}, u32[]{:S(2)}) copy-start(bf16[2,4,64,128]{3,2,1,0:T(8,128)(2,1)} %get-tuple-element.49.refs_3_) | copy-start | bytes 393220
  1.8 5.2 %collective-permute-start = (bf16[2,4,64,128]{3,2,1,0:T(8,128)(2,1)}, bf16[2,4,64,128]{3,2,1,0:T(8,128)(2,1)S(1)}, u32[]{:S(2)}, u32[]{:S(2)}) collective-permute-start(bf16[2,4,64,128]{3,2,1,0:T(8,128)(2,1)} %get-tuple-element.37), channel_id=1, source_target_pairs={{0,1},{1,0},{2,3},{3,2},{4,5},{5,4},{6,7},{7,6},{8,9},{9,8},{10,11... | collective-permute-start | bytes 393224 | tf_op jit(solution)/shard_map/ppermute | solution.py:418
  2.3 10.5 %collective-permute-start.2 = (bf16[2,4,64,128]{3,2,1,0:T(8,128)(2,1)}, bf16[2,4,64,128]{3,2,1,0:T(8,128)(2,1)S(1)}, u32[]{:S(2)}, u32[]{:S(2)}) collective-permute-start(bf16[2,4,64,128]{3,2,1,0:T(8,128)(2,1)} %get-tuple-element.49.refs_3_), channel_id=1, source_target_pairs={{0,4},{4,0},{8,12},{12,8},{1,5},{5,1},{9,13},{13,9},{2,6},{6,2},{1... | collective-permute-start | bytes 393224 | tf_op jit(solution)/shard_map/ppermute | solution.py:412
  4.7 11.2 %collective-permute-start.3 = (bf16[2,4,64,128]{3,2,1,0:T(8,128)(2,1)}, bf16[2,4,64,128]{3,2,1,0:T(8,128)(2,1)S(1)}, u32[]{:S(2)}, u32[]{:S(2)}) collective-permute-start(bf16[2,4,64,128]{3,2,1,0:T(8,128)(2,1)} %get-tuple-element.49.refs_3_), channel_id=1, source_target_pairs={{0,12},{4,8},{8,4},{12,0},{1,13},{5,9},{9,5},{13,1},{2,14},{6,10},... | collective-permute-start | bytes 393224 | tf_op jit(solution)/shard_map/ppermute | solution.py:412
  7.0 7.4 %collective-permute-start.11 = (bf16[2,4,64,128]{3,2,1,0:T(8,128)(2,1)S(1)}, bf16[2,4,64,128]{3,2,1,0:T(8,128)(2,1)S(1)}, u32[]{:S(2)}, u32[]{:S(2)}) collective-permute-start(bf16[2,4,64,128]{3,2,1,0:T(8,128)(2,1)S(1)} %collective-permute-done.refs_4_), channel_id=1, source_target_pairs={{0,2},{2,0},{1,3},{3,1},{4,6},{6,4},{5,7},{7,5},{8,10},{10,8},{9,1... | collective-permute-start | bytes 393224 | tf_op jit(solution)/shard_map/ppermute | solution.py:415
  8.3 9.0 %collective-permute-start.4 = (bf16[2,4,64,128]{3,2,1,0:T(8,128)(2,1)S(1)}, bf16[2,4,64,128]{3,2,1,0:T(8,128)(2,1)S(1)}, u32[]{:S(2)}, u32[]{:S(2)}) collective-permute-start(bf16[2,4,64,128]{3,2,1,0:T(8,128)(2,1)S(1)} %collective-permute-done.refs_4_), channel_id=1, source_target_pairs={{0,12},{4,8},{8,4},{12,0},{1,13},{5,9},{9,5},{13,1},{2,14},{6,10},... | collective-permute-start | bytes 393224 | tf_op jit(solution)/shard_map/ppermute | solution.py:412
  9.4 4.7 %collective-permute-start.10 = (bf16[2,4,64,128]{3,2,1,0:T(8,128)(2,1)}, bf16[2,4,64,128]{3,2,1,0:T(8,128)(2,1)S(1)}, u32[]{:S(2)}, u32[]{:S(2)}) collective-permute-start(bf16[2,4,64,128]{3,2,1,0:T(8,128)(2,1)} %get-tuple-element.49.refs_3_), channel_id=1, source_target_pairs={{0,2},{2,0},{1,3},{3,1},{4,6},{6,4},{5,7},{7,5},{8,10},{10,8},{9,1... | collective-permute-start | bytes 393224 | tf_op jit(solution)/shard_map/ppermute | solution.py:415
  11.5 1.2 %copy-start = (bf16[64,64,128]{2,1,0:T(8,128)(2,1)S(1)}, bf16[64,64,128]{2,1,0:T(8,128)(2,1)}, u32[]{:S(2)}) copy-start(bf16[64,64,128]{2,1,0:T(8,128)(2,1)} %q_own.1) | copy-start | bytes 3145732
  12.9 6.6 %collective-permute-start.5 = (bf16[2,4,64,128]{3,2,1,0:T(8,128)(2,1)S(1)}, bf16[2,4,64,128]{3,2,1,0:T(8,128)(2,1)S(1)}, u32[]{:S(2)}, u32[]{:S(2)}) collective-permute-start(bf16[2,4,64,128]{3,2,1,0:T(8,128)(2,1)S(1)} %collective-permute-done.2.refs_3_), channel_id=1, source_target_pairs={{0,2},{2,0},{1,3},{3,1},{4,6},{6,4},{5,7},{7,5},{8,10},{10,8},{9,1... | collective-permute-start | bytes 393224 | tf_op jit(solution)/shard_map/ppermute | solution.py:415
  14.2 4.3 %collective-permute-start.8 = (bf16[2,4,64,128]{3,2,1,0:T(8,128)(2,1)S(1)}, bf16[2,4,64,128]{3,2,1,0:T(8,128)(2,1)S(1)}, u32[]{:S(2)}, u32[]{:S(2)}) collective-permute-start(bf16[2,4,64,128]{3,2,1,0:T(8,128)(2,1)S(1)} %collective-permute-done.refs_4_), channel_id=1, source_target_pairs={{0,4},{4,0},{8,12},{12,8},{1,5},{5,1},{9,13},{13,9},{2,6},{6,2},{1... | collective-permute-start | bytes 393224 | tf_op jit(solution)/shard_map/ppermute | solution.py:412
  16.0 5.9 %collective-permute-start.12 = (bf16[2,4,64,128]{3,2,1,0:T(8,128)(2,1)S(1)}, bf16[2,4,64,128]{3,2,1,0:T(8,128)(2,1)S(1)}, u32[]{:S(2)}, u32[]{:S(2)}) collective-permute-start(bf16[2,4,64,128]{3,2,1,0:T(8,128)(2,1)S(1)} %collective-permute-done.3.refs_3_), channel_id=1, source_target_pairs={{0,4},{4,0},{8,12},{12,8},{1,5},{5,1},{9,13},{13,9},{2,6},{6,2},{1... | collective-permute-start | bytes 393224 | tf_op jit(solution)/shard_map/ppermute | solution.py:412
  17.2 5.2 %collective-permute-start.7 = (bf16[2,4,64,128]{3,2,1,0:T(8,128)(2,1)S(1)}, bf16[2,4,64,128]{3,2,1,0:T(8,128)(2,1)S(1)}, u32[]{:S(2)}, u32[]{:S(2)}) collective-permute-start(bf16[2,4,64,128]{3,2,1,0:T(8,128)(2,1)S(1)} %collective-permute-done.4.refs_4_), channel_id=1, source_target_pairs={{0,2},{2,0},{1,3},{3,1},{4,6},{6,4},{5,7},{7,5},{8,10},{10,8},{9,1... | collective-permute-start | bytes 393224 | tf_op jit(solution)/shard_map/ppermute | solution.py:415
  18.5 5.4 %collective-permute-start.9 = (bf16[2,4,64,128]{3,2,1,0:T(8,128)(2,1)S(1)}, bf16[2,4,64,128]{3,2,1,0:T(8,128)(2,1)S(1)}, u32[]{:S(2)}, u32[]{:S(2)}) collective-permute-start(bf16[2,4,64,128]{3,2,1,0:T(8,128)(2,1)S(1)} %collective-permute-done.8.refs_4_), channel_id=1, source_target_pairs={{0,2},{2,0},{1,3},{3,1},{4,6},{6,4},{5,7},{7,5},{8,10},{10,8},{9,1... | collective-permute-start | bytes 393224 | tf_op jit(solution)/shard_map/ppermute | solution.py:415
  19.5 6.2 %collective-permute-start.6 = (bf16[2,4,64,128]{3,2,1,0:T(8,128)(2,1)S(1)}, bf16[2,4,64,128]{3,2,1,0:T(8,128)(2,1)S(1)}, u32[]{:S(2)}, u32[]{:S(2)}) collective-permute-start(bf16[2,4,64,128]{3,2,1,0:T(8,128)(2,1)S(1)} %collective-permute-done.3.refs_3_), channel_id=1, source_target_pairs={{0,2},{2,0},{1,3},{3,1},{4,6},{6,4},{5,7},{7,5},{8,10},{10,8},{9,1... | collective-permute-start | bytes 393224 | tf_op jit(solution)/shard_map/ppermute | solution.py:415
  20.0 7.6 %collective-permute-start.13 = (bf16[2,4,64,128]{3,2,1,0:T(8,128)(2,1)S(1)}, bf16[2,4,64,128]{3,2,1,0:T(8,128)(2,1)S(1)}, u32[]{:S(2)}, u32[]{:S(2)}) collective-permute-start(bf16[2,4,64,128]{3,2,1,0:T(8,128)(2,1)S(1)} %collective-permute-done.4.refs_4_), channel_id=1, source_target_pairs={{0,4},{4,0},{8,12},{12,8},{1,5},{5,1},{9,13},{13,9},{2,6},{6,2},{1... | collective-permute-start | bytes 393224 | tf_op jit(solution)/shard_map/ppermute | solution.py:412
  21.8 6.2 %collective-permute-start.14 = (bf16[2,4,64,128]{3,2,1,0:T(8,128)(2,1)S(1)}, bf16[2,4,64,128]{3,2,1,0:T(8,128)(2,1)S(1)}, u32[]{:S(2)}, u32[]{:S(2)}) collective-permute-start(bf16[2,4,64,128]{3,2,1,0:T(8,128)(2,1)S(1)} %collective-permute-done.12.refs_3_), channel_id=1, source_target_pairs={{0,2},{2,0},{1,3},{3,1},{4,6},{6,4},{5,7},{7,5},{8,10},{10,8},{9,1... | collective-permute-start | bytes 393224 | tf_op jit(solution)/shard_map/ppermute | solution.py:415
  22.4 5.7 %collective-permute-start.15 = (bf16[2,4,64,128]{3,2,1,0:T(8,128)(2,1)S(1)}, bf16[2,4,64,128]{3,2,1,0:T(8,128)(2,1)S(1)}, u32[]{:S(2)}, u32[]{:S(2)}) collective-permute-start(bf16[2,4,64,128]{3,2,1,0:T(8,128)(2,1)S(1)} %collective-permute-done.7.refs_6_), channel_id=1, source_target_pairs={{0,4},{4,0},{8,12},{12,8},{1,5},{5,1},{9,13},{13,9},{2,6},{6,2},{1... | collective-permute-start | bytes 393224 | tf_op jit(solution)/shard_map/ppermute | solution.py:412
  29.2 6.4 %collective-permute-start.16 = (bf16[64,32,128]{2,1,0:T(8,128)(2,1)S(1)}, bf16[64,32,128]{2,1,0:T(8,128)(2,1)S(1)}, u32[]{:S(2)}, u32[]{:S(2)}) collective-permute-start(bf16[64,32,128]{2,1,0:T(8,128)(2,1)S(1)} %attend.8), channel_id=1, source_target_pairs={{0,1},{1,0},{2,3},{3,2},{4,5},{5,4},{6,7},{7,6},{8,9},{9,8},{10,11... | collective-permute-start | bytes 1572872 | tf_op jit(solution)/shard_map/ppermute | solution.py:418

commit v5 on v4

--- a/solution.py
+++ b/solution.py
@@ -433,7 +433,7 @@
     q_keep, q_sib = turn_queries(core_id, queries, sibling_queries, 2 * give.shape[1])
     lists = jnp.concatenate([vert_lists.T, vert_count[None], slash_offsets.T, slash_count[None]])
     bias = pattern_bias(ids, 4 * planes, vert_blocks.shape[1], slash_offsets.shape[1], lists)
-    late_b, near_a, bias, q_keep, q_sib = lax.optimization_barrier((b, near_a, bias, q_keep, q_sib))
+    late_b, near_a, bias, x_b = lax.optimization_barrier((b, near_a, bias, x_b))
     near_b, x_near_a = trade(late_b, 1), across(near_a)
     state = attend_stage(0, bias, q_keep, q_sib, [a, b, x_a, x_b], ())
     early_a, state = lax.optimization_barrier((far_a, state))

time: 36.6 us -> 36.7 us (level)
  starting transfers between devices: 21.7 us -> 20.6 us
  waiting for transfers between devices: 0.6 us -> 1.67 us
    ppermute x7, starting transfers between devices: 6.08 us -> 5.22 us  [across(): return lax.ppermute(tile, 'blk', [(0, 2), (2, 0), (1, 3), (3, 1)])]
    ppermute x7, waiting for transfers between devices: 0.02 us -> 0.81 us  [trade(): return lax.ppermute(tile, 'seq', [(i, i ^ step) for i in range(planes)])]
  transfers between devices with their start and end apart: 17 -> 17, of which waited for: 1 -> 2; matrix products, arithmetic and copies ran while one was open for 3% -> 3% of each run, Pallas kernels for 27% -> 27%
where the time goes in v5:
time: 36.7 us; the launch traced here: 36.4 us
  starting transfers between devices  20.6 us (56%)
  Pallas kernels  11.9 us (32%)
  waiting for transfers between devices  1.67 us (5%)
  local copies, waits for them, and re-layouts  1.3 us (4%)
  other arithmetic  0.85 us (2%)
    ppermute x7, starting transfers between devices, trade(): return lax.ppermute(tile, 'seq', [(i, i ^ step) for i in range(planes)])  10.4 us
    pallas_call x5, Pallas kernels, attend_stage(): pl.pallas_call(functools.partial(stage_body, first_slot, rows_of, len(til...  8.2 us
    ppermute x7, starting transfers between devices, across(): return lax.ppermute(tile, 'blk', [(0, 2), (2, 0), (1, 3), (3, 1)])  5.22 us
    ppermute x3, starting transfers between devices, sibling(): return lax.ppermute(tile, 'blk', [(0, 1), (1, 0), (2, 3), (3, 2)])  5.02 us
    pallas_call x1, Pallas kernels, split_heads(): pl.pallas_call(split_body, out_shape=[half, half], in_specs=[pl.BlockSpec...  1.74 us
    unnamed x4, local copies, waits for them, and re-layouts  1.23 us
    pallas_call x1, Pallas kernels, pattern_bias(): pl.pallas_call(functools.partial(pattern_body, vert_rows, slash_rows), ou...  0.92 us
    ppermute x7, waiting for transfers between devices, across(): return lax.ppermute(tile, 'blk', [(0, 2), (2, 0), (1, 3), (3, 1)])  0.86 us
  transfers between devices with their start and end apart: 17, of which 2 were waited for; matrix products, arithmetic and copies ran while one was open for 3% of the time, Pallas kernels for 27%

profile of v5, /device:TPU:1, one launch (start us, length us, event | category | flops | bytes accessed | tf_op | source)
XLA Modules:
  0.0 36.4 jit_solution(13914247435651295336)
XLA Ops:
  0.0 0.1 collective-permute-start.1
  0.1 1.7 %split.1 = (bf16[2,4,64,128]{3,2,1,0:T(8,128)(2,1)}, bf16[2,4,64,128]{3,2,1,0:T(8,128)(2,1)}) custom-call(s32[1]{0:T(128)} %bitcast.core_ref.refs_10_, bf16[64,8,128]{2,1,0:T(8,128)(2,1)} %k_hbm.1, bf16[64,8,128]{2,1,0:T(8,128)(2,1)} %v_hbm.1), custom_call_target="tpu_custom_call" | custom-call | flops 1000 | bytes 1000 | tf_op jit(solution)/shard_map/split/pallas_call | solution.py:359
  1.8 0.0 copy-start.1
  1.8 0.5 %collective-permute-start = (bf16[2,4,64,128]{3,2,1,0:T(8,128)(2,1)}, bf16[2,4,64,128]{3,2,1,0:T(8,128)(2,1)S(1)}, u32[]{:S(2)}, u32[]{:S(2)}) collective-permute-start(bf16[2,4,64,128]{3,2,1,0:T(8,128)(2,1)} %get-tuple-element.36), channel_id=1, source_target_pairs={{0,1},{1,0},{2,3},{3,2},{4,5},{5,4},{6,7},{7,6},{8,9},{9,8},{10,11... | collective-permute-start | bytes 393224 | tf_op jit(solution)/shard_map/ppermute | solution.py:418
  2.3 2.4 %collective-permute-start.2 = (bf16[2,4,64,128]{3,2,1,0:T(8,128)(2,1)}, bf16[2,4,64,128]{3,2,1,0:T(8,128)(2,1)S(1)}, u32[]{:S(2)}, u32[]{:S(2)}) collective-permute-start(bf16[2,4,64,128]{3,2,1,0:T(8,128)(2,1)} %get-tuple-element.46.refs_3_), channel_id=1, source_target_pairs={{0,4},{4,0},{8,12},{12,8},{1,5},{5,1},{9,13},{13,9},{2,6},{6,2},{1... | collective-permute-start | bytes 393224 | tf_op jit(solution)/shard_map/ppermute | solution.py:412
  4.7 2.2 %collective-permute-start.4 = (bf16[2,4,64,128]{3,2,1,0:T(8,128)(2,1)}, bf16[2,4,64,128]{3,2,1,0:T(8,128)(2,1)S(1)}, u32[]{:S(2)}, u32[]{:S(2)}) collective-permute-start(bf16[2,4,64,128]{3,2,1,0:T(8,128)(2,1)} %get-tuple-element.46.refs_3_), channel_id=1, source_target_pairs={{0,12},{4,8},{8,4},{12,0},{1,13},{5,9},{9,5},{13,1},{2,14},{6,10},... | collective-permute-start | bytes 393224 | tf_op jit(solution)/shard_map/ppermute | solution.py:412
  6.9 0.1 broadcast_add_fusion
  7.0 0.0 collective-permute-done.refs_4_
  7.0 0.0 collective-permute-done.1.q_sib
  7.0 1.3 %collective-permute-start.3 = (bf16[2,4,64,128]{3,2,1,0:T(8,128)(2,1)S(1)}, bf16[2,4,64,128]{3,2,1,0:T(8,128)(2,1)S(1)}, u32[]{:S(2)}, u32[]{:S(2)}) collective-permute-start(bf16[2,4,64,128]{3,2,1,0:T(8,128)(2,1)S(1)} %collective-permute-done.refs_4_), channel_id=1, source_target_pairs={{0,2},{2,0},{1,3},{3,1},{4,6},{6,4},{5,7},{7,5},{8,10},{10,8},{9,1... | collective-permute-start | bytes 393224 | tf_op jit(solution)/shard_map/ppermute | solution.py:415
  8.3 1.2 %collective-permute-start.5 = (bf16[2,4,64,128]{3,2,1,0:T(8,128)(2,1)S(1)}, bf16[2,4,64,128]{3,2,1,0:T(8,128)(2,1)S(1)}, u32[]{:S(2)}, u32[]{:S(2)}) collective-permute-start(bf16[2,4,64,128]{3,2,1,0:T(8,128)(2,1)S(1)} %collective-permute-done.refs_4_), channel_id=1, source_target_pairs={{0,12},{4,8},{8,4},{12,0},{1,13},{5,9},{9,5},{13,1},{2,14},{6,10},... | collective-permute-start | bytes 393224 | tf_op jit(solution)/shard_map/ppermute | solution.py:412
  9.4 0.3 collective-permute-start.11
  9.7 0.1 concatenate.6.ids
  9.8 0.8 %pad_add_fusion.lists = s32[32,64]{1,0:T(8,128)S(1)} fusion(s32[1,64]{1,0:T(1,128)} %bitcast.13, s32[14,64]{1,0:T(8,128)} %bitcast.11, s32[1,64]{1,0:T(1,128)} %bitcast.14, s32[16,64]{1,0:T(8,128)} %bitcast.12), kind=kLoop, calls=%fused_computation | loop fusion | flops 6144 | bytes 16384 | tf_op jit(solution)/shard_map/concatenate | solution.py:434
  10.5 0.9 %pattern.1.refs_0_ = f32[2,32,1024]{2,1,0:T(8,128)S(1)} custom-call(s32[19]{0:T(128)S(1)} %concatenate.6.ids, s32[32,64]{1,0:T(8,128)S(1)} %pad_add_fusion.lists), custom_call_target="tpu_custom_call" | custom-call | bytes 16777216 | tf_op jit(solution)/shard_map/pattern/pallas_call | solution.py:207
  11.5 0.0 copy-start
  11.5 1.2 %copy-done = bf16[64,64,128]{2,1,0:T(8,128)(2,1)S(1)} copy-done((bf16[64,64,128]{2,1,0:T(8,128)(2,1)S(1)}, bf16[64,64,128]{2,1,0:T(8,128)(2,1)}, u32[]{:S(2)}) %copy-start) | copy-done | bytes 1048600
  12.7 0.2 turn.1
  12.9 0.0 collective-permute-done.2.refs_3_
  12.9 0.0 collective-permute-done.3.refs_6_
  12.9 1.3 %collective-permute-start.6 = (bf16[2,4,64,128]{3,2,1,0:T(8,128)(2,1)S(1)}, bf16[2,4,64,128]{3,2,1,0:T(8,128)(2,1)S(1)}, u32[]{:S(2)}, u32[]{:S(2)}) collective-permute-start(bf16[2,4,64,128]{3,2,1,0:T(8,128)(2,1)S(1)} %collective-permute-done.2.refs_3_), channel_id=1, source_target_pairs={{0,2},{2,0},{1,3},{3,1},{4,6},{6,4},{5,7},{7,5},{8,10},{10,8},{9,1... | collective-permute-start | bytes 393224 | tf_op jit(solution)/shard_map/ppermute | solution.py:415
  14.2 0.0 collective-permute-start.9
  14.2 0.0 collective-permute-done.11.refs_5_
  14.2 0.0 copy-done.1
  14.2 1.5 %attend.5 = (f32[2,4,512,128]{3,2,1,0:T(8,128)S(1)}, f32[2,4,512,128]{3,2,1,0:T(8,128)S(1)}, f32[2,4,512,128]{3,2,1,0:T(8,128)S(1)}) custom-call(f32[2,32,1024]{2,1,0:T(8,128)S(1)} %pattern.1.refs_0_, bf16[4,512,128]{2,1,0:T(8,128)(2,1)S(1)} %get-tuple-element.40.refs_1_, bf16[4,512,128]{2,1,0:T(8,128)(2,1)S(1)} %get-tuple-element.41.refs_2_, ...), custom_call_target="tpu_custom_call" | custom-call | flops 1000 | bytes 1000 | tf_op jit(solution)/shard_map/attend/pallas_call | solution.py:303
  15.7 0.0 collective-permute-done.4.refs_3_
  15.7 1.5 %collective-permute-start.12 = (bf16[2,4,64,128]{3,2,1,0:T(8,128)(2,1)S(1)}, bf16[2,4,64,128]{3,2,1,0:T(8,128)(2,1)S(1)}, u32[]{:S(2)}, u32[]{:S(2)}) collective-permute-start(bf16[2,4,64,128]{3,2,1,0:T(8,128)(2,1)S(1)} %collective-permute-done.4.refs_3_), channel_id=1, source_target_pairs={{0,4},{4,0},{8,12},{12,8},{1,5},{5,1},{9,13},{13,9},{2,6},{6,2},{1... | collective-permute-start | bytes 393224 | tf_op jit(solution)/shard_map/ppermute | solution.py:412
  17.2 0.0 collective-permute-done.5.refs_4_
  17.2 0.3 collective-permute-start.8
  17.5 0.8 %collective-permute-done.9.refs_4_ = bf16[2,4,64,128]{3,2,1,0:T(8,128)(2,1)S(1)} collective-permute-done((bf16[2,4,64,128]{3,2,1,0:T(8,128)(2,1)S(1)}, bf16[2,4,64,128]{3,2,1,0:T(8,128)(2,1)S(1)}, u32[]{:S(2)}, u32[]{:S(2)}) %collective-permute-start.9) | collective-permute-done | bytes 131104 | tf_op jit(solution)/shard_map/ppermute | solution.py:412
  18.3 1.2 %collective-permute-start.10 = (bf16[2,4,64,128]{3,2,1,0:T(8,128)(2,1)S(1)}, bf16[2,4,64,128]{3,2,1,0:T(8,128)(2,1)S(1)}, u32[]{:S(2)}, u32[]{:S(2)}) collective-permute-start(bf16[2,4,64,128]{3,2,1,0:T(8,128)(2,1)S(1)} %collective-permute-done.9.refs_4_), channel_id=1, source_target_pairs={{0,2},{2,0},{1,3},{3,1},{4,6},{6,4},{5,7},{7,5},{8,10},{10,8},{9,1... | collective-permute-start | bytes 393224 | tf_op jit(solution)/shard_map/ppermute | solution.py:415
  19.5 0.0 collective-permute-done.6.refs_5_
  19.5 0.3 collective-permute-start.7
  19.8 2.1 %collective-permute-start.13 = (bf16[2,4,64,128]{3,2,1,0:T(8,128)(2,1)S(1)}, bf16[2,4,64,128]{3,2,1,0:T(8,128)(2,1)S(1)}, u32[]{:S(2)}, u32[]{:S(2)}) collective-permute-start(bf16[2,4,64,128]{3,2,1,0:T(8,128)(2,1)S(1)} %collective-permute-done.5.refs_4_), channel_id=1, source_target_pairs={{0,4},{4,0},{8,12},{12,8},{1,5},{5,1},{9,13},{13,9},{2,6},{6,2},{1... | collective-permute-start | bytes 393224 | tf_op jit(solution)/shard_map/ppermute | solution.py:412
  21.8 0.0 collective-permute-done.12.refs_3_
  21.8 0.7 %collective-permute-start.14 = (bf16[2,4,64,128]{3,2,1,0:T(8,128)(2,1)S(1)}, bf16[2,4,64,128]{3,2,1,0:T(8,128)(2,1)S(1)}, u32[]{:S(2)}, u32[]{:S(2)}) collective-permute-start(bf16[2,4,64,128]{3,2,1,0:T(8,128)(2,1)S(1)} %collective-permute-done.12.refs_3_), channel_id=1, source_target_pairs={{0,2},{2,0},{1,3},{3,1},{4,6},{6,4},{5,7},{7,5},{8,10},{10,8},{9,1... | collective-permute-start | bytes 393224 | tf_op jit(solution)/shard_map/ppermute | solution.py:415
  22.5 0.0 collective-permute-done.8.refs_6_
  22.5 1.0 %collective-permute-start.15 = (bf16[2,4,64,128]{3,2,1,0:T(8,128)(2,1)S(1)}, bf16[2,4,64,128]{3,2,1,0:T(8,128)(2,1)S(1)}, u32[]{:S(2)}, u32[]{:S(2)}) collective-permute-start(bf16[2,4,64,128]{3,2,1,0:T(8,128)(2,1)S(1)} %collective-permute-done.8.refs_6_), channel_id=1, source_target_pairs={{0,4},{4,0},{8,12},{12,8},{1,5},{5,1},{9,13},{13,9},{2,6},{6,2},{1... | collective-permute-start | bytes 393224 | tf_op jit(solution)/shard_map/ppermute | solution.py:412
  23.6 0.0 collective-permute-done.10.refs_6_
  23.6 1.8 %attend.6 = (f32[2,4,512,128]{3,2,1,0:T(8,128)S(1)}, f32[2,4,512,128]{3,2,1,0:T(8,128)S(1)}, f32[2,4,512,128]{3,2,1,0:T(8,128)S(1)}) custom-call(f32[2,32,1024]{2,1,0:T(8,128)S(1)} %pattern.1.refs_0_, bf16[4,512,128]{2,1,0:T(8,128)(2,1)S(1)} %get-tuple-element.40.refs_1_, bf16[4,512,128]{2,1,0:T(8,128)(2,1)S(1)} %get-tuple-element.41.refs_2_, ...), custom_call_target="tpu_custom_call" | custom-call | flops 1000 | bytes 1000 | tf_op jit(solution)/shard_map/attend/pallas_call | solution.py:303
  25.4 0.0 collective-permute-done.7.refs_5_
  25.4 1.8 %attend.7 = (f32[2,4,512,128]{3,2,1,0:T(8,128)S(1)}, f32[2,4,512,128]{3,2,1,0:T(8,128)S(1)}, f32[2,4,512,128]{3,2,1,0:T(8,128)S(1)}) custom-call(f32[2,32,1024]{2,1,0:T(8,128)S(1)} %pattern.1.refs_0_, bf16[4,512,128]{2,1,0:T(8,128)(2,1)S(1)} %get-tuple-element.40.refs_1_, bf16[4,512,128]{2,1,0:T(8,128)(2,1)S(1)} %get-tuple-element.41.refs_2_, ...), custom_call_target="tpu_custom_call" | custom-call | flops 1000 | bytes 1000 | tf_op jit(solution)/shard_map/attend/pallas_call | solution.py:303
  27.2 0.0 collective-permute-done.13.refs_4_
  27.2 0.8 %collective-permute-done.14.refs_5_ = bf16[2,4,64,128]{3,2,1,0:T(8,128)(2,1)S(1)} collective-permute-done((bf16[2,4,64,128]{3,2,1,0:T(8,128)(2,1)S(1)}, bf16[2,4,64,128]{3,2,1,0:T(8,128)(2,1)S(1)}, u32[]{:S(2)}, u32[]{:S(2)}) %collective-permute-start.14) | collective-permute-done | bytes 131104 | tf_op jit(solution)/shard_map/ppermute | solution.py:415
  28.1 0.0 collective-permute-done.15.refs_6_
  28.1 1.2 %attend.8 = bf16[64,32,128]{2,1,0:T(8,128)(2,1)S(1)} custom-call(f32[2,32,1024]{2,1,0:T(8,128)S(1)} %pattern.1.refs_0_, bf16[4,512,128]{2,1,0:T(8,128)(2,1)S(1)} %get-tuple-element.40.refs_1_, bf16[4,512,128]{2,1,0:T(8,128)(2,1)S(1)} %get-tuple-element.41.refs_2_, bf16[2,4,64,128]{3,2,1,0:T(8,128)(2,1)S(1)} %collective-permute-done.12.refs_3_, ...), custom_call_target="tpu_custom_call" | custom-call | flops 1000 | bytes 1000 | tf_op jit(solution)/shard_map/attend/pallas_call | solution.py:303
  29.2 4.4 %collective-permute-start.16 = (bf16[64,32,128]{2,1,0:T(8,128)(2,1)S(1)}, bf16[64,32,128]{2,1,0:T(8,128)(2,1)S(1)}, u32[]{:S(2)}, u32[]{:S(2)}) collective-permute-start(bf16[64,32,128]{2,1,0:T(8,128)(2,1)S(1)} %attend.8), channel_id=1, source_target_pairs={{0,1},{1,0},{2,3},{3,2},{4,5},{5,4},{6,7},{7,6},{8,9},{9,8},{10,11... | collective-permute-start | bytes 1572872 | tf_op jit(solution)/shard_map/ppermute | solution.py:418
  33.7 1.9 %attend.9.begun_ref = bf16[64,64,128]{2,1,0:T(8,128)(2,1)} custom-call(f32[2,32,1024]{2,1,0:T(8,128)S(1)} %pattern.1.refs_0_, bf16[4,512,128]{2,1,0:T(8,128)(2,1)S(1)} %get-tuple-element.40.refs_1_, bf16[4,512,128]{2,1,0:T(8,128)(2,1)S(1)} %get-tuple-element.41.refs_2_, bf16[2,4,64,128]{3,2,1,0:T(8,128)(2,1)S(1)} %collective-permute-done.12.refs_3_, ...), custom_call_target="tpu_custom_call" | custom-call | flops 1000 | bytes 1000 | tf_op jit(solution)/shard_map/attend/pallas_call | solution.py:303
  35.6 0.0 collective-permute-done.16.other_ref
  35.6 0.8 %join.1 = bf16[64,64,128]{2,1,0:T(8,128)(2,1)} custom-call(s32[1]{0:T(128)} %bitcast.core_ref.refs_10_, bf16[64,32,128]{2,1,0:T(8,128)(2,1)S(1)} %collective-permute-done.16.other_ref, bf16[64,64,128]{2,1,0:T(8,128)(2,1)} %attend.9.begun_ref), custom_call_target="tpu_custom_call", output_to_operand_aliasing={{}: (2, {})} | custom-call | flops 1000 | bytes 1000 | tf_op jit(solution)/shard_map/join/pallas_call | solution.py:392
  (1 shorter events, 0.0 us)
Async XLA Ops:
  0.0 7.0 %collective-permute-start.1 = (bf16[64,64,128]{2,1,0:T(8,128)(2,1)}, bf16[64,64,128]{2,1,0:T(8,128)(2,1)S(1)}, u32[]{:S(2)}, u32[]{:S(2)}) collective-permute-start(bf16[64,64,128]{2,1,0:T(8,128)(2,1)} %q_own.1), channel_id=1, source_target_pairs={{0,1},{1,0},{2,3},{3,2},{4,5},{5,4},{6,7},{7,6},{8,9},{9,8},{10,11... | collective-permute-start | bytes 3145736 | tf_op jit(solution)/shard_map/ppermute | solution.py:418
  1.8 12.4 %copy-start.1 = (bf16[2,4,64,128]{3,2,1,0:T(8,128)(2,1)S(1)}, bf16[2,4,64,128]{3,2,1,0:T(8,128)(2,1)}, u32[]{:S(2)}) copy-start(bf16[2,4,64,128]{3,2,1,0:T(8,128)(2,1)} %get-tuple-element.46.refs_3_) | copy-start | bytes 393220
  1.8 5.2 %collective-permute-start = (bf16[2,4,64,128]{3,2,1,0:T(8,128)(2,1)}, bf16[2,4,64,128]{3,2,1,0:T(8,128)(2,1)S(1)}, u32[]{:S(2)}, u32[]{:S(2)}) collective-permute-start(bf16[2,4,64,128]{3,2,1,0:T(8,128)(2,1)} %get-tuple-element.36), channel_id=1, source_target_pairs={{0,1},{1,0},{2,3},{3,2},{4,5},{5,4},{6,7},{7,6},{8,9},{9,8},{10,11... | collective-permute-start | bytes 393224 | tf_op jit(solution)/shard_map/ppermute | solution.py:418
  2.3 10.5 %collective-permute-start.2 = (bf16[2,4,64,128]{3,2,1,0:T(8,128)(2,1)}, bf16[2,4,64,128]{3,2,1,0:T(8,128)(2,1)S(1)}, u32[]{:S(2)}, u32[]{:S(2)}) collective-permute-start(bf16[2,4,64,128]{3,2,1,0:T(8,128)(2,1)} %get-tuple-element.46.refs_3_), channel_id=1, source_target_pairs={{0,4},{4,0},{8,12},{12,8},{1,5},{5,1},{9,13},{13,9},{2,6},{6,2},{1... | collective-permute-start | bytes 393224 | tf_op jit(solution)/shard_map/ppermute | solution.py:412
  4.7 11.0 %collective-permute-start.4 = (bf16[2,4,64,128]{3,2,1,0:T(8,128)(2,1)}, bf16[2,4,64,128]{3,2,1,0:T(8,128)(2,1)S(1)}, u32[]{:S(2)}, u32[]{:S(2)}) collective-permute-start(bf16[2,4,64,128]{3,2,1,0:T(8,128)(2,1)} %get-tuple-element.46.refs_3_), channel_id=1, source_target_pairs={{0,12},{4,8},{8,4},{12,0},{1,13},{5,9},{9,5},{13,1},{2,14},{6,10},... | collective-permute-start | bytes 393224 | tf_op jit(solution)/shard_map/ppermute | solution.py:412
  7.0 5.9 %collective-permute-start.3 = (bf16[2,4,64,128]{3,2,1,0:T(8,128)(2,1)S(1)}, bf16[2,4,64,128]{3,2,1,0:T(8,128)(2,1)S(1)}, u32[]{:S(2)}, u32[]{:S(2)}) collective-permute-start(bf16[2,4,64,128]{3,2,1,0:T(8,128)(2,1)S(1)} %collective-permute-done.refs_4_), channel_id=1, source_target_pairs={{0,2},{2,0},{1,3},{3,1},{4,6},{6,4},{5,7},{7,5},{8,10},{10,8},{9,1... | collective-permute-start | bytes 393224 | tf_op jit(solution)/shard_map/ppermute | solution.py:415
  8.3 9.0 %collective-permute-start.5 = (bf16[2,4,64,128]{3,2,1,0:T(8,128)(2,1)S(1)}, bf16[2,4,64,128]{3,2,1,0:T(8,128)(2,1)S(1)}, u32[]{:S(2)}, u32[]{:S(2)}) collective-permute-start(bf16[2,4,64,128]{3,2,1,0:T(8,128)(2,1)S(1)} %collective-permute-done.refs_4_), channel_id=1, source_target_pairs={{0,12},{4,8},{8,4},{12,0},{1,13},{5,9},{9,5},{13,1},{2,14},{6,10},... | collective-permute-start | bytes 393224 | tf_op jit(solution)/shard_map/ppermute | solution.py:412
  9.4 4.8 %collective-permute-start.11 = (bf16[2,4,64,128]{3,2,1,0:T(8,128)(2,1)}, bf16[2,4,64,128]{3,2,1,0:T(8,128)(2,1)S(1)}, u32[]{:S(2)}, u32[]{:S(2)}) collective-permute-start(bf16[2,4,64,128]{3,2,1,0:T(8,128)(2,1)} %get-tuple-element.46.refs_3_), channel_id=1, source_target_pairs={{0,2},{2,0},{1,3},{3,1},{4,6},{6,4},{5,7},{7,5},{8,10},{10,8},{9,1... | collective-permute-start | bytes 393224 | tf_op jit(solution)/shard_map/ppermute | solution.py:415
  11.5 1.2 %copy-start = (bf16[64,64,128]{2,1,0:T(8,128)(2,1)S(1)}, bf16[64,64,128]{2,1,0:T(8,128)(2,1)}, u32[]{:S(2)}) copy-start(bf16[64,64,128]{2,1,0:T(8,128)(2,1)} %q_own.1) | copy-start | bytes 3145732
  12.9 6.6 %collective-permute-start.6 = (bf16[2,4,64,128]{3,2,1,0:T(8,128)(2,1)S(1)}, bf16[2,4,64,128]{3,2,1,0:T(8,128)(2,1)S(1)}, u32[]{:S(2)}, u32[]{:S(2)}) collective-permute-start(bf16[2,4,64,128]{3,2,1,0:T(8,128)(2,1)S(1)} %collective-permute-done.2.refs_3_), channel_id=1, source_target_pairs={{0,2},{2,0},{1,3},{3,1},{4,6},{6,4},{5,7},{7,5},{8,10},{10,8},{9,1... | collective-permute-start | bytes 393224 | tf_op jit(solution)/shard_map/ppermute | solution.py:415
  14.2 4.1 %collective-permute-start.9 = (bf16[2,4,64,128]{3,2,1,0:T(8,128)(2,1)S(1)}, bf16[2,4,64,128]{3,2,1,0:T(8,128)(2,1)S(1)}, u32[]{:S(2)}, u32[]{:S(2)}) collective-permute-start(bf16[2,4,64,128]{3,2,1,0:T(8,128)(2,1)S(1)} %collective-permute-done.refs_4_), channel_id=1, source_target_pairs={{0,4},{4,0},{8,12},{12,8},{1,5},{5,1},{9,13},{13,9},{2,6},{6,2},{1... | collective-permute-start | bytes 393224 | tf_op jit(solution)/shard_map/ppermute | solution.py:412
  15.7 6.1 %collective-permute-start.12 = (bf16[2,4,64,128]{3,2,1,0:T(8,128)(2,1)S(1)}, bf16[2,4,64,128]{3,2,1,0:T(8,128)(2,1)S(1)}, u32[]{:S(2)}, u32[]{:S(2)}) collective-permute-start(bf16[2,4,64,128]{3,2,1,0:T(8,128)(2,1)S(1)} %collective-permute-done.4.refs_3_), channel_id=1, source_target_pairs={{0,4},{4,0},{8,12},{12,8},{1,5},{5,1},{9,13},{13,9},{2,6},{6,2},{1... | collective-permute-start | bytes 393224 | tf_op jit(solution)/shard_map/ppermute | solution.py:412
  17.2 5.3 %collective-permute-start.8 = (bf16[2,4,64,128]{3,2,1,0:T(8,128)(2,1)S(1)}, bf16[2,4,64,128]{3,2,1,0:T(8,128)(2,1)S(1)}, u32[]{:S(2)}, u32[]{:S(2)}) collective-permute-start(bf16[2,4,64,128]{3,2,1,0:T(8,128)(2,1)S(1)} %collective-permute-done.5.refs_4_), channel_id=1, source_target_pairs={{0,2},{2,0},{1,3},{3,1},{4,6},{6,4},{5,7},{7,5},{8,10},{10,8},{9,1... | collective-permute-start | bytes 393224 | tf_op jit(solution)/shard_map/ppermute | solution.py:415
  18.3 5.3 %collective-permute-start.10 = (bf16[2,4,64,128]{3,2,1,0:T(8,128)(2,1)S(1)}, bf16[2,4,64,128]{3,2,1,0:T(8,128)(2,1)S(1)}, u32[]{:S(2)}, u32[]{:S(2)}) collective-permute-start(bf16[2,4,64,128]{3,2,1,0:T(8,128)(2,1)S(1)} %collective-permute-done.9.refs_4_), channel_id=1, source_target_pairs={{0,2},{2,0},{1,3},{3,1},{4,6},{6,4},{5,7},{7,5},{8,10},{10,8},{9,1... | collective-permute-start | bytes 393224 | tf_op jit(solution)/shard_map/ppermute | solution.py:415
  19.5 5.9 %collective-permute-start.7 = (bf16[2,4,64,128]{3,2,1,0:T(8,128)(2,1)S(1)}, bf16[2,4,64,128]{3,2,1,0:T(8,128)(2,1)S(1)}, u32[]{:S(2)}, u32[]{:S(2)}) collective-permute-start(bf16[2,4,64,128]{3,2,1,0:T(8,128)(2,1)S(1)} %collective-permute-done.4.refs_3_), channel_id=1, source_target_pairs={{0,2},{2,0},{1,3},{3,1},{4,6},{6,4},{5,7},{7,5},{8,10},{10,8},{9,1... | collective-permute-start | bytes 393224 | tf_op jit(solution)/shard_map/ppermute | solution.py:415
  19.8 7.5 %collective-permute-start.13 = (bf16[2,4,64,128]{3,2,1,0:T(8,128)(2,1)S(1)}, bf16[2,4,64,128]{3,2,1,0:T(8,128)(2,1)S(1)}, u32[]{:S(2)}, u32[]{:S(2)}) collective-permute-start(bf16[2,4,64,128]{3,2,1,0:T(8,128)(2,1)S(1)} %collective-permute-done.5.refs_4_), channel_id=1, source_target_pairs={{0,4},{4,0},{8,12},{12,8},{1,5},{5,1},{9,13},{13,9},{2,6},{6,2},{1... | collective-permute-start | bytes 393224 | tf_op jit(solution)/shard_map/ppermute | solution.py:412
  21.8 6.2 %collective-permute-start.14 = (bf16[2,4,64,128]{3,2,1,0:T(8,128)(2,1)S(1)}, bf16[2,4,64,128]{3,2,1,0:T(8,128)(2,1)S(1)}, u32[]{:S(2)}, u32[]{:S(2)}) collective-permute-start(bf16[2,4,64,128]{3,2,1,0:T(8,128)(2,1)S(1)} %collective-permute-done.12.refs_3_), channel_id=1, source_target_pairs={{0,2},{2,0},{1,3},{3,1},{4,6},{6,4},{5,7},{7,5},{8,10},{10,8},{9,1... | collective-permute-start | bytes 393224 | tf_op jit(solution)/shard_map/ppermute | solution.py:415
  22.5 5.6 %collective-permute-start.15 = (bf16[2,4,64,128]{3,2,1,0:T(8,128)(2,1)S(1)}, bf16[2,4,64,128]{3,2,1,0:T(8,128)(2,1)S(1)}, u32[]{:S(2)}, u32[]{:S(2)}) collective-permute-start(bf16[2,4,64,128]{3,2,1,0:T(8,128)(2,1)S(1)} %collective-permute-done.8.refs_6_), channel_id=1, source_target_pairs={{0,4},{4,0},{8,12},{12,8},{1,5},{5,1},{9,13},{13,9},{2,6},{6,2},{1... | collective-permute-start | bytes 393224 | tf_op jit(solution)/shard_map/ppermute | solution.py:412
  29.2 6.4 %collective-permute-start.16 = (bf16[64,32,128]{2,1,0:T(8,128)(2,1)S(1)}, bf16[64,32,128]{2,1,0:T(8,128)(2,1)S(1)}, u32[]{:S(2)}, u32[]{:S(2)}) collective-permute-start(bf16[64,32,128]{2,1,0:T(8,128)(2,1)S(1)} %attend.8), channel_id=1, source_target_pairs={{0,1},{1,0},{2,3},{3,2},{4,5},{5,4},{6,7},{7,6},{8,9},{9,8},{10,11... | collective-permute-start | bytes 1572872 | tf_op jit(solution)/shard_map/ppermute | solution.py:418
